TPU v7x, 32 devices: a whole 2x2x4 slice. The times are simulated.
32 devices in a mesh: tm: 16 (over z, x, core), space: 2 (over y).
Axes of the slice: x: 2, y: 2, z: 4, core: 2. Of those that a mesh axis runs over, the one named last changes fastest.
Arguments:
- observations: bfloat16 [4096, 16, 2, 512], P(None, 'tm', 'space'), may hold values from -6 to 6
- pod_basis: bfloat16 [16, 2, 512, 1024], P(None, 'space'), may hold values from -0.046875 to 0.046875
- decay: float32 [4096, 1024], P('tm', 'space'), may hold values from 0 to 1
- step_mask: int32 [4096], P('tm'), may hold values 0 or 1
- process_var: float32 [1024], P('space'), may hold values from 0.00024414062 to 1
- obs_var: float32 [1024], P('space'), may hold values from 1 to 256
- prior_mean: float32 [1024], P('space'), may hold values from -6 to 6
- prior_var: float32 [1024], P('space'), may hold values from 0.5 to 4
Outputs:
- coefficients: float32 [4096, 1024], P('tm', 'space')
- filtered_mean: float32 [4096, 1024], P('tm', 'space')
- smoothed_mean: float32 [4096, 1024], P('tm', 'space')
- log_variance: float32 [4096, 1024], P('tm', 'space')
All inputs are finite; a program needn't handle non-finite values. No bound on the sum of `step_mask` on one device may be relied on, other than what follows from the above.
Results may differ from a plain program's by a relative error of at most 0.0003.
Values may be sent and summed in bfloat16 or wider, within the bound.
No kernel may reach another device: no remote copies, remote signals or barrier semaphores. Data moves between devices by JAX's collectives and lax.ppermute only.
A program may use at most 256 MiB of HBM per device.

v0:
```python
import functools

import jax
import jax.numpy as jnp
from jax import lax
from jax.experimental import pallas as pl
from jax.experimental.pallas import tpu as pltpu
from jax.sharding import PartitionSpec as P

CHUNK = 16
LANES = 128
F32 = jnp.float32
LIMIT = 48 * 1024 * 1024


def rotate(block, axis, turn, count, group, outer):
    route = []
    for i in range(count):
        low, high = i % group, i // group
        if outer:
            target = ((high + turn) % (count // group)) * group + low
        else:
            target = high * group + (low + turn) % group
        route.append((i, target))
    return lax.ppermute(block, axis, route)


def inner_size(count):
    group = 1
    while group * group < count:
        group *= 2
    return group if count % group == 0 else count


def gather_rows(rows, axis):
    count = lax.axis_size(axis)
    group = inner_size(count)
    near = jnp.stack([rows] + [rotate(rows, axis, s, count, group, False) for s in range(1, group)])
    far = [near] + [rotate(near, axis, s, count, group, True) for s in range(1, count // group)]
    return jnp.concatenate(far, 0)


def place(me, j, count):
    group = inner_size(count)
    rounds = count // group
    high = lax.rem(me // group - j // group + rounds, rounds)
    low = lax.rem(lax.rem(me, group) - j % group + group, group)
    return high * group + low


def lanes(ref, strip_ref):
    for m in range(strip_ref.shape[0]):
        strip_ref[m] = ref[:, m * LANES : (m + 1) * LANES]


def unlanes(strip_ref, ref):
    for m in range(strip_ref.shape[0]):
        ref[:, m * LANES : (m + 1) * LANES] = strip_ref[m]


def chunk_rows(strip_ref, i, chunks):
    rows = pl.ds(i, chunks, stride=CHUNK)
    return jnp.concatenate([strip_ref[m, rows, :] for m in range(strip_ref.shape[0])], 1)


def put_rows(strip_ref, i, chunks, value):
    rows = pl.ds(i, chunks, stride=CHUNK)
    for m in range(strip_ref.shape[0]):
        strip_ref[m, rows, :] = value[:, m * LANES : (m + 1) * LANES]


def opened(me_ref, shape):
    rows = lax.broadcasted_iota(jnp.int32, shape, 0)
    return jnp.logical_and(rows == 0, me_ref[0] == 0)


def step_terms(i, chunks, first, q, r, decay_ref, seen_ref):
    d = chunk_rows(decay_ref, i, chunks)
    seen = chunk_rows(seen_ref, i, chunks) > 0.5
    base = q
    if i == 0:
        d = jnp.where(first, 1.0, d)
        base = jnp.where(first, 0.0, q)
    return d, seen, base


def element(d, seen, base, r):
    inverse = 1.0 / (base + r)
    retain = jnp.where(seen, r * inverse, 1.0)
    return retain * d, retain * base, jnp.where(seen, d * d * inverse, 0.0), inverse


def join(early, late):
    lead, spread, weight = early
    lead_late, spread_late, weight_late = late
    factor = 1.0 / (1.0 + spread * weight_late)
    return (
        lead_late * factor * lead,
        lead_late * lead_late * factor * spread + spread_late,
        lead * lead * factor * weight_late + weight,
    )


def totals_kernel(me_ref, decay_in, seen_in, q_ref, r_ref, chunk_ref, block_ref, decay_ref, seen_ref):
    steps, modes = decay_in.shape
    lanes(decay_in, decay_ref)
    lanes(seen_in, seen_ref)
    chunks = steps // CHUNK
    shape = (chunks, modes)
    q = jnp.broadcast_to(q_ref[...], shape)
    r = jnp.broadcast_to(r_ref[...], shape)
    first = opened(me_ref, shape)
    total = None
    for i in range(CHUNK):
        step = element(*step_terms(i, chunks, first, q, r, decay_ref, seen_ref), r)[:3]
        total = step if i == 0 else join(total, step)
    for k in range(3):
        chunk_ref[k] = total[k]
    total = tuple(chunk_ref[k, 0:1, :] for k in range(3))
    for c in range(1, chunks):
        total = join(total, tuple(chunk_ref[k, c : c + 1, :] for k in range(3)))
    for k in range(3):
        block_ref[k : k + 1, :] = total[k]


def gains_kernel(
    count, me_ref, decay_in, seen_in, q_ref, r_ref, prior_ref, chunk_ref, blocks_ref,
    a_ref, b_ref, alpha_ref, beta_ref, keep_ref, lift_ref, whole_ref, carry_ref, edge_ref, log_ref,
    enter_ref, var_ref, info_ref, decay_ref, seen_ref,
):
    steps, modes = decay_in.shape
    lanes(decay_in, decay_ref)
    lanes(seen_in, seen_ref)
    chunks = steps // CHUNK
    shape = (chunks, modes)
    me = me_ref[0]
    q = jnp.broadcast_to(q_ref[...], shape)
    r = jnp.broadcast_to(r_ref[...], shape)
    first = opened(me_ref, shape)

    v = prior_ref[...]
    mine = v
    for j in range(count):
        mine = jnp.where(j == me, v, mine)
        at = place(me, j, count)
        lead, spread, weight = (blocks_ref[at, k : k + 1, :] for k in range(3))
        along = lead / (1.0 + weight * v)
        edge_ref[0, j : j + 1, :] = along
        v = spread + lead * along * v
    v = mine
    for c in range(chunks):
        enter_ref[0, c : c + 1, :] = v
        lead, spread, weight = (chunk_ref[k, c : c + 1, :] for k in range(3))
        v = spread + lead * lead * v / (1.0 + weight * v)

    info = jnp.zeros((1, modes), F32)
    mine = info
    for j in reversed(range(count)):
        mine = jnp.where(j == me, info, mine)
        at = place(me, j, count)
        lead, spread, weight = (blocks_ref[at, k : k + 1, :] for k in range(3))
        along = lead / (1.0 + spread * info)
        edge_ref[1, j : j + 1, :] = along
        info = weight + lead * along * info
    info = mine
    for c in reversed(range(chunks)):
        enter_ref[1, c : c + 1, :] = info
        lead, spread, weight = (chunk_ref[k, c : c + 1, :] for k in range(3))
        info = weight + lead * lead * info / (1.0 + spread * info)

    v = enter_ref[0]
    run = None
    for i in range(CHUNK):
        d, seen, base = step_terms(i, chunks, first, q, r, decay_ref, seen_ref)
        ahead = d * d * v + base
        inverse = 1.0 / (ahead + r)
        retain = jnp.where(seen, r * inverse, 1.0)
        v = retain * ahead
        a = retain * d
        run = a if i == 0 else a * run
        a_ref[i] = a
        b_ref[i] = jnp.where(seen, ahead * inverse, 0.0)
        var_ref[i] = v
        whole_ref[0, i] = run
    carry_ref[0] = run

    info = enter_ref[1]
    run = jnp.ones(shape, F32)
    for i in reversed(range(CHUNK)):
        lead, spread, weight, inverse = element(*step_terms(i, chunks, first, q, r, decay_ref, seen_ref), r)
        d, seen, _ = step_terms(i, chunks, first, q, r, decay_ref, seen_ref)
        factor = 1.0 / (1.0 + spread * info)
        alpha = lead * factor
        info_ref[i] = info
        whole_ref[2, i] = run
        alpha_ref[i] = alpha
        beta_ref[i] = jnp.where(seen, d * inverse * factor, 0.0)
        info = weight + lead * alpha * info
        run = alpha * run
    carry_ref[1] = run

    along = jnp.ones((1, modes), F32)
    for c in range(chunks):
        enter_ref[0, c : c + 1, :] = along
        along = along * carry_ref[0, c : c + 1, :]
    along = jnp.ones((1, modes), F32)
    for c in reversed(range(chunks)):
        enter_ref[1, c : c + 1, :] = along
        along = along * carry_ref[1, c : c + 1, :]
    onward = enter_ref[0]
    back = enter_ref[1]
    for i in range(CHUNK):
        v = var_ref[i]
        keep = 1.0 / (1.0 + v * info_ref[i])
        lift = v * keep
        weight = whole_ref[0, i] * onward
        keep_ref[i] = keep
        lift_ref[i] = lift
        whole_ref[0, i] = weight
        whole_ref[1, i] = keep * weight
        whole_ref[2, i] = lift * (whole_ref[2, i] * back)
        put_rows(decay_ref, i, chunks, jnp.log(lift))
    unlanes(decay_ref, log_ref)


def means_kernel(parts, *refs):
    part_refs = refs[:parts]
    a_ref, b_ref, alpha_ref, beta_ref, keep_ref, lift_ref, carry_ref = refs[parts : parts + 7]
    coef_ref, mean_ref, smooth_ref, block_ref, enter_ref, strip_ref = refs[parts + 7 :]
    steps, modes = coef_ref.shape
    chunks = steps // CHUNK
    c = part_refs[0][...]
    for ref in part_refs[1:]:
        c = c + ref[...]
    coef_ref[...] = c
    lanes(coef_ref, strip_ref)
    f = e = jnp.zeros((chunks, modes), F32)
    for i in range(CHUNK):
        f = a_ref[i] * f + b_ref[i] * chunk_rows(strip_ref, i, chunks)
        k = CHUNK - 1 - i
        e = alpha_ref[k] * e + beta_ref[k] * chunk_rows(strip_ref, k, chunks)
    mean_ref[0] = f
    mean_ref[1] = e
    f = e = jnp.zeros((1, modes), F32)
    for c in range(chunks):
        k = chunks - 1 - c
        enter_ref[0, c : c + 1, :] = f
        enter_ref[1, k : k + 1, :] = e
        f = mean_ref[0, c : c + 1, :] + carry_ref[0, c : c + 1, :] * f
        e = mean_ref[1, k : k + 1, :] + carry_ref[1, k : k + 1, :] * e
    block_ref[0:1, :] = f
    block_ref[1:2, :] = e
    f = enter_ref[0]
    e = enter_ref[1]
    for i in range(CHUNK):
        f = a_ref[i] * f + b_ref[i] * chunk_rows(strip_ref, i, chunks)
        mean_ref[i] = f
    for i in reversed(range(CHUNK)):
        smooth_ref[i] = keep_ref[i] * mean_ref[i] + lift_ref[i] * e
        e = alpha_ref[i] * e + beta_ref[i] * chunk_rows(strip_ref, i, chunks)


def finish_kernel(count, me_ref, prior_ref, whole_ref, edge_ref, blocks_ref, mean_ref, smooth_ref, out_mean_ref, out_smooth_ref, mean_strip_ref, smooth_strip_ref):
    steps, modes = out_mean_ref.shape
    chunks = steps // CHUNK
    me = me_ref[0]
    f = prior_ref[...]
    e = jnp.zeros((1, modes), F32)
    for j in range(count - 1):
        at = place(me, j, count)
        f = jnp.where(j < me, blocks_ref[at, 0:1, :] + edge_ref[0, j : j + 1, :] * f, f)
        k = count - 1 - j
        at = place(me, k, count)
        e = jnp.where(k > me, blocks_ref[at, 1:2, :] + edge_ref[1, k : k + 1, :] * e, e)
    f = jnp.broadcast_to(f, (chunks, modes))
    e = jnp.broadcast_to(e, (chunks, modes))
    for i in range(CHUNK):
        put_rows(mean_strip_ref, i, chunks, mean_ref[i] + whole_ref[0, i] * f)
        put_rows(smooth_strip_ref, i, chunks, smooth_ref[i] + whole_ref[1, i] * f + whole_ref[2, i] * e)
    unlanes(mean_strip_ref, out_mean_ref)
    unlanes(smooth_strip_ref, out_smooth_ref)


def project_kernel(at_ref, slab_ref, basis_ref, out_ref, slab_area, basis_area, slab_sems, basis_sems):
    count = slab_ref.shape[0]
    owners, steps, modes = out_ref.shape
    copies = []
    for g in range(count):
        copies.append((
            pltpu.make_async_copy(slab_ref.at[g], slab_area.at[g], slab_sems.at[g]),
            pltpu.make_async_copy(basis_ref.at[at_ref[0] + g], basis_area.at[g], basis_sems.at[g]),
        ))
    for pair in copies:
        for copy in pair:
            copy.start()
    for g in range(count):
        for copy in copies[g]:
            copy.wait()
        for turn in range(owners):
            owner = lax.rem(at_ref[1] + turn, owners)
            columns = pl.ds(pl.multiple_of(owner * modes, LANES), modes)
            term = jnp.dot(slab_area[g], basis_area[g, :, columns], preferred_element_type=F32)
            out_ref[turn] = term if g == 0 else out_ref[turn] + term


def project(slabs, basis, first, side, owners):
    count, steps, cells = slabs.shape
    modes = basis.shape[2] // owners
    return pl.pallas_call(
        project_kernel,
        in_specs=[
            pl.BlockSpec(memory_space=pltpu.SMEM),
            pl.BlockSpec(memory_space=pl.ANY),
            pl.BlockSpec(memory_space=pl.ANY),
        ],
        out_specs=pl.BlockSpec(memory_space=pltpu.VMEM),
        out_shape=jax.ShapeDtypeStruct((owners, steps, modes), F32),
        scratch_shapes=[
            pltpu.VMEM(slabs.shape, slabs.dtype),
            pltpu.VMEM((count,) + basis.shape[1:], basis.dtype),
            pltpu.SemaphoreType.DMA((count,)),
            pltpu.SemaphoreType.DMA((count,)),
        ],
        compiler_params=pltpu.CompilerParams(vmem_limit_bytes=LIMIT),
        cost_estimate=pl.CostEstimate(
            flops=2 * count * steps * cells * modes * owners,
            bytes_accessed=2 * count * cells * (steps + modes * owners) + 4 * steps * modes * owners,
            transcendentals=0,
        ),
    )(jnp.stack([first, side]), slabs, basis)


def call(kernel, inputs, outputs, scratch, flops):
    smem = pl.BlockSpec(memory_space=pltpu.SMEM)
    vmem = pl.BlockSpec(memory_space=pltpu.VMEM)
    moved = sum(4 * x.size for x in inputs) + sum(4 * x.size for x in outputs)
    return pl.pallas_call(
        kernel,
        in_specs=[smem if x.dtype == jnp.int32 else vmem for x in inputs],
        out_specs=[vmem] * len(outputs),
        out_shape=outputs,
        scratch_shapes=scratch,
        compiler_params=pltpu.CompilerParams(vmem_limit_bytes=LIMIT),
        cost_estimate=pl.CostEstimate(flops=flops, bytes_accessed=moved, transcendentals=0),
    )(*inputs)


def swap_halves(block, axis):
    half = lax.axis_size(axis) // 2
    return lax.ppermute(block, axis, [(i, (i + half) % (2 * half)) for i in range(2 * half)])


def sum_over(terms, axis):
    count = lax.axis_size(axis)
    arrived = [
        lax.ppermute(terms[turn], axis, [(i, (i + turn) % count) for i in range(count)]) for turn in range(1, count)
    ]
    return [terms[0]] + arrived


def body(observations, pod_basis, decay, step_mask, process_var, obs_var, prior_mean, prior_var):
    tm_count = lax.axis_size("tm")
    space_count = lax.axis_size("space")
    steps, modes = decay.shape
    chunks = steps // CHUNK
    rank = lax.axis_index("tm").astype(jnp.int32)
    me = rank.reshape(1)
    side = lax.axis_index("space").astype(jnp.int32)
    shape = functools.partial(jax.ShapeDtypeStruct, dtype=F32)
    area = pltpu.VMEM
    group = tm_count // 2
    groups = [[half * group + i for i in range(group)] for half in range(2)]
    half = rank // group

    slabs = observations.reshape(2, group, steps, observations.shape[3])
    basis = pod_basis.reshape(tm_count, -1, pod_basis.shape[3])
    far = lax.dynamic_index_in_dim(slabs, 1 - half, 0, keepdims=False)
    far = lax.all_to_all(far, "tm", 0, 0, axis_index_groups=groups, tiled=True)
    near = lax.dynamic_index_in_dim(slabs, half, 0, keepdims=False)
    near = lax.all_to_all(near, "tm", 0, 0, axis_index_groups=groups, tiled=True)
    far = project(far, basis, half * group, side, space_count)
    crossing = swap_halves(sum(sum_over(far, "space")), "tm")
    near = project(near, basis, half * group, side, space_count)
    parts = sum_over(near, "space") + [crossing]

    seen = jnp.broadcast_to(step_mask.astype(F32)[:, None], (steps, modes))
    q, r = process_var[None, :], obs_var[None, :]
    flat = (chunks, modes)
    deep = (CHUNK, chunks, modes)
    strips = area((modes // LANES, steps, LANES), F32)
    chunk_totals, block_totals = call(
        totals_kernel, (me, decay, seen, q, r), [shape((3,) + flat), shape((3, modes))], [strips] * 2, 40 * steps * modes
    )
    blocks = gather_rows(block_totals, "tm")
    *maps, whole, carry, edge, log_variance = call(
        functools.partial(gains_kernel, tm_count),
        (me, decay, seen, q, r, prior_var[None, :], chunk_totals, blocks),
        [shape(deep)] * 6 + [shape((3,) + deep), shape((2,) + flat), shape((2, tm_count, modes)), shape((steps, modes))],
        [area((2,) + flat, F32), area(deep, F32), area(deep, F32), strips, strips],
        80 * steps * modes,
    )

    coefficients, mean, smooth, ends = call(
        functools.partial(means_kernel, len(parts)),
        (*parts, *maps, carry),
        [shape((steps, modes)), shape(deep), shape(deep), shape((2, modes))],
        [area((2,) + flat, F32), strips],
        12 * steps * modes,
    )
    ends = gather_rows(ends, "tm")
    filtered, smoothed = call(
        functools.partial(finish_kernel, tm_count),
        (me, prior_mean[None, :], whole, edge, ends, mean, smooth),
        [shape((steps, modes))] * 2,
        [strips, strips],
        8 * steps * modes,
    )
    return coefficients, filtered, smoothed, log_variance


def solution(mesh):
    return jax.shard_map(
        body,
        mesh=mesh,
        in_specs=(
            P(None, "tm", "space", None),
            P(None, "space", None, None),
            P("tm", "space"),
            P("tm"),
            P("space"),
            P("space"),
            P("space"),
            P("space"),
        ),
        out_specs=(P("tm", "space"), P("tm", "space"), P("tm", "space"), P("tm", "space")),
        check_vma=False,
    )
```

profile of v0, /device:TPU:0, one launch (start us, length us, event | category | flops | bytes accessed | tf_op | source)
XLA Modules:
  0.0 132.8 jit_solution(957040278869192783)
XLA Ops:
  0.7 3.8 %dynamic-slice_bitcast_fusion = (bf16[8,256,512]{2,1,0:T(8,128)(2,1)S(1)}, bf16[8,256,512]{2,1,0:T(8,128)(2,1)}) fusion(bf16[2,8,256,512]{3,2,1,0:T(8,128)(2,1)} %bitcast.49, s32[]{:T(128)S(6)} %select_n.14, s32[]{:T(128)S(6)} %select_n.13), kind=kLoop, calls=%fused_computation | loop fusion | bytes 8388616 | tf_op jit(solution)/shard_map/jit(dynamic_index_in_dim)/squeeze | solution.py:377
  4.5 31.1 %all_to_all.10.slab_ref = bf16[8,256,512]{2,1,0:T(8,128)(2,1)} all-to-all(bf16[8,256,512]{2,1,0:T(8,128)(2,1)S(1)} %get-tuple-element.40), channel_id=1, replica_groups={{0,2,4,6,8,10,12,14},{16,18,20,22,24,26,28,30},{1,3,5,7,9,11,13,15},{17..., dimensions={0} | all-to-all | bytes 4194304 | tf_op jit(solution)/shard_map/all_to_all | solution.py:378
  35.6 3.7 %all-to-all-start = ((bf16[8,256,512]{2,1,0:T(8,128)(2,1)}), bf16[8,256,512]{2,1,0:T(8,128)(2,1)S(1)}, u32[]{:S(2)}, u32[]{:S(2)}) async-start(bf16[8,256,512]{2,1,0:T(8,128)(2,1)} %get-tuple-element.41), calls=%async_computation | async-start | bytes 4194304 | tf_op jit(solution)/shard_map/all_to_all | solution.py:380
  40.4 1.7 %collective-permute-start.5 = (f32[3,512]{1,0:T(4,128)S(1)}, f32[3,512]{1,0:T(4,128)S(1)}, u32[]{:S(2)}, u32[]{:S(2)}) collective-permute-start(f32[3,512]{1,0:T(4,128)S(1)} %get-tuple-element.23), channel_id=1, source_target_pairs={{0,6},{2,0},{4,2},{6,4},{8,14},{10,8},{12,10},{14,12},{16,22},{18,... | collective-permute-start | bytes 18440 | tf_op jit(solution)/shard_map/ppermute | solution.py:25
  42.7 20.4 %collective-permute-done.5 = f32[3,512]{1,0:T(4,128)S(1)} collective-permute-done((f32[3,512]{1,0:T(4,128)S(1)}, f32[3,512]{1,0:T(4,128)S(1)}, u32[]{:S(2)}, u32[]{:S(2)}) %collective-permute-start.5) | collective-permute-done | bytes 6176 | tf_op jit(solution)/shard_map/ppermute | solution.py:25
  63.1 2.2 %collective-permute-done.4 = f32[3,512]{1,0:T(4,128)S(1)} collective-permute-done((f32[3,512]{1,0:T(4,128)S(1)}, f32[3,512]{1,0:T(4,128)S(1)}, u32[]{:S(2)}, u32[]{:S(2)}) %collective-permute-start.4) | collective-permute-done | bytes 6176 | tf_op jit(solution)/shard_map/ppermute | solution.py:25
  65.4 3.6 %collective-permute-start.8 = (f32[4,3,512]{2,1,0:T(4,128)S(1)}, f32[4,3,512]{2,1,0:T(4,128)S(1)}, u32[]{:S(2)}, u32[]{:S(2)}) collective-permute-start(f32[4,3,512]{2,1,0:T(4,128)S(1)} %pad_maximum_fusion), channel_id=1, source_target_pairs={{0,24},{2,26},{4,28},{6,30},{8,0},{10,2},{12,4},{14,6},{16,8},{18,... | collective-permute-start | bytes 73736 | tf_op jit(solution)/shard_map/ppermute | solution.py:25
  68.9 1.1 collective-permute-start.6
  70.0 1.6 %copy-done = bf16[8,256,512]{2,1,0:T(8,128)(2,1)S(1)} copy-done((bf16[8,256,512]{2,1,0:T(8,128)(2,1)S(1)}, bf16[8,256,512]{2,1,0:T(8,128)(2,1)}, u32[]{:S(2)}) %copy-start) | copy-done | bytes 2097176
  71.6 4.7 %shard_map.112 = f32[2,256,512]{2,1,0:T(8,128)S(1)} custom-call(s32[2]{0:T(128)S(1)} %pad_add_fusion.at_ref, bf16[8,256,512]{2,1,0:T(8,128)(2,1)S(1)} %copy-done, bf16[16,512,1024]{2,1,0:T(8,128)(2,1)} %bitcast.47), custom_call_target="tpu_custom_call" | custom-call | flops 2147483648 | bytes 11534336 | tf_op jit(solution)/shard_map/pallas_call | solution.py:309
  76.3 0.9 slice_bitcast_fusion
  77.2 1.5 %collective-permute-start.1 = (f32[256,512]{1,0:T(8,128)}, f32[256,512]{1,0:T(8,128)}, u32[]{:S(2)}, u32[]{:S(2)}) collective-permute-start(f32[256,512]{1,0:T(8,128)} %slice_bitcast_fusion), channel_id=1, source_target_pairs={{0,1},{1,0},{2,3},{3,2},{4,5},{5,4},{6,7},{7,6},{8,9},{9,8},{10,11... | collective-permute-start | bytes 1572872 | tf_op jit(solution)/shard_map/ppermute | solution.py:356
  78.7 4.7 %shard_map.111 = f32[2,256,512]{2,1,0:T(8,128)S(1)} custom-call(s32[2]{0:T(128)S(1)} %pad_add_fusion.at_ref, bf16[8,256,512]{2,1,0:T(8,128)(2,1)S(1)} %all-to-all-done.slab_ref, bf16[16,512,1024]{2,1,0:T(8,128)(2,1)} %bitcast.48), custom_call_target="tpu_custom_call" | custom-call | flops 2147483648 | bytes 11534336 | tf_op jit(solution)/shard_map/pallas_call | solution.py:309
  84.1 8.3 %collective-permute-done.1 = f32[256,512]{1,0:T(8,128)} collective-permute-done((f32[256,512]{1,0:T(8,128)}, f32[256,512]{1,0:T(8,128)}, u32[]{:S(2)}, u32[]{:S(2)}) %collective-permute-start.1) | collective-permute-done | bytes 524320 | tf_op jit(solution)/shard_map/ppermute | solution.py:356
  92.4 1.1 fusion
  93.5 1.9 %collective-permute-start.2 = (f32[256,512]{1,0:T(8,128)S(1)}, f32[256,512]{1,0:T(8,128)S(1)}, u32[]{:S(2)}, u32[]{:S(2)}) collective-permute-start(f32[256,512]{1,0:T(8,128)S(1)} %fusion), channel_id=1, source_target_pairs={{0,16},{2,18},{4,20},{6,22},{8,24},{10,26},{12,28},{14,30},{16,0},... | collective-permute-start | bytes 1572872 | tf_op jit(solution)/shard_map/ppermute | solution.py:350
  95.5 2.8 %shard_map.114 = (f32[16,16,512]{2,1,0:T(8,128)S(1)}, f32[16,16,512]{2,1,0:T(8,128)S(1)}, f32[16,16,512]{2,1,0:T(8,128)S(1)}, f32[16,16,512]{2,1,0:T(8,128)S(1)}...) custom-call(s32[1]{0:T(128)} %bitcast.10.me_ref, ...), custom_call_target="tpu_custom_call" | custom-call | flops 10485760 | bytes 6625284 | tf_op jit(solution)/shard_map/pallas_call | solution.py:337
  98.3 3.3 %collective-permute-done.refs_1_ = f32[256,512]{1,0:T(8,128)S(1)} collective-permute-done((f32[256,512]{1,0:T(8,128)S(1)}, f32[256,512]{1,0:T(8,128)S(1)}, u32[]{:S(2)}, u32[]{:S(2)}) %collective-permute-start) | collective-permute-done | bytes 524320 | tf_op jit(solution)/shard_map/ppermute | solution.py:356
  101.6 14.2 %collective-permute-done.2.refs_2_ = f32[256,512]{1,0:T(8,128)S(1)} collective-permute-done((f32[256,512]{1,0:T(8,128)S(1)}, f32[256,512]{1,0:T(8,128)S(1)}, u32[]{:S(2)}, u32[]{:S(2)}) %collective-permute-start.2) | collective-permute-done | bytes 524320 | tf_op jit(solution)/shard_map/ppermute | solution.py:350
  115.8 1.7 %shard_map.115 = (f32[256,512]{1,0:T(8,128)}, f32[16,16,512]{2,1,0:T(8,128)S(1)}, f32[16,16,512]{2,1,0:T(8,128)S(1)}, f32[2,512]{1,0:T(2,128)S(1)}) custom-call(f32[256,512]{1,0:T(8,128)S(1)} %get-tuple-element.43.refs_0_, f32[256,512]{1,0:T(8,128)S(1)} %collective-permute-done.refs_1_, f32[256,512]{1,0:T(8,128)S(1)} %collective-permute-done.2.refs_2_, ...), custom_call_target="tpu_custom_call" | custom-call | flops 1572864 | bytes 6361088 | tf_op jit(solution)/shard_map/pallas_call | solution.py:337
  118.8 2.3 %collective-permute-done.10 = f32[2,512]{1,0:T(2,128)S(1)} collective-permute-done((f32[2,512]{1,0:T(2,128)S(1)}, f32[2,512]{1,0:T(2,128)S(1)}, u32[]{:S(2)}, u32[]{:S(2)}) %collective-permute-start.10) | collective-permute-done | bytes 4128 | tf_op jit(solution)/shard_map/ppermute | solution.py:25
  121.1 4.4 %collective-permute-start.14 = (f32[4,2,512]{2,1,0:T(2,128)S(1)}, f32[4,2,512]{2,1,0:T(2,128)S(1)}, u32[]{:S(2)}, u32[]{:S(2)}) collective-permute-start(f32[4,2,512]{2,1,0:T(2,128)S(1)} %pad_maximum_fusion.1), channel_id=1, source_target_pairs={{0,24},{2,26},{4,28},{6,30},{8,0},{10,2},{12,4},{14,6},{16,8},{18,... | collective-permute-start | bytes 49160 | tf_op jit(solution)/shard_map/ppermute | solution.py:25
  126.2 4.9 %collective-permute-done.12 = f32[4,2,512]{2,1,0:T(2,128)S(1)} collective-permute-done((f32[4,2,512]{2,1,0:T(2,128)S(1)}, f32[4,2,512]{2,1,0:T(2,128)S(1)}, u32[]{:S(2)}, u32[]{:S(2)}) %collective-permute-start.12) | collective-permute-done | bytes 16416 | tf_op jit(solution)/shard_map/ppermute | solution.py:25
  131.1 1.7 %shard_map.116 = (f32[256,512]{1,0:T(8,128)}, f32[256,512]{1,0:T(8,128)}) custom-call(s32[1]{0:T(128)} %bitcast.10.me_ref, f32[1,512]{1,0:T(1,128)S(1)} %bitcast.46, f32[3,16,16,512]{3,2,1,0:T(8,128)S(1)} %get-tuple-element.32.whole_ref, f32[2,16,512]{2,1,0:T(8,128)S(1)} %get-tuple-element.33.edge_ref, ...), custom_call_target="tpu_custom_call" | custom-call | flops 1048576 | bytes 3803140 | tf_op jit(solution)/shard_map/pallas_call | solution.py:337
  (56 shorter events, 4.4 us)
Async XLA Ops:
  35.6 3.8 %copy-start.8 = (s32[256]{0:T(256)S(1)}, s32[256]{0:T(256)}, u32[]{:S(2)}) copy-start(s32[256]{0:T(256)} %param.11) | copy-start | bytes 3076
  35.6 3.9 %copy-start.3 = (f32[256,512]{1,0:T(8,128)S(1)}, f32[256,512]{1,0:T(8,128)}, u32[]{:S(2)}) copy-start(f32[256,512]{1,0:T(8,128)} %decay_in.3) | copy-start | bytes 1572868
  35.6 3.9 %copy-start.4 = (f32[512]{0:T(512)S(1)}, f32[512]{0:T(512)}, u32[]{:S(2)}) copy-start(f32[512]{0:T(512)} %param.12) | copy-start | bytes 6148
  35.6 3.9 %copy-start.5 = (f32[512]{0:T(512)S(1)}, f32[512]{0:T(512)}, u32[]{:S(2)}) copy-start(f32[512]{0:T(512)} %param.13) | copy-start | bytes 6148
  35.6 43.1 %all-to-all-start = ((bf16[8,256,512]{2,1,0:T(8,128)(2,1)}), bf16[8,256,512]{2,1,0:T(8,128)(2,1)S(1)}, u32[]{:S(2)}, u32[]{:S(2)}) async-start(bf16[8,256,512]{2,1,0:T(8,128)(2,1)} %get-tuple-element.41), calls=%async_computation | async-start | bytes 4194304 | tf_op jit(solution)/shard_map/all_to_all | solution.py:380
  40.4 22.7 %collective-permute-start.5 = (f32[3,512]{1,0:T(4,128)S(1)}, f32[3,512]{1,0:T(4,128)S(1)}, u32[]{:S(2)}, u32[]{:S(2)}) collective-permute-start(f32[3,512]{1,0:T(4,128)S(1)} %get-tuple-element.23), channel_id=1, source_target_pairs={{0,6},{2,0},{4,2},{6,4},{8,14},{10,8},{12,10},{14,12},{16,22},{18,... | collective-permute-start | bytes 18440 | tf_op jit(solution)/shard_map/ppermute | solution.py:25
  42.2 23.2 %collective-permute-start.4 = (f32[3,512]{1,0:T(4,128)S(1)}, f32[3,512]{1,0:T(4,128)S(1)}, u32[]{:S(2)}, u32[]{:S(2)}) collective-permute-start(f32[3,512]{1,0:T(4,128)S(1)} %get-tuple-element.23), channel_id=1, source_target_pairs={{0,4},{2,6},{4,0},{6,2},{8,12},{10,14},{12,8},{14,10},{16,20},{18,... | collective-permute-start | bytes 18440 | tf_op jit(solution)/shard_map/ppermute | solution.py:25
  42.5 22.8 %collective-permute-start.3 = (f32[3,512]{1,0:T(4,128)S(1)}, f32[3,512]{1,0:T(4,128)S(1)}, u32[]{:S(2)}, u32[]{:S(2)}) collective-permute-start(f32[3,512]{1,0:T(4,128)S(1)} %get-tuple-element.23), channel_id=1, source_target_pairs={{0,2},{2,4},{4,6},{6,0},{8,10},{10,12},{12,14},{14,8},{16,18},{18,... | collective-permute-start | bytes 18440 | tf_op jit(solution)/shard_map/ppermute | solution.py:25
  65.4 30.1 %collective-permute-start.8 = (f32[4,3,512]{2,1,0:T(4,128)S(1)}, f32[4,3,512]{2,1,0:T(4,128)S(1)}, u32[]{:S(2)}, u32[]{:S(2)}) collective-permute-start(f32[4,3,512]{2,1,0:T(4,128)S(1)} %pad_maximum_fusion), channel_id=1, source_target_pairs={{0,24},{2,26},{4,28},{6,30},{8,0},{10,2},{12,4},{14,6},{16,8},{18,... | collective-permute-start | bytes 73736 | tf_op jit(solution)/shard_map/ppermute | solution.py:25
  68.9 26.5 %collective-permute-start.7 = (f32[4,3,512]{2,1,0:T(4,128)S(1)}, f32[4,3,512]{2,1,0:T(4,128)S(1)}, u32[]{:S(2)}, u32[]{:S(2)}) collective-permute-start(f32[4,3,512]{2,1,0:T(4,128)S(1)} %pad_maximum_fusion), channel_id=1, source_target_pairs={{0,16},{2,18},{4,20},{6,22},{8,24},{10,26},{12,28},{14,30},{16,0},... | collective-permute-start | bytes 73736 | tf_op jit(solution)/shard_map/ppermute | solution.py:25
  68.9 26.5 %collective-permute-start.6 = (f32[4,3,512]{2,1,0:T(4,128)S(1)}, f32[4,3,512]{2,1,0:T(4,128)S(1)}, u32[]{:S(2)}, u32[]{:S(2)}) collective-permute-start(f32[4,3,512]{2,1,0:T(4,128)S(1)} %pad_maximum_fusion), channel_id=1, source_target_pairs={{0,8},{2,10},{4,12},{6,14},{8,16},{10,18},{12,20},{14,22},{16,24},... | collective-permute-start | bytes 73736 | tf_op jit(solution)/shard_map/ppermute | solution.py:25
  76.3 2.4 %copy-start.1 = (f32[2,256,512]{2,1,0:T(8,128)}, f32[2,256,512]{2,1,0:T(8,128)S(1)}, u32[]{:S(2)}) copy-start(f32[2,256,512]{2,1,0:T(8,128)S(1)} %shard_map.112) | copy-start | bytes 3145732
  77.2 15.2 %collective-permute-start.1 = (f32[256,512]{1,0:T(8,128)}, f32[256,512]{1,0:T(8,128)}, u32[]{:S(2)}, u32[]{:S(2)}) collective-permute-start(f32[256,512]{1,0:T(8,128)} %slice_bitcast_fusion), channel_id=1, source_target_pairs={{0,1},{1,0},{2,3},{3,2},{4,5},{5,4},{6,7},{7,6},{8,9},{9,8},{10,11... | collective-permute-start | bytes 1572872 | tf_op jit(solution)/shard_map/ppermute | solution.py:356
  83.4 9.0 %copy-start.2 = (f32[2,256,512]{2,1,0:T(8,128)S(1)}, f32[2,256,512]{2,1,0:T(8,128)}, u32[]{:S(2)}) copy-start(f32[2,256,512]{2,1,0:T(8,128)} %copy-done.1) | copy-start | bytes 3145732
  83.4 12.1 %copy-start.6 = (f32[512]{0:T(512)S(1)}, f32[512]{0:T(512)}, u32[]{:S(2)}) copy-start(f32[512]{0:T(512)} %param.15) | copy-start | bytes 6148
  83.5 18.1 %collective-permute-start = (f32[256,512]{1,0:T(8,128)S(1)}, f32[256,512]{1,0:T(8,128)S(1)}, u32[]{:S(2)}, u32[]{:S(2)}) collective-permute-start(f32[256,512]{1,0:T(8,128)S(1)} %get-tuple-element.42), channel_id=1, source_target_pairs={{0,1},{1,0},{2,3},{3,2},{4,5},{5,4},{6,7},{7,6},{8,9},{9,8},{10,11... | collective-permute-start | bytes 1572872 | tf_op jit(solution)/shard_map/ppermute | solution.py:356
  93.5 22.3 %collective-permute-start.2 = (f32[256,512]{1,0:T(8,128)S(1)}, f32[256,512]{1,0:T(8,128)S(1)}, u32[]{:S(2)}, u32[]{:S(2)}) collective-permute-start(f32[256,512]{1,0:T(8,128)S(1)} %fusion), channel_id=1, source_target_pairs={{0,16},{2,18},{4,20},{6,22},{8,24},{10,26},{12,28},{14,30},{16,0},... | collective-permute-start | bytes 1572872 | tf_op jit(solution)/shard_map/ppermute | solution.py:350
  115.8 15.3 %copy-start.7 = (f32[512]{0:T(512)S(1)}, f32[512]{0:T(512)}, u32[]{:S(2)}) copy-start(f32[512]{0:T(512)} %param.14) | copy-start | bytes 6148
  117.5 1.3 %collective-permute-start.11 = (f32[2,512]{1,0:T(2,128)S(1)}, f32[2,512]{1,0:T(2,128)S(1)}, u32[]{:S(2)}, u32[]{:S(2)}) collective-permute-start(f32[2,512]{1,0:T(2,128)S(1)} %get-tuple-element.34), channel_id=1, source_target_pairs={{0,6},{2,0},{4,2},{6,4},{8,14},{10,8},{12,10},{14,12},{16,22},{18,... | collective-permute-start | bytes 12296 | tf_op jit(solution)/shard_map/ppermute | solution.py:25
  117.5 3.6 %collective-permute-start.10 = (f32[2,512]{1,0:T(2,128)S(1)}, f32[2,512]{1,0:T(2,128)S(1)}, u32[]{:S(2)}, u32[]{:S(2)}) collective-permute-start(f32[2,512]{1,0:T(2,128)S(1)} %get-tuple-element.34), channel_id=1, source_target_pairs={{0,4},{2,6},{4,0},{6,2},{8,12},{10,14},{12,8},{14,10},{16,20},{18,... | collective-permute-start | bytes 12296 | tf_op jit(solution)/shard_map/ppermute | solution.py:25
  118.0 3.1 %collective-permute-start.9 = (f32[2,512]{1,0:T(2,128)S(1)}, f32[2,512]{1,0:T(2,128)S(1)}, u32[]{:S(2)}, u32[]{:S(2)}) collective-permute-start(f32[2,512]{1,0:T(2,128)S(1)} %get-tuple-element.34), channel_id=1, source_target_pairs={{0,2},{2,4},{4,6},{6,0},{8,10},{10,12},{12,14},{14,8},{16,18},{18,... | collective-permute-start | bytes 12296 | tf_op jit(solution)/shard_map/ppermute | solution.py:25
  121.1 10.0 %collective-permute-start.14 = (f32[4,2,512]{2,1,0:T(2,128)S(1)}, f32[4,2,512]{2,1,0:T(2,128)S(1)}, u32[]{:S(2)}, u32[]{:S(2)}) collective-permute-start(f32[4,2,512]{2,1,0:T(2,128)S(1)} %pad_maximum_fusion.1), channel_id=1, source_target_pairs={{0,24},{2,26},{4,28},{6,30},{8,0},{10,2},{12,4},{14,6},{16,8},{18,... | collective-permute-start | bytes 49160 | tf_op jit(solution)/shard_map/ppermute | solution.py:25
  125.5 5.6 %collective-permute-start.13 = (f32[4,2,512]{2,1,0:T(2,128)S(1)}, f32[4,2,512]{2,1,0:T(2,128)S(1)}, u32[]{:S(2)}, u32[]{:S(2)}) collective-permute-start(f32[4,2,512]{2,1,0:T(2,128)S(1)} %pad_maximum_fusion.1), channel_id=1, source_target_pairs={{0,16},{2,18},{4,20},{6,22},{8,24},{10,26},{12,28},{14,30},{16,0},... | collective-permute-start | bytes 49160 | tf_op jit(solution)/shard_map/ppermute | solution.py:25
  125.5 5.5 %collective-permute-start.12 = (f32[4,2,512]{2,1,0:T(2,128)S(1)}, f32[4,2,512]{2,1,0:T(2,128)S(1)}, u32[]{:S(2)}, u32[]{:S(2)}) collective-permute-start(f32[4,2,512]{2,1,0:T(2,128)S(1)} %pad_maximum_fusion.1), channel_id=1, source_target_pairs={{0,8},{2,10},{4,12},{6,14},{8,16},{10,18},{12,20},{14,22},{16,24},... | collective-permute-start | bytes 49160 | tf_op jit(solution)/shard_map/ppermute | solution.py:25
  (1 other events, 1.6 us)
where the time goes:
time: 133 us
  waiting for transfers between devices  56.1 us (42%)
  blocking collectives  31.1 us (23%)
  starting transfers between devices  20.4 us (15%)
  Pallas kernels  16.4 us (12%)
  local copies, waits for them, and re-layouts  6.65 us (5%)
    all_to_all x1, blocking collectives, body(): far = lax.all_to_all(far, 'tm', 0, 0, axis_index_groups=groups, tiled=True)  31.1 us
    ppermute x12, waiting for transfers between devices, rotate(): return lax.ppermute(block, axis, route)  30.3 us
    ppermute x1, waiting for transfers between devices, swap_halves(): lax.ppermute(block, axis, [(i, (i + half) % (2 * half)) for i in range(2...  14.2 us
    ppermute x12, starting transfers between devices, rotate(): return lax.ppermute(block, axis, route)  12.7 us
    ppermute x2, waiting for transfers between devices, sum_over(): lax.ppermute(terms[turn], axis, [(i, (i + turn) % count) for i in range(c...  11.6 us
    pallas_call x2, Pallas kernels, project(): pl.pallas_call(project_kernel, in_specs=[pl.BlockSpec(memory_space=pltpu....  9.31 us
    pallas_call x4, Pallas kernels, call(): pl.pallas_call(kernel, in_specs=[smem if x.dtype == jnp.int32 else vmem f...  7.06 us
    squeeze x1, local copies, waits for them, and re-layouts, body(): far = lax.dynamic_index_in_dim(slabs, 1 - half, 0, keepdims=False)  3.85 us
  transfers between devices with their start and end apart: 16, of which 8 were waited for; matrix products, arithmetic and copies ran while one was open for 2% of the time, Pallas kernels for 10%

commit v1 on v0

--- a/solution.py
+++ b/solution.py
@@ -267,11 +267,9 @@
     f = prior_ref[...]
     e = jnp.zeros((1, modes), F32)
     for j in range(count - 1):
-        at = place(me, j, count)
-        f = jnp.where(j < me, blocks_ref[at, 0:1, :] + edge_ref[0, j : j + 1, :] * f, f)
+        f = jnp.where(j < me, blocks_ref[j, 0:1, :] + edge_ref[0, j : j + 1, :] * f, f)
         k = count - 1 - j
-        at = place(me, k, count)
-        e = jnp.where(k > me, blocks_ref[at, 1:2, :] + edge_ref[1, k : k + 1, :] * e, e)
+        e = jnp.where(k > me, blocks_ref[k, 1:2, :] + edge_ref[1, k : k + 1, :] * e, e)
     f = jnp.broadcast_to(f, (chunks, modes))
     e = jnp.broadcast_to(e, (chunks, modes))
     for i in range(CHUNK):
@@ -283,12 +281,13 @@
 
 def project_kernel(at_ref, slab_ref, basis_ref, out_ref, slab_area, basis_area, slab_sems, basis_sems):
     count = slab_ref.shape[0]
-    owners, steps, modes = out_ref.shape
+    modes = out_ref.shape[1]
+    columns = pl.ds(pl.multiple_of(at_ref[1] * modes, LANES), modes)
     copies = []
     for g in range(count):
         copies.append((
             pltpu.make_async_copy(slab_ref.at[g], slab_area.at[g], slab_sems.at[g]),
-            pltpu.make_async_copy(basis_ref.at[at_ref[0] + g], basis_area.at[g], basis_sems.at[g]),
+            pltpu.make_async_copy(basis_ref.at[at_ref[0] + g, :, columns], basis_area.at[g], basis_sems.at[g]),
         ))
     for pair in copies:
         for copy in pair:
@@ -296,16 +295,12 @@
     for g in range(count):
         for copy in copies[g]:
             copy.wait()
-        for turn in range(owners):
-            owner = lax.rem(at_ref[1] + turn, owners)
-            columns = pl.ds(pl.multiple_of(owner * modes, LANES), modes)
-            term = jnp.dot(slab_area[g], basis_area[g, :, columns], preferred_element_type=F32)
-            out_ref[turn] = term if g == 0 else out_ref[turn] + term
-
-
-def project(slabs, basis, first, side, owners):
+        term = jnp.dot(slab_area[g], basis_area[g], preferred_element_type=F32)
+        out_ref[...] = term if g == 0 else out_ref[...] + term
+
+
+def project(slabs, basis, first, owner, modes):
     count, steps, cells = slabs.shape
-    modes = basis.shape[2] // owners
     return pl.pallas_call(
         project_kernel,
         in_specs=[
@@ -314,20 +309,20 @@
             pl.BlockSpec(memory_space=pl.ANY),
         ],
         out_specs=pl.BlockSpec(memory_space=pltpu.VMEM),
-        out_shape=jax.ShapeDtypeStruct((owners, steps, modes), F32),
+        out_shape=jax.ShapeDtypeStruct((steps, modes), F32),
         scratch_shapes=[
             pltpu.VMEM(slabs.shape, slabs.dtype),
-            pltpu.VMEM((count,) + basis.shape[1:], basis.dtype),
+            pltpu.VMEM((count, cells, modes), basis.dtype),
             pltpu.SemaphoreType.DMA((count,)),
             pltpu.SemaphoreType.DMA((count,)),
         ],
         compiler_params=pltpu.CompilerParams(vmem_limit_bytes=LIMIT),
         cost_estimate=pl.CostEstimate(
-            flops=2 * count * steps * cells * modes * owners,
-            bytes_accessed=2 * count * cells * (steps + modes * owners) + 4 * steps * modes * owners,
+            flops=2 * count * steps * cells * modes,
+            bytes_accessed=2 * count * cells * (steps + modes) + 4 * steps * modes,
             transcendentals=0,
         ),
-    )(jnp.stack([first, side]), slabs, basis)
+    )(jnp.stack([first, owner]), slabs, basis)
 
 
 def call(kernel, inputs, outputs, scratch, flops):
@@ -350,12 +345,12 @@
     return lax.ppermute(block, axis, [(i, (i + half) % (2 * half)) for i in range(2 * half)])
 
 
-def sum_over(terms, axis):
-    count = lax.axis_size(axis)
-    arrived = [
-        lax.ppermute(terms[turn], axis, [(i, (i + turn) % count) for i in range(count)]) for turn in range(1, count)
-    ]
-    return [terms[0]] + arrived
+def project_all(slabs, basis, first, side, count, modes):
+    arriving = []
+    for turn in range(1, count):
+        theirs = project(slabs, basis, first, lax.rem(side + turn, count), modes)
+        arriving.append(lax.ppermute(theirs, "space", [(i, (i + turn) % count) for i in range(count)]))
+    return [project(slabs, basis, first, side, modes)] + arriving
 
 
 def body(observations, pod_basis, decay, step_mask, process_var, obs_var, prior_mean, prior_var):
@@ -372,26 +367,27 @@
     groups = [[half * group + i for i in range(group)] for half in range(2)]
     half = rank // group
 
-    slabs = observations.reshape(2, group, steps, observations.shape[3])
-    basis = pod_basis.reshape(tm_count, -1, pod_basis.shape[3])
-    far = lax.dynamic_index_in_dim(slabs, 1 - half, 0, keepdims=False)
-    far = lax.all_to_all(far, "tm", 0, 0, axis_index_groups=groups, tiled=True)
-    near = lax.dynamic_index_in_dim(slabs, half, 0, keepdims=False)
-    near = lax.all_to_all(near, "tm", 0, 0, axis_index_groups=groups, tiled=True)
-    far = project(far, basis, half * group, side, space_count)
-    crossing = swap_halves(sum(sum_over(far, "space")), "tm")
-    near = project(near, basis, half * group, side, space_count)
-    parts = sum_over(near, "space") + [crossing]
-
     seen = jnp.broadcast_to(step_mask.astype(F32)[:, None], (steps, modes))
     q, r = process_var[None, :], obs_var[None, :]
     flat = (chunks, modes)
     deep = (CHUNK, chunks, modes)
     strips = area((modes // LANES, steps, LANES), F32)
+    slabs = observations.reshape(2, group, steps, observations.shape[3])
+    basis = pod_basis.reshape(tm_count, -1, pod_basis.shape[3])
+    far = lax.dynamic_index_in_dim(slabs, 1 - half, 0, keepdims=False)
+    far, seen = lax.optimization_barrier((far, seen))
+    far = lax.all_to_all(far, "tm", 0, 0, axis_index_groups=groups, tiled=True)
     chunk_totals, block_totals = call(
         totals_kernel, (me, decay, seen, q, r), [shape((3,) + flat), shape((3, modes))], [strips] * 2, 40 * steps * modes
     )
+    block_totals, own_half = lax.optimization_barrier((block_totals, half))
+    near = lax.dynamic_index_in_dim(slabs, own_half, 0, keepdims=False)
+    far, near, chunk_totals = lax.optimization_barrier((far, near, chunk_totals))
+    near = lax.all_to_all(near, "tm", 0, 0, axis_index_groups=groups, tiled=True)
     blocks = gather_rows(block_totals, "tm")
+    crossing = sum(project_all(far, basis, half * group, side, space_count, modes))
+    crossing, blocks = lax.optimization_barrier((crossing, blocks))
+    crossing = swap_halves(crossing, "tm")
     *maps, whole, carry, edge, log_variance = call(
         functools.partial(gains_kernel, tm_count),
         (me, decay, seen, q, r, prior_var[None, :], chunk_totals, blocks),
@@ -399,6 +395,8 @@
         [area((2,) + flat, F32), area(deep, F32), area(deep, F32), strips, strips],
         80 * steps * modes,
     )
+    near, maps = lax.optimization_barrier((near, maps))
+    parts = project_all(near, basis, half * group, side, space_count, modes) + [crossing]
 
     coefficients, mean, smooth, ends = call(
         functools.partial(means_kernel, len(parts)),
@@ -407,7 +405,8 @@
         [area((2,) + flat, F32), strips],
         12 * steps * modes,
     )
-    ends = gather_rows(ends, "tm")
+    ends = jnp.broadcast_to(ends[None], (tm_count,) + ends.shape)
+    ends = lax.all_to_all(ends, "tm", 0, 0, tiled=True)
     filtered, smoothed = call(
         functools.partial(finish_kernel, tm_count),
         (me, prior_mean[None, :], whole, edge, ends, mean, smooth),

time: 133 us -> 131 us (0.985)
  blocking collectives: 31.1 us -> 10.4 us
  local copies, waits for them, and re-layouts: 6.65 us -> 15.2 us
  Pallas kernels: 16.4 us -> 20.9 us
  waiting for transfers between devices: 56.1 us -> 60.4 us
    all_to_all x0 -> x1, waiting for transfers between devices: none -> 21.7 us  [body(): far = lax.all_to_all(far, 'tm', 0, 0, axis_index_groups=groups, tiled=True)]
    all_to_all x1, blocking collectives: 31.1 us -> 10.4 us  [body(): ends = lax.all_to_all(ends, 'tm', 0, 0, tiled=True)]
    ppermute x1, waiting for transfers between devices: 14.2 us -> 5.23 us  [swap_halves(): lax.ppermute(block, axis, [(i, (i + half) % (2 * half)) for i in range(2...]
    unnamed x30 -> x48, local copies, waits for them, and re-layouts: 1.72 us -> 8.96 us
    ppermute x12 -> x6, waiting for transfers between devices: 30.3 us -> 23.6 us  [rotate(): return lax.ppermute(block, axis, route)]
    ppermute x12 -> x6, starting transfers between devices: 12.7 us -> 6.85 us  [rotate(): return lax.ppermute(block, axis, route)]
    all_to_all x0 -> x1, starting transfers between devices: none -> 5.37 us  [body(): far = lax.all_to_all(far, 'tm', 0, 0, axis_index_groups=groups, tiled=True)]
    pallas_call x2 -> x4, Pallas kernels: 9.31 us -> 13.5 us  [project(): pl.pallas_call(project_kernel, in_specs=[pl.BlockSpec(memory_space=pltpu....]
  transfers between devices with their start and end apart: 16 -> 11, of which waited for: 8 -> 6; matrix products, arithmetic and copies ran while one was open for 2% -> 3% of each run, Pallas kernels for 10% -> 13%
where the time goes in v1:
time: 131 us
  waiting for transfers between devices  60.4 us (46%)
  starting transfers between devices  21.1 us (16%)
  Pallas kernels  20.9 us (16%)
  local copies, waits for them, and re-layouts  15.2 us (12%)
  blocking collectives  10.4 us (8%)
  other arithmetic  1.71 us (1%)
    ppermute x6, waiting for transfers between devices, rotate(): return lax.ppermute(block, axis, route)  23.6 us
    all_to_all x1, waiting for transfers between devices, body(): far = lax.all_to_all(far, 'tm', 0, 0, axis_index_groups=groups, tiled=True)  21.7 us
    pallas_call x4, Pallas kernels, project(): pl.pallas_call(project_kernel, in_specs=[pl.BlockSpec(memory_space=pltpu....  13.5 us
    all_to_all x1, blocking collectives, body(): ends = lax.all_to_all(ends, 'tm', 0, 0, tiled=True)  10.4 us
    ppermute x2, waiting for transfers between devices, project_all(): lax.ppermute(theirs, 'space', [(i, (i + turn) % count) for i in range(cou...  9.83 us
    unnamed x48, local copies, waits for them, and re-layouts  8.96 us
    pallas_call x4, Pallas kernels, call(): pl.pallas_call(kernel, in_specs=[smem if x.dtype == jnp.int32 else vmem f...  7.42 us
    ppermute x6, starting transfers between devices, rotate(): return lax.ppermute(block, axis, route)  6.85 us
  transfers between devices with their start and end apart: 11, of which 6 were waited for; matrix products, arithmetic and copies ran while one was open for 3% of the time, Pallas kernels for 13%

profile of v1, /device:TPU:0, one launch (start us, length us, event | category | flops | bytes accessed | tf_op | source)
XLA Modules:
  0.0 130.7 jit_solution(12109884930810977454)
XLA Ops:
  1.3 3.1 %dynamic-slice_bitcast_fusion.1 = bf16[8,256,512]{2,1,0:T(8,128)(2,1)} fusion(bf16[2,8,256,512]{3,2,1,0:T(8,128)(2,1)} %bitcast.33, s32[]{:T(128)S(6)} %select_n.13), kind=kLoop, calls=%fused_computation.1 | loop fusion | bytes 4194308 | tf_op jit(solution)/shard_map/jit(dynamic_index_in_dim)/squeeze | solution.py:377
  4.5 5.4 %all-to-all-start = ((bf16[8,256,512]{2,1,0:T(8,128)(2,1)}), bf16[8,256,512]{2,1,0:T(8,128)(2,1)S(1)}, u32[]{:S(2)}, u32[]{:S(2)}) async-start(bf16[8,256,512]{2,1,0:T(8,128)(2,1)} %dynamic-slice_bitcast_fusion.1), calls=%async_computation | async-start | bytes 4194304 | tf_op jit(solution)/shard_map/all_to_all | solution.py:379
  10.8 3.1 %dynamic-slice_bitcast_fusion = bf16[8,256,512]{2,1,0:T(8,128)(2,1)} fusion(bf16[2,8,256,512]{3,2,1,0:T(8,128)(2,1)} %bitcast.34, s32[]{:T(128)S(6)} %select_n.14), kind=kLoop, calls=%fused_computation | loop fusion | bytes 4194308 | tf_op jit(solution)/shard_map/jit(dynamic_index_in_dim)/squeeze | solution.py:384
  13.9 21.7 %all-to-all-done.slab_ref = bf16[8,256,512]{2,1,0:T(8,128)(2,1)S(1)} async-done(((bf16[8,256,512]{2,1,0:T(8,128)(2,1)}), bf16[8,256,512]{2,1,0:T(8,128)(2,1)S(1)}, u32[]{:S(2)}, u32[]{:S(2)}) %all-to-all-start) | async-done | bytes 2097184 | tf_op jit(solution)/shard_map/all_to_all | solution.py:379
  36.9 3.6 %all-to-all-start.1 = ((bf16[8,256,512]{2,1,0:T(8,128)(2,1)}), bf16[8,256,512]{2,1,0:T(8,128)(2,1)S(1)}, u32[]{:S(2)}, u32[]{:S(2)}) async-start(bf16[8,256,512]{2,1,0:T(8,128)(2,1)} %dynamic-slice_bitcast_fusion), calls=%async_computation.1 | async-start | bytes 4194304 | tf_op jit(solution)/shard_map/all_to_all | solution.py:386
  40.6 1.7 %collective-permute-start.3 = (f32[3,512]{1,0:T(4,128)S(1)}, f32[3,512]{1,0:T(4,128)S(1)}, u32[]{:S(2)}, u32[]{:S(2)}) collective-permute-start(f32[3,512]{1,0:T(4,128)S(1)} %get-tuple-element.46), channel_id=1, source_target_pairs={{0,6},{2,0},{4,2},{6,4},{8,14},{10,8},{12,10},{14,12},{16,22},{18,... | collective-permute-start | bytes 18440 | tf_op jit(solution)/shard_map/ppermute | solution.py:25
  42.9 21.4 %collective-permute-done.3 = f32[3,512]{1,0:T(4,128)S(1)} collective-permute-done((f32[3,512]{1,0:T(4,128)S(1)}, f32[3,512]{1,0:T(4,128)S(1)}, u32[]{:S(2)}, u32[]{:S(2)}) %collective-permute-start.3) | collective-permute-done | bytes 6176 | tf_op jit(solution)/shard_map/ppermute | solution.py:25
  64.3 2.2 %collective-permute-done.2 = f32[3,512]{1,0:T(4,128)S(1)} collective-permute-done((f32[3,512]{1,0:T(4,128)S(1)}, f32[3,512]{1,0:T(4,128)S(1)}, u32[]{:S(2)}, u32[]{:S(2)}) %collective-permute-start.2) | collective-permute-done | bytes 6176 | tf_op jit(solution)/shard_map/ppermute | solution.py:25
  66.5 3.6 %collective-permute-start.6 = (f32[4,3,512]{2,1,0:T(4,128)S(1)}, f32[4,3,512]{2,1,0:T(4,128)S(1)}, u32[]{:S(2)}, u32[]{:S(2)}) collective-permute-start(f32[4,3,512]{2,1,0:T(4,128)S(1)} %pad_maximum_fusion), channel_id=1, source_target_pairs={{0,24},{2,26},{4,28},{6,30},{8,0},{10,2},{12,4},{14,6},{16,8},{18,... | collective-permute-start | bytes 73736 | tf_op jit(solution)/shard_map/ppermute | solution.py:25
  71.2 1.6 %copy-done.1 = bf16[8,256,512]{2,1,0:T(8,128)(2,1)S(1)} copy-done((bf16[8,256,512]{2,1,0:T(8,128)(2,1)S(1)}, bf16[8,256,512]{2,1,0:T(8,128)(2,1)}, u32[]{:S(2)}) %copy-start.1) | copy-done | bytes 2097176
  72.8 3.4 %shard_map.113 = f32[256,512]{1,0:T(8,128)S(1)} custom-call(s32[2]{0:T(128)S(1)} %pad_add_fusion.1.at_ref, bf16[8,256,512]{2,1,0:T(8,128)(2,1)S(1)} %copy-done.1, bf16[16,512,1024]{2,1,0:T(8,128)(2,1)} %bitcast.29), custom_call_target="tpu_custom_call" | custom-call | flops 1073741824 | bytes 6815744 | tf_op jit(solution)/shard_map/pallas_call | solution.py:304
  76.2 1.6 %collective-permute-start = (f32[256,512]{1,0:T(8,128)S(1)}, f32[256,512]{1,0:T(8,128)S(1)}, u32[]{:S(2)}, u32[]{:S(2)}) collective-permute-start(f32[256,512]{1,0:T(8,128)S(1)} %shard_map.113), channel_id=1, source_target_pairs={{0,1},{1,0},{2,3},{3,2},{4,5},{5,4},{6,7},{7,6},{8,9},{9,8},{10,11... | collective-permute-start | bytes 1572872 | tf_op jit(solution)/shard_map/ppermute | solution.py:352
  77.9 3.4 %shard_map.112 = f32[256,512]{1,0:T(8,128)S(1)} custom-call(s32[2]{0:T(128)S(1)} %pad_add_fusion.at_ref, bf16[8,256,512]{2,1,0:T(8,128)(2,1)S(1)} %copy-done.1, bf16[16,512,1024]{2,1,0:T(8,128)(2,1)} %bitcast.30), custom_call_target="tpu_custom_call" | custom-call | flops 1073741824 | bytes 6815744 | tf_op jit(solution)/shard_map/pallas_call | solution.py:304
  81.2 7.9 %collective-permute-done = f32[256,512]{1,0:T(8,128)S(1)} collective-permute-done((f32[256,512]{1,0:T(8,128)S(1)}, f32[256,512]{1,0:T(8,128)S(1)}, u32[]{:S(2)}, u32[]{:S(2)}) %collective-permute-start) | collective-permute-done | bytes 524320 | tf_op jit(solution)/shard_map/ppermute | solution.py:352
  90.0 2.1 %collective-permute-start.8 = (f32[256,512]{1,0:T(8,128)}, f32[256,512]{1,0:T(8,128)}, u32[]{:S(2)}, u32[]{:S(2)}) collective-permute-start(f32[256,512]{1,0:T(8,128)} %add.19), channel_id=1, source_target_pairs={{0,16},{2,18},{4,20},{6,22},{8,24},{10,26},{12,28},{14,30},{16,0},... | collective-permute-start | bytes 1572872 | tf_op jit(solution)/shard_map/ppermute | solution.py:345
  92.2 2.8 %shard_map.114 = (f32[16,16,512]{2,1,0:T(8,128)S(1)}, f32[16,16,512]{2,1,0:T(8,128)S(1)}, f32[16,16,512]{2,1,0:T(8,128)S(1)}, f32[16,16,512]{2,1,0:T(8,128)S(1)}...) custom-call(s32[1]{0:T(128)} %bitcast.4.me_ref, ...), custom_call_target="tpu_custom_call" | custom-call | flops 10485760 | bytes 6625284 | tf_op jit(solution)/shard_map/pallas_call | solution.py:332
  100.9 3.4 %shard_map.116 = f32[256,512]{1,0:T(8,128)S(1)} custom-call(s32[2]{0:T(128)S(1)} %pad_add_fusion.1.at_ref, bf16[8,256,512]{2,1,0:T(8,128)(2,1)S(1)} %all-to-all-done.1.slab_ref, bf16[16,512,1024]{2,1,0:T(8,128)(2,1)} %bitcast.31), custom_call_target="tpu_custom_call" | custom-call | flops 1073741824 | bytes 6815744 | tf_op jit(solution)/shard_map/pallas_call | solution.py:304
  104.3 1.6 %collective-permute-start.7 = (f32[256,512]{1,0:T(8,128)S(1)}, f32[256,512]{1,0:T(8,128)S(1)}, u32[]{:S(2)}, u32[]{:S(2)}) collective-permute-start(f32[256,512]{1,0:T(8,128)S(1)} %shard_map.116), channel_id=1, source_target_pairs={{0,1},{1,0},{2,3},{3,2},{4,5},{5,4},{6,7},{7,6},{8,9},{9,8},{10,11... | collective-permute-start | bytes 1572872 | tf_op jit(solution)/shard_map/ppermute | solution.py:352
  105.9 3.4 %shard_map.115.refs_0_ = f32[256,512]{1,0:T(8,128)S(1)} custom-call(s32[2]{0:T(128)S(1)} %pad_add_fusion.at_ref, bf16[8,256,512]{2,1,0:T(8,128)(2,1)S(1)} %all-to-all-done.1.slab_ref, bf16[16,512,1024]{2,1,0:T(8,128)(2,1)} %bitcast.32), custom_call_target="tpu_custom_call" | custom-call | flops 1073741824 | bytes 6815744 | tf_op jit(solution)/shard_map/pallas_call | solution.py:304
  109.3 5.2 %collective-permute-done.8.refs_2_ = f32[256,512]{1,0:T(8,128)} collective-permute-done((f32[256,512]{1,0:T(8,128)}, f32[256,512]{1,0:T(8,128)}, u32[]{:S(2)}, u32[]{:S(2)}) %collective-permute-start.8) | collective-permute-done | bytes 524320 | tf_op jit(solution)/shard_map/ppermute | solution.py:345
  114.5 1.9 %collective-permute-done.7.refs_1_ = f32[256,512]{1,0:T(8,128)S(1)} collective-permute-done((f32[256,512]{1,0:T(8,128)S(1)}, f32[256,512]{1,0:T(8,128)S(1)}, u32[]{:S(2)}, u32[]{:S(2)}) %collective-permute-start.7) | collective-permute-done | bytes 524320 | tf_op jit(solution)/shard_map/ppermute | solution.py:352
  116.5 2.1 %shard_map.117 = (f32[256,512]{1,0:T(8,128)}, f32[16,16,512]{2,1,0:T(8,128)S(1)}, f32[16,16,512]{2,1,0:T(8,128)S(1)}, f32[2,512]{1,0:T(2,128)S(1)}) custom-call(f32[256,512]{1,0:T(8,128)S(1)} %shard_map.115.refs_0_, f32[256,512]{1,0:T(8,128)S(1)} %collective-permute-done.7.refs_1_, f32[256,512]{1,0:T(8,128)} %collective-permute-done.8.refs_2_, ...), custom_call_target="tpu_custom_call" | custom-call | flops 1572864 | bytes 6361088 | tf_op jit(solution)/shard_map/pallas_call | solution.py:332
  118.6 10.4 %all_to_all.15.blocks_ref = f32[16,2,512]{2,1,0:T(2,128)S(1)} all-to-all(f32[16,2,512]{2,1,0:T(2,128)S(1)} %broadcast_in_dim.29), channel_id=1, replica_groups=mesh['tm'=16,'space'=2] {'tm'}, dimensions={0} | all-to-all | bytes 131072 | tf_op jit(solution)/shard_map/all_to_all | solution.py:409
  129.0 1.6 %shard_map.118 = (f32[256,512]{1,0:T(8,128)}, f32[256,512]{1,0:T(8,128)}) custom-call(s32[1]{0:T(128)} %bitcast.4.me_ref, f32[1,512]{1,0:T(1,128)S(1)} %bitcast.28, f32[3,16,16,512]{3,2,1,0:T(8,128)S(1)} %copy-done.4, f32[2,16,512]{2,1,0:T(8,128)S(1)} %get-tuple-element.65.edge_ref, f32[16,2,512]{2,1,0:T(2,128)S(1)} %all_to_all.15.blocks_ref, ...), custom_call_target="tpu_custom_call" | custom-call | flops 1048576 | bytes 3803140 | tf_op jit(solution)/shard_map/pallas_call | solution.py:332
  (65 shorter events, 11.7 us)
Async XLA Ops:
  4.5 5.4 %copy-start.2 = (f32[256,512]{1,0:T(8,128)S(1)}, f32[256,512]{1,0:T(8,128)}, u32[]{:S(2)}) copy-start(f32[256,512]{1,0:T(8,128)} %decay_in.3) | copy-start | bytes 1572868
  4.5 5.4 %copy-start.17 = (f32[512]{0:T(512)S(1)}, f32[512]{0:T(512)}, u32[]{:S(2)}) copy-start(f32[512]{0:T(512)} %param.12) | copy-start | bytes 6148
  4.5 5.4 %copy-start.18 = (f32[512]{0:T(512)S(1)}, f32[512]{0:T(512)}, u32[]{:S(2)}) copy-start(f32[512]{0:T(512)} %param.13) | copy-start | bytes 6148
  4.5 31.1 %all-to-all-start = ((bf16[8,256,512]{2,1,0:T(8,128)(2,1)}), bf16[8,256,512]{2,1,0:T(8,128)(2,1)S(1)}, u32[]{:S(2)}, u32[]{:S(2)}) async-start(bf16[8,256,512]{2,1,0:T(8,128)(2,1)} %dynamic-slice_bitcast_fusion.1), calls=%async_computation | async-start | bytes 4194304 | tf_op jit(solution)/shard_map/all_to_all | solution.py:379
  36.9 63.9 %all-to-all-start.1 = ((bf16[8,256,512]{2,1,0:T(8,128)(2,1)}), bf16[8,256,512]{2,1,0:T(8,128)(2,1)S(1)}, u32[]{:S(2)}, u32[]{:S(2)}) async-start(bf16[8,256,512]{2,1,0:T(8,128)(2,1)} %dynamic-slice_bitcast_fusion), calls=%async_computation.1 | async-start | bytes 4194304 | tf_op jit(solution)/shard_map/all_to_all | solution.py:386
  40.6 23.8 %collective-permute-start.3 = (f32[3,512]{1,0:T(4,128)S(1)}, f32[3,512]{1,0:T(4,128)S(1)}, u32[]{:S(2)}, u32[]{:S(2)}) collective-permute-start(f32[3,512]{1,0:T(4,128)S(1)} %get-tuple-element.46), channel_id=1, source_target_pairs={{0,6},{2,0},{4,2},{6,4},{8,14},{10,8},{12,10},{14,12},{16,22},{18,... | collective-permute-start | bytes 18440 | tf_op jit(solution)/shard_map/ppermute | solution.py:25
  42.2 24.3 %collective-permute-start.2 = (f32[3,512]{1,0:T(4,128)S(1)}, f32[3,512]{1,0:T(4,128)S(1)}, u32[]{:S(2)}, u32[]{:S(2)}) collective-permute-start(f32[3,512]{1,0:T(4,128)S(1)} %get-tuple-element.46), channel_id=1, source_target_pairs={{0,4},{2,6},{4,0},{6,2},{8,12},{10,14},{12,8},{14,10},{16,20},{18,... | collective-permute-start | bytes 18440 | tf_op jit(solution)/shard_map/ppermute | solution.py:25
  42.6 23.9 %collective-permute-start.1 = (f32[3,512]{1,0:T(4,128)S(1)}, f32[3,512]{1,0:T(4,128)S(1)}, u32[]{:S(2)}, u32[]{:S(2)}) collective-permute-start(f32[3,512]{1,0:T(4,128)S(1)} %get-tuple-element.46), channel_id=1, source_target_pairs={{0,2},{2,4},{4,6},{6,0},{8,10},{10,12},{12,14},{14,8},{16,18},{18,... | collective-permute-start | bytes 18440 | tf_op jit(solution)/shard_map/ppermute | solution.py:25
  66.5 11.3 %collective-permute-start.6 = (f32[4,3,512]{2,1,0:T(4,128)S(1)}, f32[4,3,512]{2,1,0:T(4,128)S(1)}, u32[]{:S(2)}, u32[]{:S(2)}) collective-permute-start(f32[4,3,512]{2,1,0:T(4,128)S(1)} %pad_maximum_fusion), channel_id=1, source_target_pairs={{0,24},{2,26},{4,28},{6,30},{8,0},{10,2},{12,4},{14,6},{16,8},{18,... | collective-permute-start | bytes 73736 | tf_op jit(solution)/shard_map/ppermute | solution.py:25
  70.1 7.7 %collective-permute-start.5 = (f32[4,3,512]{2,1,0:T(4,128)S(1)}, f32[4,3,512]{2,1,0:T(4,128)S(1)}, u32[]{:S(2)}, u32[]{:S(2)}) collective-permute-start(f32[4,3,512]{2,1,0:T(4,128)S(1)} %pad_maximum_fusion), channel_id=1, source_target_pairs={{0,16},{2,18},{4,20},{6,22},{8,24},{10,26},{12,28},{14,30},{16,0},... | collective-permute-start | bytes 73736 | tf_op jit(solution)/shard_map/ppermute | solution.py:25
  70.1 7.7 %collective-permute-start.4 = (f32[4,3,512]{2,1,0:T(4,128)S(1)}, f32[4,3,512]{2,1,0:T(4,128)S(1)}, u32[]{:S(2)}, u32[]{:S(2)}) collective-permute-start(f32[4,3,512]{2,1,0:T(4,128)S(1)} %pad_maximum_fusion), channel_id=1, source_target_pairs={{0,8},{2,10},{4,12},{6,14},{8,16},{10,18},{12,20},{14,22},{16,24},... | collective-permute-start | bytes 73736 | tf_op jit(solution)/shard_map/ppermute | solution.py:25
  71.2 1.6 %copy-start.1 = (bf16[8,256,512]{2,1,0:T(8,128)(2,1)S(1)}, bf16[8,256,512]{2,1,0:T(8,128)(2,1)}, u32[]{:S(2)}) copy-start(bf16[8,256,512]{2,1,0:T(8,128)(2,1)} %copy-done) | copy-start | bytes 6291460
  76.2 13.0 %collective-permute-start = (f32[256,512]{1,0:T(8,128)S(1)}, f32[256,512]{1,0:T(8,128)S(1)}, u32[]{:S(2)}, u32[]{:S(2)}) collective-permute-start(f32[256,512]{1,0:T(8,128)S(1)} %shard_map.113), channel_id=1, source_target_pairs={{0,1},{1,0},{2,3},{3,2},{4,5},{5,4},{6,7},{7,6},{8,9},{9,8},{10,11... | collective-permute-start | bytes 1572872 | tf_op jit(solution)/shard_map/ppermute | solution.py:352
  77.8 14.3 %copy-start.19 = (f32[512]{0:T(512)S(1)}, f32[512]{0:T(512)}, u32[]{:S(2)}) copy-start(f32[512]{0:T(512)} %param.15) | copy-start | bytes 6148
  90.0 24.5 %collective-permute-start.8 = (f32[256,512]{1,0:T(8,128)}, f32[256,512]{1,0:T(8,128)}, u32[]{:S(2)}, u32[]{:S(2)}) collective-permute-start(f32[256,512]{1,0:T(8,128)} %add.19), channel_id=1, source_target_pairs={{0,16},{2,18},{4,20},{6,22},{8,24},{10,26},{12,28},{14,30},{16,0},... | collective-permute-start | bytes 1572872 | tf_op jit(solution)/shard_map/ppermute | solution.py:345
  104.3 12.1 %copy-start.6 = (f32[16,16,512]{2,1,0:T(8,128)S(1)}, f32[16,16,512]{2,1,0:T(8,128)}, u32[]{:S(2)}) copy-start(f32[16,16,512]{2,1,0:T(8,128)} %copy-done.5) | copy-start | bytes 1572868
  104.3 12.1 %copy-start.8 = (f32[16,16,512]{2,1,0:T(8,128)S(1)}, f32[16,16,512]{2,1,0:T(8,128)}, u32[]{:S(2)}) copy-start(f32[16,16,512]{2,1,0:T(8,128)} %copy-done.7) | copy-start | bytes 1572868
  104.3 12.1 %copy-start.10 = (f32[16,16,512]{2,1,0:T(8,128)S(1)}, f32[16,16,512]{2,1,0:T(8,128)}, u32[]{:S(2)}) copy-start(f32[16,16,512]{2,1,0:T(8,128)} %copy-done.9) | copy-start | bytes 1572868
  104.3 12.1 %copy-start.12 = (f32[16,16,512]{2,1,0:T(8,128)S(1)}, f32[16,16,512]{2,1,0:T(8,128)}, u32[]{:S(2)}) copy-start(f32[16,16,512]{2,1,0:T(8,128)} %copy-done.11) | copy-start | bytes 1572868
  104.3 12.1 %copy-start.14 = (f32[16,16,512]{2,1,0:T(8,128)S(1)}, f32[16,16,512]{2,1,0:T(8,128)}, u32[]{:S(2)}) copy-start(f32[16,16,512]{2,1,0:T(8,128)} %copy-done.13) | copy-start | bytes 1572868
  104.3 12.1 %copy-start.16 = (f32[16,16,512]{2,1,0:T(8,128)S(1)}, f32[16,16,512]{2,1,0:T(8,128)}, u32[]{:S(2)}) copy-start(f32[16,16,512]{2,1,0:T(8,128)} %copy-done.15) | copy-start | bytes 1572868
  104.3 12.1 %collective-permute-start.7 = (f32[256,512]{1,0:T(8,128)S(1)}, f32[256,512]{1,0:T(8,128)S(1)}, u32[]{:S(2)}, u32[]{:S(2)}) collective-permute-start(f32[256,512]{1,0:T(8,128)S(1)} %shard_map.116), channel_id=1, source_target_pairs={{0,1},{1,0},{2,3},{3,2},{4,5},{5,4},{6,7},{7,6},{8,9},{9,8},{10,11... | collective-permute-start | bytes 1572872 | tf_op jit(solution)/shard_map/ppermute | solution.py:352
  116.4 12.6 %copy-start.4 = (f32[3,16,16,512]{3,2,1,0:T(8,128)S(1)}, f32[3,16,16,512]{3,2,1,0:T(8,128)}, u32[]{:S(2)}) copy-start(f32[3,16,16,512]{3,2,1,0:T(8,128)} %copy-done.3) | copy-start | bytes 4718596
  116.4 12.6 %copy-start.20 = (f32[512]{0:T(512)S(1)}, f32[512]{0:T(512)}, u32[]{:S(2)}) copy-start(f32[512]{0:T(512)} %param.14) | copy-start | bytes 6148
  (8 other events, 7.3 us)

commit v2 on v1

--- a/solution.py
+++ b/solution.py
@@ -10,7 +10,7 @@
 CHUNK = 16
 LANES = 128
 F32 = jnp.float32
-LIMIT = 48 * 1024 * 1024
+LIMIT = 16 * 1024 * 1024
 
 
 def rotate(block, axis, turn, count, group, outer):
@@ -32,12 +32,16 @@
     return group if count % group == 0 else count
 
 
-def gather_rows(rows, axis):
+def gather_near(rows, axis):
     count = lax.axis_size(axis)
     group = inner_size(count)
-    near = jnp.stack([rows] + [rotate(rows, axis, s, count, group, False) for s in range(1, group)])
-    far = [near] + [rotate(near, axis, s, count, group, True) for s in range(1, count // group)]
-    return jnp.concatenate(far, 0)
+    return jnp.stack([rows] + [rotate(rows, axis, s, count, group, False) for s in range(1, group)])
+
+
+def gather_far(near, axis):
+    count = lax.axis_size(axis)
+    group = inner_size(count)
+    return [rotate(near, axis, s, count, group, True) for s in range(1, count // group)]
 
 
 def place(me, j, count):
@@ -279,50 +283,55 @@
     unlanes(smooth_strip_ref, out_smooth_ref)
 
 
-def project_kernel(at_ref, slab_ref, basis_ref, out_ref, slab_area, basis_area, slab_sems, basis_sems):
-    count = slab_ref.shape[0]
+def take_kernel(at_ref, slabs_ref, out_ref, sems):
+    copies = [
+        pltpu.make_async_copy(slabs_ref.at[at_ref[0], g], out_ref.at[g], sems.at[g]) for g in range(out_ref.shape[0])
+    ]
+    for copy in copies:
+        copy.start()
+    for copy in copies:
+        copy.wait()
+
+
+def take(slabs, half, limit):
+    shape = slabs.shape[1:]
+    return pl.pallas_call(
+        take_kernel,
+        in_specs=[pl.BlockSpec(memory_space=pltpu.SMEM), pl.BlockSpec(memory_space=pl.ANY)],
+        out_specs=pl.BlockSpec(memory_space=pl.ANY),
+        out_shape=jax.ShapeDtypeStruct(shape, slabs.dtype),
+        scratch_shapes=[pltpu.SemaphoreType.DMA((shape[0],))],
+        compiler_params=pltpu.CompilerParams(vmem_limit_bytes=limit * LIMIT // 16),
+        cost_estimate=pl.CostEstimate(flops=0, bytes_accessed=2 * slabs.size, transcendentals=0),
+    )(half.reshape(1), slabs)
+
+
+def project_kernel(at_ref, slab_ref, basis_ref, out_ref):
     modes = out_ref.shape[1]
-    columns = pl.ds(pl.multiple_of(at_ref[1] * modes, LANES), modes)
-    copies = []
-    for g in range(count):
-        copies.append((
-            pltpu.make_async_copy(slab_ref.at[g], slab_area.at[g], slab_sems.at[g]),
-            pltpu.make_async_copy(basis_ref.at[at_ref[0] + g, :, columns], basis_area.at[g], basis_sems.at[g]),
-        ))
-    for pair in copies:
-        for copy in pair:
-            copy.start()
-    for g in range(count):
-        for copy in copies[g]:
-            copy.wait()
-        term = jnp.dot(slab_area[g], basis_area[g], preferred_element_type=F32)
+    columns = pl.ds(pl.multiple_of(at_ref[0] * modes, LANES), modes)
+    for g in range(slab_ref.shape[0]):
+        term = jnp.dot(slab_ref[g], basis_ref[g, :, columns], preferred_element_type=F32)
         out_ref[...] = term if g == 0 else out_ref[...] + term
 
 
-def project(slabs, basis, first, owner, modes):
+def project(slabs, basis, owner, modes):
     count, steps, cells = slabs.shape
     return pl.pallas_call(
         project_kernel,
         in_specs=[
             pl.BlockSpec(memory_space=pltpu.SMEM),
-            pl.BlockSpec(memory_space=pl.ANY),
-            pl.BlockSpec(memory_space=pl.ANY),
+            pl.BlockSpec(memory_space=pltpu.VMEM),
+            pl.BlockSpec(memory_space=pltpu.VMEM),
         ],
         out_specs=pl.BlockSpec(memory_space=pltpu.VMEM),
         out_shape=jax.ShapeDtypeStruct((steps, modes), F32),
-        scratch_shapes=[
-            pltpu.VMEM(slabs.shape, slabs.dtype),
-            pltpu.VMEM((count, cells, modes), basis.dtype),
-            pltpu.SemaphoreType.DMA((count,)),
-            pltpu.SemaphoreType.DMA((count,)),
-        ],
-        compiler_params=pltpu.CompilerParams(vmem_limit_bytes=LIMIT),
+        compiler_params=pltpu.CompilerParams(vmem_limit_bytes=2 * LIMIT),
         cost_estimate=pl.CostEstimate(
             flops=2 * count * steps * cells * modes,
             bytes_accessed=2 * count * cells * (steps + modes) + 4 * steps * modes,
             transcendentals=0,
         ),
-    )(jnp.stack([first, owner]), slabs, basis)
+    )(owner.reshape(1), slabs, basis)
 
 
 def call(kernel, inputs, outputs, scratch, flops):
@@ -345,12 +354,12 @@
     return lax.ppermute(block, axis, [(i, (i + half) % (2 * half)) for i in range(2 * half)])
 
 
-def project_all(slabs, basis, first, side, count, modes):
+def project_all(slabs, basis, side, count, modes):
     arriving = []
     for turn in range(1, count):
-        theirs = project(slabs, basis, first, lax.rem(side + turn, count), modes)
+        theirs = project(slabs, basis, lax.rem(side + turn, count), modes)
         arriving.append(lax.ppermute(theirs, "space", [(i, (i + turn) % count) for i in range(count)]))
-    return [project(slabs, basis, first, side, modes)] + arriving
+    return [project(slabs, basis, side, modes)] + arriving
 
 
 def body(observations, pod_basis, decay, step_mask, process_var, obs_var, prior_mean, prior_var):
@@ -373,21 +382,25 @@
     deep = (CHUNK, chunks, modes)
     strips = area((modes // LANES, steps, LANES), F32)
     slabs = observations.reshape(2, group, steps, observations.shape[3])
-    basis = pod_basis.reshape(tm_count, -1, pod_basis.shape[3])
-    far = lax.dynamic_index_in_dim(slabs, 1 - half, 0, keepdims=False)
-    far, seen = lax.optimization_barrier((far, seen))
+    far = take(slabs, 1 - half, 60)
+    far, q = lax.optimization_barrier((far, q))
     far = lax.all_to_all(far, "tm", 0, 0, axis_index_groups=groups, tiled=True)
     chunk_totals, block_totals = call(
         totals_kernel, (me, decay, seen, q, r), [shape((3,) + flat), shape((3, modes))], [strips] * 2, 40 * steps * modes
     )
     block_totals, own_half = lax.optimization_barrier((block_totals, half))
-    near = lax.dynamic_index_in_dim(slabs, own_half, 0, keepdims=False)
-    far, near, chunk_totals = lax.optimization_barrier((far, near, chunk_totals))
+    near = take(slabs, own_half, 60)
+    basis = take(pod_basis.reshape(2, group, -1, pod_basis.shape[3]), own_half, 44)
+    blocks = gather_near(block_totals, "tm")
+    far, near, blocks = lax.optimization_barrier((far, near, blocks))
     near = lax.all_to_all(near, "tm", 0, 0, axis_index_groups=groups, tiled=True)
-    blocks = gather_rows(block_totals, "tm")
-    crossing = sum(project_all(far, basis, half * group, side, space_count, modes))
-    crossing, blocks = lax.optimization_barrier((crossing, blocks))
+    terms = project_all(far, basis, side, space_count, modes)
+    terms[0], blocks = lax.optimization_barrier((terms[0], blocks))
+    rest = gather_far(blocks, "tm")
+    crossing = sum(terms)
+    rest, chunk_totals, _ = lax.optimization_barrier((rest, chunk_totals, crossing))
     crossing = swap_halves(crossing, "tm")
+    blocks = jnp.concatenate([blocks] + rest, 0)
     *maps, whole, carry, edge, log_variance = call(
         functools.partial(gains_kernel, tm_count),
         (me, decay, seen, q, r, prior_var[None, :], chunk_totals, blocks),
@@ -395,8 +408,8 @@
         [area((2,) + flat, F32), area(deep, F32), area(deep, F32), strips, strips],
         80 * steps * modes,
     )
-    near, maps = lax.optimization_barrier((near, maps))
-    parts = project_all(near, basis, half * group, side, space_count, modes) + [crossing]
+    near, carry = lax.optimization_barrier((near, carry))
+    parts = project_all(near, basis, side, space_count, modes) + [crossing]
 
     coefficients, mean, smooth, ends = call(
         functools.partial(means_kernel, len(parts)),

time: 131 us -> 218 us (1.66)
  Pallas kernels: 20.9 us -> 145 us
  waiting for transfers between devices: 60.4 us -> 27.2 us
  local copies, waits for them, and re-layouts: 15.2 us -> 11.3 us
    pallas_call x0 -> x3, Pallas kernels: none -> 133 us  [take(): pl.pallas_call(take_kernel, in_specs=[pl.BlockSpec(memory_space=pltpu.SME...]
    all_to_all x1, waiting for transfers between devices: 21.7 us -> 0.01 us  [body(): far = lax.all_to_all(far, 'tm', 0, 0, axis_index_groups=groups, tiled=True)]
    ppermute x6, waiting for transfers between devices: 23.6 us -> 8.99 us  [rotate(): return lax.ppermute(block, axis, route)]
    pallas_call x4, Pallas kernels: 13.5 us -> 4.98 us  [project(): pl.pallas_call(project_kernel, in_specs=[pl.BlockSpec(memory_space=pltpu....]
    ppermute x2, waiting for transfers between devices: 9.83 us -> 18 us  [project_all(): lax.ppermute(theirs, 'space', [(i, (i + turn) % count) for i in range(cou...]
    squeeze x2 -> x0, local copies, waits for them, and re-layouts: 6.15 us -> none  [the longest x1 3.09 us: body(): near = lax.dynamic_index_in_dim(slabs, own_half, 0, keepdims=False)]
    ppermute x1, waiting for transfers between devices: 5.23 us -> 0.19 us  [swap_halves(): lax.ppermute(block, axis, [(i, (i + half) % (2 * half)) for i in range(2...]
    unnamed x48, local copies, waits for them, and re-layouts: 8.96 us -> 11.2 us
  transfers between devices with their start and end apart: 11 -> 11, of which waited for: 6 -> 4; matrix products, arithmetic and copies ran while one was open for 3% -> 0% of each run, Pallas kernels for 13% -> 35%
where the time goes in v2:
time: 218 us; the launch traced here: 217 us
  Pallas kernels  145 us (67%)
  waiting for transfers between devices  27.2 us (12%)
  starting transfers between devices  22.2 us (10%)
  local copies, waits for them, and re-layouts  11.3 us (5%)
  blocking collectives  9.48 us (4%)
    pallas_call x3, Pallas kernels, take(): pl.pallas_call(take_kernel, in_specs=[pl.BlockSpec(memory_space=pltpu.SME...  133 us
    ppermute x2, waiting for transfers between devices, project_all(): lax.ppermute(theirs, 'space', [(i, (i + turn) % count) for i in range(cou...  18 us
    unnamed x48, local copies, waits for them, and re-layouts  11.2 us
    all_to_all x1, blocking collectives, body(): ends = lax.all_to_all(ends, 'tm', 0, 0, tiled=True)  9.48 us
    ppermute x6, waiting for transfers between devices, rotate(): return lax.ppermute(block, axis, route)  8.99 us
    pallas_call x4, Pallas kernels, call(): pl.pallas_call(kernel, in_specs=[smem if x.dtype == jnp.int32 else vmem f...  7.4 us
    ppermute x6, starting transfers between devices, rotate(): return lax.ppermute(block, axis, route)  7.07 us
    all_to_all x1, starting transfers between devices, body(): far = lax.all_to_all(far, 'tm', 0, 0, axis_index_groups=groups, tiled=True)  5.37 us
  transfers between devices with their start and end apart: 11, of which 4 were waited for; matrix products, arithmetic and copies ran while one was open for 0% of the time, Pallas kernels for 35%

profile of v2, /device:TPU:0, one launch (start us, length us, event | category | flops | bytes accessed | tf_op | source)
XLA Modules:
  0.0 217.5 jit_solution(6284073645958114886)
XLA Ops:
  0.6 64.7 %shard_map.111 = bf16[8,256,512]{2,1,0:T(8,128)(2,1)} custom-call(s32[1]{0:T(128)} %bitcast.1.at_ref, bf16[2,8,256,512]{3,2,1,0:T(8,128)(2,1)} %bitcast.22), custom_call_target="tpu_custom_call" | custom-call | bytes 4194304 | tf_op jit(solution)/shard_map/pallas_call | solution.py:298
  65.4 5.4 %all-to-all-start = ((bf16[8,256,512]{2,1,0:T(8,128)(2,1)}), bf16[8,256,512]{2,1,0:T(8,128)(2,1)S(1)}, u32[]{:S(2)}, u32[]{:S(2)}) async-start(bf16[8,256,512]{2,1,0:T(8,128)(2,1)} %shard_map.111), calls=%async_computation | async-start | bytes 4194304 | tf_op jit(solution)/shard_map/all_to_all | solution.py:387
  71.8 1.8 collective-permute-start.2
  74.2 64.7 %shard_map.113 = bf16[8,256,512]{2,1,0:T(8,128)(2,1)} custom-call(s32[1]{0:T(128)} %bitcast.6.at_ref, bf16[2,8,256,512]{3,2,1,0:T(8,128)(2,1)} %bitcast.23), custom_call_target="tpu_custom_call" | custom-call | bytes 4194304 | tf_op jit(solution)/shard_map/pallas_call | solution.py:298
  138.9 1.4 copy-done.2
  140.3 4.0 %all-to-all-start.1 = ((bf16[8,256,512]{2,1,0:T(8,128)(2,1)}), bf16[8,256,512]{2,1,0:T(8,128)(2,1)S(1)}, u32[]{:S(2)}, u32[]{:S(2)}) async-start(bf16[8,256,512]{2,1,0:T(8,128)(2,1)} %shard_map.113), calls=%async_computation.1 | async-start | bytes 4194304 | tf_op jit(solution)/shard_map/all_to_all | solution.py:396
  144.3 3.6 %shard_map.114.basis_ref = bf16[8,512,1024]{2,1,0:T(8,128)(2,1)S(1)} custom-call(s32[1]{0:T(128)} %bitcast.6.at_ref, bf16[2,8,512,1024]{3,2,1,0:T(8,128)(2,1)} %bitcast.24), custom_call_target="tpu_custom_call" | custom-call | bytes 16777216 | tf_op jit(solution)/shard_map/pallas_call | solution.py:298
  148.3 1.3 shard_map.116
  149.6 1.6 collective-permute-start.6
  151.2 1.2 shard_map.115
  152.4 4.1 %collective-permute-start.5 = (f32[4,3,512]{2,1,0:T(4,128)S(1)}, f32[4,3,512]{2,1,0:T(4,128)S(1)}, u32[]{:S(2)}, u32[]{:S(2)}) collective-permute-start(f32[4,3,512]{2,1,0:T(4,128)S(1)} %pad_maximum_fusion.1), channel_id=1, source_target_pairs={{0,24},{2,26},{4,28},{6,30},{8,0},{10,2},{12,4},{14,6},{16,8},{18,... | collective-permute-start | bytes 73736 | tf_op jit(solution)/shard_map/ppermute | solution.py:25
  157.2 7.0 %collective-permute-done.6 = f32[256,512]{1,0:T(8,128)S(1)} collective-permute-done((f32[256,512]{1,0:T(8,128)S(1)}, f32[256,512]{1,0:T(8,128)S(1)}, u32[]{:S(2)}, u32[]{:S(2)}) %collective-permute-start.6) | collective-permute-done | bytes 524320 | tf_op jit(solution)/shard_map/ppermute | solution.py:361
  165.1 2.6 %collective-permute-start.8 = (f32[256,512]{1,0:T(8,128)}, f32[256,512]{1,0:T(8,128)}, u32[]{:S(2)}, u32[]{:S(2)}) collective-permute-start(f32[256,512]{1,0:T(8,128)} %add.9), channel_id=1, source_target_pairs={{0,16},{2,18},{4,20},{6,22},{8,24},{10,26},{12,28},{14,30},{16,0},... | collective-permute-start | bytes 1572872 | tf_op jit(solution)/shard_map/ppermute | solution.py:354
  167.7 9.0 %collective-permute-done.5 = f32[4,3,512]{2,1,0:T(4,128)S(1)} collective-permute-done((f32[4,3,512]{2,1,0:T(4,128)S(1)}, f32[4,3,512]{2,1,0:T(4,128)S(1)}, u32[]{:S(2)}, u32[]{:S(2)}) %collective-permute-start.5) | collective-permute-done | bytes 24608 | tf_op jit(solution)/shard_map/ppermute | solution.py:25
  176.7 2.8 %shard_map.117 = (f32[16,16,512]{2,1,0:T(8,128)S(1)}, f32[16,16,512]{2,1,0:T(8,128)S(1)}, f32[16,16,512]{2,1,0:T(8,128)S(1)}, f32[16,16,512]{2,1,0:T(8,128)S(1)}...) custom-call(s32[1]{0:T(128)} %bitcast.4.me_ref, ...), custom_call_target="tpu_custom_call" | custom-call | flops 10485760 | bytes 6625284 | tf_op jit(solution)/shard_map/pallas_call | solution.py:341
  179.5 1.2 copy-done.5
  185.5 3.4 %copy-done.1 = bf16[8,512,1024]{2,1,0:T(8,128)(2,1)S(1)} copy-done((bf16[8,512,1024]{2,1,0:T(8,128)(2,1)S(1)}, bf16[8,512,1024]{2,1,0:T(8,128)(2,1)}, u32[]{:S(2)}) %copy-start.1) | copy-done | bytes 8388632
  188.9 1.2 shard_map.119
  190.2 1.6 collective-permute-start.7
  191.8 1.2 shard_map.118.refs_0_
  193.2 11.0 %collective-permute-done.7.refs_1_ = f32[256,512]{1,0:T(8,128)S(1)} collective-permute-done((f32[256,512]{1,0:T(8,128)S(1)}, f32[256,512]{1,0:T(8,128)S(1)}, u32[]{:S(2)}, u32[]{:S(2)}) %collective-permute-start.7) | collective-permute-done | bytes 524320 | tf_op jit(solution)/shard_map/ppermute | solution.py:361
  204.3 2.1 shard_map.120
  206.4 9.5 %all_to_all.15.blocks_ref = f32[16,2,512]{2,1,0:T(2,128)S(1)} all-to-all(f32[16,2,512]{2,1,0:T(2,128)S(1)} %broadcast_in_dim.29), channel_id=1, replica_groups=mesh['tm'=16,'space'=2] {'tm'}, dimensions={0} | all-to-all | bytes 131072 | tf_op jit(solution)/shard_map/all_to_all | solution.py:422
  215.9 1.6 shard_map.121
  (64 shorter events, 8.6 us)
Async XLA Ops:
  65.4 5.4 %copy-start.23 = (s32[256]{0:T(256)S(1)}, s32[256]{0:T(256)}, u32[]{:S(2)}) copy-start(s32[256]{0:T(256)} %param.11) | copy-start | bytes 3076
  65.4 5.5 %copy-start.4 = (f32[256,512]{1,0:T(8,128)S(1)}, f32[256,512]{1,0:T(8,128)}, u32[]{:S(2)}) copy-start(f32[256,512]{1,0:T(8,128)} %decay_in.3) | copy-start | bytes 1572868
  65.4 5.5 %copy-start.19 = (f32[512]{0:T(512)S(1)}, f32[512]{0:T(512)}, u32[]{:S(2)}) copy-start(f32[512]{0:T(512)} %param.12) | copy-start | bytes 6148
  65.4 5.5 %copy-start.20 = (f32[512]{0:T(512)S(1)}, f32[512]{0:T(512)}, u32[]{:S(2)}) copy-start(f32[512]{0:T(512)} %param.13) | copy-start | bytes 6148
  65.4 73.5 %all-to-all-start = ((bf16[8,256,512]{2,1,0:T(8,128)(2,1)}), bf16[8,256,512]{2,1,0:T(8,128)(2,1)S(1)}, u32[]{:S(2)}, u32[]{:S(2)}) async-start(bf16[8,256,512]{2,1,0:T(8,128)(2,1)} %shard_map.111), calls=%async_computation | async-start | bytes 4194304 | tf_op jit(solution)/shard_map/all_to_all | solution.py:387
  71.8 67.0 %collective-permute-start.2 = (f32[3,512]{1,0:T(4,128)S(1)}, f32[3,512]{1,0:T(4,128)S(1)}, u32[]{:S(2)}, u32[]{:S(2)}) collective-permute-start(f32[3,512]{1,0:T(4,128)S(1)} %get-tuple-element.41), channel_id=1, source_target_pairs={{0,6},{2,0},{4,2},{6,4},{8,14},{10,8},{12,10},{14,12},{16,22},{18,... | collective-permute-start | bytes 18440 | tf_op jit(solution)/shard_map/ppermute | solution.py:25
  73.6 65.2 %collective-permute-start.1 = (f32[3,512]{1,0:T(4,128)S(1)}, f32[3,512]{1,0:T(4,128)S(1)}, u32[]{:S(2)}, u32[]{:S(2)}) collective-permute-start(f32[3,512]{1,0:T(4,128)S(1)} %get-tuple-element.41), channel_id=1, source_target_pairs={{0,4},{2,6},{4,0},{6,2},{8,12},{10,14},{12,8},{14,10},{16,20},{18,... | collective-permute-start | bytes 18440 | tf_op jit(solution)/shard_map/ppermute | solution.py:25
  74.0 64.9 %collective-permute-start = (f32[3,512]{1,0:T(4,128)S(1)}, f32[3,512]{1,0:T(4,128)S(1)}, u32[]{:S(2)}, u32[]{:S(2)}) collective-permute-start(f32[3,512]{1,0:T(4,128)S(1)} %get-tuple-element.41), channel_id=1, source_target_pairs={{0,2},{2,4},{4,6},{6,0},{8,10},{10,12},{12,14},{14,8},{16,18},{18,... | collective-permute-start | bytes 18440 | tf_op jit(solution)/shard_map/ppermute | solution.py:25
  140.3 45.2 %all-to-all-start.1 = ((bf16[8,256,512]{2,1,0:T(8,128)(2,1)}), bf16[8,256,512]{2,1,0:T(8,128)(2,1)S(1)}, u32[]{:S(2)}, u32[]{:S(2)}) async-start(bf16[8,256,512]{2,1,0:T(8,128)(2,1)} %shard_map.113), calls=%async_computation.1 | async-start | bytes 4194304 | tf_op jit(solution)/shard_map/all_to_all | solution.py:396
  149.6 14.6 %collective-permute-start.6 = (f32[256,512]{1,0:T(8,128)S(1)}, f32[256,512]{1,0:T(8,128)S(1)}, u32[]{:S(2)}, u32[]{:S(2)}) collective-permute-start(f32[256,512]{1,0:T(8,128)S(1)} %shard_map.116), channel_id=1, source_target_pairs={{0,1},{1,0},{2,3},{3,2},{4,5},{5,4},{6,7},{7,6},{8,9},{9,8},{10,11... | collective-permute-start | bytes 1572872 | tf_op jit(solution)/shard_map/ppermute | solution.py:361
  151.2 25.5 %copy-start.21 = (f32[512]{0:T(512)S(1)}, f32[512]{0:T(512)}, u32[]{:S(2)}) copy-start(f32[512]{0:T(512)} %param.15) | copy-start | bytes 6148
  152.4 24.2 %collective-permute-start.5 = (f32[4,3,512]{2,1,0:T(4,128)S(1)}, f32[4,3,512]{2,1,0:T(4,128)S(1)}, u32[]{:S(2)}, u32[]{:S(2)}) collective-permute-start(f32[4,3,512]{2,1,0:T(4,128)S(1)} %pad_maximum_fusion.1), channel_id=1, source_target_pairs={{0,24},{2,26},{4,28},{6,30},{8,0},{10,2},{12,4},{14,6},{16,8},{18,... | collective-permute-start | bytes 73736 | tf_op jit(solution)/shard_map/ppermute | solution.py:25
  156.6 20.1 %collective-permute-start.4 = (f32[4,3,512]{2,1,0:T(4,128)S(1)}, f32[4,3,512]{2,1,0:T(4,128)S(1)}, u32[]{:S(2)}, u32[]{:S(2)}) collective-permute-start(f32[4,3,512]{2,1,0:T(4,128)S(1)} %pad_maximum_fusion.1), channel_id=1, source_target_pairs={{0,16},{2,18},{4,20},{6,22},{8,24},{10,26},{12,28},{14,30},{16,0},... | collective-permute-start | bytes 73736 | tf_op jit(solution)/shard_map/ppermute | solution.py:25
  156.6 20.1 %collective-permute-start.3 = (f32[4,3,512]{2,1,0:T(4,128)S(1)}, f32[4,3,512]{2,1,0:T(4,128)S(1)}, u32[]{:S(2)}, u32[]{:S(2)}) collective-permute-start(f32[4,3,512]{2,1,0:T(4,128)S(1)} %pad_maximum_fusion.1), channel_id=1, source_target_pairs={{0,8},{2,10},{4,12},{6,14},{8,16},{10,18},{12,20},{14,22},{16,24},... | collective-permute-start | bytes 73736 | tf_op jit(solution)/shard_map/ppermute | solution.py:25
  165.1 28.1 %collective-permute-start.8 = (f32[256,512]{1,0:T(8,128)}, f32[256,512]{1,0:T(8,128)}, u32[]{:S(2)}, u32[]{:S(2)}) collective-permute-start(f32[256,512]{1,0:T(8,128)} %add.9), channel_id=1, source_target_pairs={{0,16},{2,18},{4,20},{6,22},{8,24},{10,26},{12,28},{14,30},{16,0},... | collective-permute-start | bytes 1572872 | tf_op jit(solution)/shard_map/ppermute | solution.py:354
  190.1 14.1 %copy-start.8 = (f32[16,16,512]{2,1,0:T(8,128)S(1)}, f32[16,16,512]{2,1,0:T(8,128)}, u32[]{:S(2)}) copy-start(f32[16,16,512]{2,1,0:T(8,128)} %copy-done.7) | copy-start | bytes 1572868
  190.1 14.1 %copy-start.10 = (f32[16,16,512]{2,1,0:T(8,128)S(1)}, f32[16,16,512]{2,1,0:T(8,128)}, u32[]{:S(2)}) copy-start(f32[16,16,512]{2,1,0:T(8,128)} %copy-done.9) | copy-start | bytes 1572868
  190.1 14.1 %copy-start.12 = (f32[16,16,512]{2,1,0:T(8,128)S(1)}, f32[16,16,512]{2,1,0:T(8,128)}, u32[]{:S(2)}) copy-start(f32[16,16,512]{2,1,0:T(8,128)} %copy-done.11) | copy-start | bytes 1572868
  190.2 14.1 %copy-start.14 = (f32[16,16,512]{2,1,0:T(8,128)S(1)}, f32[16,16,512]{2,1,0:T(8,128)}, u32[]{:S(2)}) copy-start(f32[16,16,512]{2,1,0:T(8,128)} %copy-done.13) | copy-start | bytes 1572868
  190.2 14.1 %copy-start.16 = (f32[16,16,512]{2,1,0:T(8,128)S(1)}, f32[16,16,512]{2,1,0:T(8,128)}, u32[]{:S(2)}) copy-start(f32[16,16,512]{2,1,0:T(8,128)} %copy-done.15) | copy-start | bytes 1572868
  190.2 14.1 %copy-start.18 = (f32[16,16,512]{2,1,0:T(8,128)S(1)}, f32[16,16,512]{2,1,0:T(8,128)}, u32[]{:S(2)}) copy-start(f32[16,16,512]{2,1,0:T(8,128)} %copy-done.17) | copy-start | bytes 1572868
  190.2 14.0 %collective-permute-start.7 = (f32[256,512]{1,0:T(8,128)S(1)}, f32[256,512]{1,0:T(8,128)S(1)}, u32[]{:S(2)}, u32[]{:S(2)}) collective-permute-start(f32[256,512]{1,0:T(8,128)S(1)} %shard_map.119), channel_id=1, source_target_pairs={{0,1},{1,0},{2,3},{3,2},{4,5},{5,4},{6,7},{7,6},{8,9},{9,8},{10,11... | collective-permute-start | bytes 1572872 | tf_op jit(solution)/shard_map/ppermute | solution.py:361
  204.3 11.6 %copy-start.6 = (f32[3,16,16,512]{3,2,1,0:T(8,128)S(1)}, f32[3,16,16,512]{3,2,1,0:T(8,128)}, u32[]{:S(2)}) copy-start(f32[3,16,16,512]{3,2,1,0:T(8,128)} %copy-done.5) | copy-start | bytes 4718596
  204.3 11.6 %copy-start.22 = (f32[512]{0:T(512)S(1)}, f32[512]{0:T(512)}, u32[]{:S(2)}) copy-start(f32[512]{0:T(512)} %param.14) | copy-start | bytes 6148
  (11 other events, 18.1 us)

commit v3 on v2

--- a/solution.py
+++ b/solution.py
@@ -283,9 +283,35 @@
     unlanes(smooth_strip_ref, out_smooth_ref)
 
 
-def take_kernel(at_ref, slabs_ref, out_ref, sems):
+def cut_kernel(at_ref, slabs_ref, *refs):
+    out_refs, sems = refs[:-1], refs[-1]
+    copies = []
+    for turn, ref in enumerate(out_refs):
+        block = lax.bitwise_xor(at_ref[1], turn)
+        copies.append(pltpu.make_async_copy(slabs_ref.at[at_ref[0], block], ref, sems.at[turn]))
+    for copy in copies:
+        copy.start()
+    for copy in copies:
+        copy.wait()
+
+
+def cut(slabs, half, place, limit):
+    count = slabs.shape[1]
+    shape = slabs.shape[2:]
+    return pl.pallas_call(
+        cut_kernel,
+        in_specs=[pl.BlockSpec(memory_space=pltpu.SMEM), pl.BlockSpec(memory_space=pl.ANY)],
+        out_specs=[pl.BlockSpec(memory_space=pltpu.VMEM)] * count,
+        out_shape=[jax.ShapeDtypeStruct(shape, slabs.dtype)] * count,
+        scratch_shapes=[pltpu.SemaphoreType.DMA((count,))],
+        compiler_params=pltpu.CompilerParams(vmem_limit_bytes=limit * LIMIT // 16),
+        cost_estimate=pl.CostEstimate(flops=0, bytes_accessed=2 * slabs.size, transcendentals=0),
+    )(jnp.stack([half, place]), slabs)
+
+
+def stage_kernel(at_ref, basis_ref, out_ref, sems):
     copies = [
-        pltpu.make_async_copy(slabs_ref.at[at_ref[0], g], out_ref.at[g], sems.at[g]) for g in range(out_ref.shape[0])
+        pltpu.make_async_copy(basis_ref.at[at_ref[0], g], out_ref.at[g], sems.at[g]) for g in range(out_ref.shape[0])
     ]
     for copy in copies:
         copy.start()
@@ -293,36 +319,35 @@
         copy.wait()
 
 
-def take(slabs, half, limit):
-    shape = slabs.shape[1:]
+def stage(basis, half):
+    shape = basis.shape[1:]
     return pl.pallas_call(
-        take_kernel,
+        stage_kernel,
         in_specs=[pl.BlockSpec(memory_space=pltpu.SMEM), pl.BlockSpec(memory_space=pl.ANY)],
-        out_specs=pl.BlockSpec(memory_space=pl.ANY),
-        out_shape=jax.ShapeDtypeStruct(shape, slabs.dtype),
+        out_specs=pl.BlockSpec(memory_space=pltpu.VMEM),
+        out_shape=jax.ShapeDtypeStruct(shape, basis.dtype),
         scratch_shapes=[pltpu.SemaphoreType.DMA((shape[0],))],
-        compiler_params=pltpu.CompilerParams(vmem_limit_bytes=limit * LIMIT // 16),
-        cost_estimate=pl.CostEstimate(flops=0, bytes_accessed=2 * slabs.size, transcendentals=0),
-    )(half.reshape(1), slabs)
-
-
-def project_kernel(at_ref, slab_ref, basis_ref, out_ref):
+        compiler_params=pltpu.CompilerParams(vmem_limit_bytes=44 * LIMIT // 16),
+        cost_estimate=pl.CostEstimate(flops=0, bytes_accessed=2 * basis.size, transcendentals=0),
+    )(half.reshape(1), basis)
+
+
+def project_kernel(at_ref, basis_ref, *refs):
+    slab_refs, out_ref = refs[:-1], refs[-1]
     modes = out_ref.shape[1]
     columns = pl.ds(pl.multiple_of(at_ref[0] * modes, LANES), modes)
-    for g in range(slab_ref.shape[0]):
-        term = jnp.dot(slab_ref[g], basis_ref[g, :, columns], preferred_element_type=F32)
-        out_ref[...] = term if g == 0 else out_ref[...] + term
-
-
-def project(slabs, basis, owner, modes):
-    count, steps, cells = slabs.shape
+    for turn, slab_ref in enumerate(slab_refs):
+        g = lax.bitwise_xor(at_ref[1], turn)
+        term = jnp.dot(slab_ref[...], basis_ref[g, :, columns], preferred_element_type=F32)
+        out_ref[...] = term if turn == 0 else out_ref[...] + term
+
+
+def project(slabs, basis, owner, place, modes):
+    count = len(slabs)
+    steps, cells = slabs[0].shape
     return pl.pallas_call(
         project_kernel,
-        in_specs=[
-            pl.BlockSpec(memory_space=pltpu.SMEM),
-            pl.BlockSpec(memory_space=pltpu.VMEM),
-            pl.BlockSpec(memory_space=pltpu.VMEM),
-        ],
+        in_specs=[pl.BlockSpec(memory_space=pltpu.SMEM)] + [pl.BlockSpec(memory_space=pltpu.VMEM)] * (count + 1),
         out_specs=pl.BlockSpec(memory_space=pltpu.VMEM),
         out_shape=jax.ShapeDtypeStruct((steps, modes), F32),
         compiler_params=pltpu.CompilerParams(vmem_limit_bytes=2 * LIMIT),
@@ -331,7 +356,7 @@
             bytes_accessed=2 * count * cells * (steps + modes) + 4 * steps * modes,
             transcendentals=0,
         ),
-    )(owner.reshape(1), slabs, basis)
+    )(jnp.stack([owner, place]), basis, *slabs)
 
 
 def call(kernel, inputs, outputs, scratch, flops):
@@ -354,12 +379,16 @@
     return lax.ppermute(block, axis, [(i, (i + half) % (2 * half)) for i in range(2 * half)])
 
 
-def project_all(slabs, basis, side, count, modes):
+def project_all(slabs, basis, side, place, count, modes):
     arriving = []
     for turn in range(1, count):
-        theirs = project(slabs, basis, lax.rem(side + turn, count), modes)
+        theirs = project(slabs, basis, lax.rem(side + turn, count), place, modes)
         arriving.append(lax.ppermute(theirs, "space", [(i, (i + turn) % count) for i in range(count)]))
-    return [project(slabs, basis, side, modes)] + arriving
+    return [project(slabs, basis, side, place, modes)] + arriving
+
+
+def swap(block, axis, turn):
+    return lax.ppermute(block, axis, [(i, i ^ turn) for i in range(lax.axis_size(axis))])
 
 
 def body(observations, pod_basis, decay, step_mask, process_var, obs_var, prior_mean, prior_var):
@@ -373,7 +402,6 @@
     shape = functools.partial(jax.ShapeDtypeStruct, dtype=F32)
     area = pltpu.VMEM
     group = tm_count // 2
-    groups = [[half * group + i for i in range(group)] for half in range(2)]
     half = rank // group
 
     seen = jnp.broadcast_to(step_mask.astype(F32)[:, None], (steps, modes))
@@ -382,19 +410,24 @@
     deep = (CHUNK, chunks, modes)
     strips = area((modes // LANES, steps, LANES), F32)
     slabs = observations.reshape(2, group, steps, observations.shape[3])
-    far = take(slabs, 1 - half, 60)
+    inside = lax.rem(rank, group)
+    far = cut(slabs, 1 - half, inside, 58)
     far, q = lax.optimization_barrier((far, q))
-    far = lax.all_to_all(far, "tm", 0, 0, axis_index_groups=groups, tiled=True)
+    turns = list(reversed(range(1, group)))
+    far = [far[0]] + [swap(far[turn], "tm", turn) for turn in range(1, group)]
     chunk_totals, block_totals = call(
         totals_kernel, (me, decay, seen, q, r), [shape((3,) + flat), shape((3, modes))], [strips] * 2, 40 * steps * modes
     )
     block_totals, own_half = lax.optimization_barrier((block_totals, half))
-    near = take(slabs, own_half, 60)
-    basis = take(pod_basis.reshape(2, group, -1, pod_basis.shape[3]), own_half, 44)
+    near = cut(slabs, own_half, inside, 52)
+    basis = stage(pod_basis.reshape(2, group, -1, pod_basis.shape[3]), own_half)
     blocks = gather_near(block_totals, "tm")
-    far, near, blocks = lax.optimization_barrier((far, near, blocks))
-    near = lax.all_to_all(near, "tm", 0, 0, axis_index_groups=groups, tiled=True)
-    terms = project_all(far, basis, side, space_count, modes)
+    near, basis = lax.optimization_barrier((list(near), basis))
+    for turn in turns:
+        far[turn], near[turn], far[0] = lax.optimization_barrier((far[turn], near[turn], far[0]))
+        near[turn] = swap(near[turn], "tm", turn)
+    far[0], blocks = lax.optimization_barrier((far[0], blocks))
+    terms = project_all(far, basis, side, inside, space_count, modes)
     terms[0], blocks = lax.optimization_barrier((terms[0], blocks))
     rest = gather_far(blocks, "tm")
     crossing = sum(terms)
@@ -408,8 +441,8 @@
         [area((2,) + flat, F32), area(deep, F32), area(deep, F32), strips, strips],
         80 * steps * modes,
     )
-    near, carry = lax.optimization_barrier((near, carry))
-    parts = project_all(near, basis, side, space_count, modes) + [crossing]
+    near[0], carry = lax.optimization_barrier((near[0], carry))
+    parts = project_all(near, basis, side, inside, space_count, modes) + [crossing]
 
     coefficients, mean, smooth, ends = call(
         functools.partial(means_kernel, len(parts)),

time: 218 us -> 118 us (0.54)
  Pallas kernels: 145 us -> 24.2 us
  waiting for transfers between devices: 27.2 us -> 50.7 us
  local copies, waits for them, and re-layouts: 11.3 us -> 2.56 us
  starting transfers between devices: 22.2 us -> 27.7 us
    pallas_call x3, Pallas kernels: 133 us -> 9.87 us  [the longest x2 6.36 us: cut(): pl.pallas_call(cut_kernel, in_specs=[pl.BlockSpec(memory_space=pltpu.SMEM...]
    ppermute x0 -> x14, waiting for transfers between devices: none -> 30.6 us  [swap(): lax.ppermute(block, axis, [(i, i ^ turn) for i in range(lax.axis_size(axi...]
    ppermute x0 -> x14, starting transfers between devices: none -> 18.9 us  [swap(): lax.ppermute(block, axis, [(i, i ^ turn) for i in range(lax.axis_size(axi...]
    all_to_all x2 -> x0, starting transfers between devices: 9.35 us -> none  [the longest x1 5.37 us: body(): far = lax.all_to_all(far, 'tm', 0, 0, axis_index_groups=groups, tiled=True)]
    unnamed x48 -> x20, local copies, waits for them, and re-layouts: 11.2 us -> 2.44 us
    ppermute x2, waiting for transfers between devices: 18 us -> 11.5 us  [project_all(): lax.ppermute(theirs, 'space', [(i, (i + turn) % count) for i in range(cou...]
    pallas_call x4, Pallas kernels: 4.98 us -> 7.25 us  [project(): pl.pallas_call(project_kernel, in_specs=[pl.BlockSpec(memory_space=pltpu....]
  transfers between devices with their start and end apart: 11 -> 23, of which waited for: 4 -> 10; matrix products, arithmetic and copies ran while one was open for 0% -> 1% of each run, Pallas kernels for 35% -> 13%
where the time goes in v3:
time: 118 us
  waiting for transfers between devices  50.7 us (43%)
  starting transfers between devices  27.7 us (23%)
  Pallas kernels  24.2 us (21%)
  blocking collectives  10.2 us (9%)
  local copies, waits for them, and re-layouts  2.56 us (2%)
  other arithmetic  1.68 us (1%)
    ppermute x14, waiting for transfers between devices, swap(): lax.ppermute(block, axis, [(i, i ^ turn) for i in range(lax.axis_size(axi...  30.6 us
    ppermute x14, starting transfers between devices, swap(): lax.ppermute(block, axis, [(i, i ^ turn) for i in range(lax.axis_size(axi...  18.9 us
    ppermute x2, waiting for transfers between devices, project_all(): lax.ppermute(theirs, 'space', [(i, (i + turn) % count) for i in range(cou...  11.5 us
    all_to_all x1, blocking collectives, body(): ends = lax.all_to_all(ends, 'tm', 0, 0, tiled=True)  10.2 us
    ppermute x6, waiting for transfers between devices, rotate(): return lax.ppermute(block, axis, route)  8.57 us
    pallas_call x4, Pallas kernels, project(): pl.pallas_call(project_kernel, in_specs=[pl.BlockSpec(memory_space=pltpu....  7.25 us
    pallas_call x4, Pallas kernels, call(): pl.pallas_call(kernel, in_specs=[smem if x.dtype == jnp.int32 else vmem f...  7.1 us
    pallas_call x2, Pallas kernels, cut(): pl.pallas_call(cut_kernel, in_specs=[pl.BlockSpec(memory_space=pltpu.SMEM...  6.36 us
  transfers between devices with their start and end apart: 23, of which 10 were waited for; matrix products, arithmetic and copies ran while one was open for 1% of the time, Pallas kernels for 13%

profile of v3, /device:TPU:0, one launch (start us, length us, event | category | flops | bytes accessed | tf_op | source)
XLA Modules:
  0.0 117.9 jit_solution(16267806405789541954)
XLA Ops:
  1.3 3.5 %shard_map.111 = (bf16[256,512]{1,0:T(8,128)(2,1)}, bf16[256,512]{1,0:T(8,128)(2,1)}, bf16[256,512]{1,0:T(8,128)(2,1)}, bf16[256,512]{1,0:T(8,128)(2,1)}, bf16[2...) custom-call(s32[2]{0:T(128)} %pad_add_fusion.1.at_ref, ...), custom_call_target="tpu_custom_call" | custom-call | bytes 4194304 | tf_op jit(solution)/shard_map/pallas_call | solution.py:301
  4.8 4.0 %collective-permute-start.5 = (bf16[256,512]{1,0:T(8,128)(2,1)}, bf16[256,512]{1,0:T(8,128)(2,1)S(1)}, u32[]{:S(2)}, u32[]{:S(2)}) collective-permute-start(bf16[256,512]{1,0:T(8,128)(2,1)} %get-tuple-element.120), channel_id=1, source_target_pairs={{0,12},{2,14},{4,8},{6,10},{8,4},{10,6},{12,0},{14,2},{16,28},{18,... | collective-permute-start | bytes 786440 | tf_op jit(solution)/shard_map/ppermute | solution.py:391
  13.0 1.7 %collective-permute-start.9 = (f32[3,512]{1,0:T(4,128)S(1)}, f32[3,512]{1,0:T(4,128)S(1)}, u32[]{:S(2)}, u32[]{:S(2)}) collective-permute-start(f32[3,512]{1,0:T(4,128)S(1)} %get-tuple-element.132), channel_id=1, source_target_pairs={{0,6},{2,0},{4,2},{6,4},{8,14},{10,8},{12,10},{14,12},{16,22},{18,... | collective-permute-start | bytes 18440 | tf_op jit(solution)/shard_map/ppermute | solution.py:25
  16.0 5.3 %collective-permute-start = (bf16[256,512]{1,0:T(8,128)(2,1)}, bf16[256,512]{1,0:T(8,128)(2,1)S(1)}, u32[]{:S(2)}, u32[]{:S(2)}) collective-permute-start(bf16[256,512]{1,0:T(8,128)(2,1)} %get-tuple-element.110), channel_id=1, source_target_pairs={{0,2},{2,0},{4,6},{6,4},{8,10},{10,8},{12,14},{14,12},{16,18},{18,... | collective-permute-start | bytes 786440 | tf_op jit(solution)/shard_map/ppermute | solution.py:391
  23.0 1.6 %collective-permute-start.3 = (bf16[256,512]{1,0:T(8,128)(2,1)}, bf16[256,512]{1,0:T(8,128)(2,1)S(1)}, u32[]{:S(2)}, u32[]{:S(2)}) collective-permute-start(bf16[256,512]{1,0:T(8,128)(2,1)} %get-tuple-element.116), channel_id=1, source_target_pairs={{0,8},{2,10},{4,12},{6,14},{8,0},{10,2},{12,4},{14,6},{16,24},{18,... | collective-permute-start | bytes 786440 | tf_op jit(solution)/shard_map/ppermute | solution.py:391
  25.0 2.8 %shard_map.113 = (bf16[256,512]{1,0:T(8,128)(2,1)S(1)}, bf16[256,512]{1,0:T(8,128)(2,1)S(1)}, bf16[256,512]{1,0:T(8,128)(2,1)S(1)}, bf16[256,512]{1,0:T(8,128)(2...) custom-call(s32[2]{0:T(128)S(1)} %pad_add_fusion.2.at_ref, ...), custom_call_target="tpu_custom_call" | custom-call | bytes 4194304 | tf_op jit(solution)/shard_map/pallas_call | solution.py:301
  27.8 3.5 %shard_map.114.basis_ref = bf16[8,512,1024]{2,1,0:T(8,128)(2,1)S(1)} custom-call(s32[1]{0:T(128)} %bitcast.7.at_ref, bf16[2,8,512,1024]{3,2,1,0:T(8,128)(2,1)} %bitcast.23), custom_call_target="tpu_custom_call" | custom-call | bytes 16777216 | tf_op jit(solution)/shard_map/pallas_call | solution.py:324
  31.4 5.7 %collective-permute-done.4.refs_5_ = bf16[256,512]{1,0:T(8,128)(2,1)S(1)} collective-permute-done((bf16[256,512]{1,0:T(8,128)(2,1)}, bf16[256,512]{1,0:T(8,128)(2,1)S(1)}, u32[]{:S(2)}, u32[]{:S(2)}) %collective-permute-start.4) | collective-permute-done | bytes 262176 | tf_op jit(solution)/shard_map/ppermute | solution.py:391
  37.1 1.8 %shard_map.116 = f32[256,512]{1,0:T(8,128)S(1)} custom-call(s32[2]{0:T(128)S(1)} %pad_add_fusion.3.at_ref, bf16[8,512,1024]{2,1,0:T(8,128)(2,1)S(1)} %shard_map.114.basis_ref, bf16[256,512]{1,0:T(8,128)(2,1)S(1)} %copy-done.2, bf16[256,512]{1,0:T(8,128)(2,1)S(1)} %collective-permute-done.refs_1_, bf16[256,512]{1,0:T(8,128)(2,1)S(1)} %collective-permute-done.1.refs_2_, ...), custom_call_target="tpu_custom_call" | custom-call | flops 1073741824 | bytes 6815744 | tf_op jit(solution)/shard_map/pallas_call | solution.py:348
  39.0 1.9 %collective-permute-start.13 = (f32[256,512]{1,0:T(8,128)S(1)}, f32[256,512]{1,0:T(8,128)S(1)}, u32[]{:S(2)}, u32[]{:S(2)}) collective-permute-start(f32[256,512]{1,0:T(8,128)S(1)} %shard_map.116), channel_id=1, source_target_pairs={{0,1},{1,0},{2,3},{3,2},{4,5},{5,4},{6,7},{7,6},{8,9},{9,8},{10,11... | collective-permute-start | bytes 1572872 | tf_op jit(solution)/shard_map/ppermute | solution.py:386
  42.6 1.8 %shard_map.115 = f32[256,512]{1,0:T(8,128)S(1)} custom-call(s32[2]{0:T(128)S(1)} %pad_add_fusion.at_ref, bf16[8,512,1024]{2,1,0:T(8,128)(2,1)S(1)} %shard_map.114.basis_ref, bf16[256,512]{1,0:T(8,128)(2,1)S(1)} %copy-done.2, bf16[256,512]{1,0:T(8,128)(2,1)S(1)} %collective-permute-done.refs_1_, bf16[256,512]{1,0:T(8,128)(2,1)S(1)} %collective-permute-done.1.refs_2_, ...), custom_call_target="tpu_custom_call" | custom-call | flops 1073741824 | bytes 6815744 | tf_op jit(solution)/shard_map/pallas_call | solution.py:348
  44.4 3.6 %collective-permute-start.12 = (f32[4,3,512]{2,1,0:T(4,128)S(1)}, f32[4,3,512]{2,1,0:T(4,128)S(1)}, u32[]{:S(2)}, u32[]{:S(2)}) collective-permute-start(f32[4,3,512]{2,1,0:T(4,128)S(1)} %pad_maximum_fusion.1), channel_id=1, source_target_pairs={{0,24},{2,26},{4,28},{6,30},{8,0},{10,2},{12,4},{14,6},{16,8},{18,... | collective-permute-start | bytes 73736 | tf_op jit(solution)/shard_map/ppermute | solution.py:25
  50.0 2.9 %collective-permute-done.11 = f32[4,3,512]{2,1,0:T(4,128)S(1)} collective-permute-done((f32[4,3,512]{2,1,0:T(4,128)S(1)}, f32[4,3,512]{2,1,0:T(4,128)S(1)}, u32[]{:S(2)}, u32[]{:S(2)}) %collective-permute-start.11) | collective-permute-done | bytes 24608 | tf_op jit(solution)/shard_map/ppermute | solution.py:25
  52.9 2.8 %collective-permute-done.10 = f32[4,3,512]{2,1,0:T(4,128)S(1)} collective-permute-done((f32[4,3,512]{2,1,0:T(4,128)S(1)}, f32[4,3,512]{2,1,0:T(4,128)S(1)}, u32[]{:S(2)}, u32[]{:S(2)}) %collective-permute-start.10) | collective-permute-done | bytes 24608 | tf_op jit(solution)/shard_map/ppermute | solution.py:25
  55.8 1.9 %collective-permute-start.19 = (bf16[256,512]{1,0:T(8,128)(2,1)S(1)}, bf16[256,512]{1,0:T(8,128)(2,1)S(1)}, u32[]{:S(2)}, u32[]{:S(2)}) collective-permute-start(bf16[256,512]{1,0:T(8,128)(2,1)S(1)} %get-tuple-element.156), channel_id=1, source_target_pairs={{0,12},{2,14},{4,8},{6,10},{8,4},{10,6},{12,0},{14,2},{16,28},{18,... | collective-permute-start | bytes 786440 | tf_op jit(solution)/shard_map/ppermute | solution.py:391
  57.7 2.4 %collective-permute-start.20 = (bf16[256,512]{1,0:T(8,128)(2,1)S(1)}, bf16[256,512]{1,0:T(8,128)(2,1)S(1)}, u32[]{:S(2)}, u32[]{:S(2)}) collective-permute-start(bf16[256,512]{1,0:T(8,128)(2,1)S(1)} %copy-done.9), channel_id=1, source_target_pairs={{0,14},{2,12},{4,10},{6,8},{8,6},{10,4},{12,2},{14,0},{16,30},{18,... | collective-permute-start | bytes 786440 | tf_op jit(solution)/shard_map/ppermute | solution.py:391
  60.3 2.8 %shard_map.117 = (f32[16,16,512]{2,1,0:T(8,128)S(1)}, f32[16,16,512]{2,1,0:T(8,128)S(1)}, f32[16,16,512]{2,1,0:T(8,128)S(1)}, f32[16,16,512]{2,1,0:T(8,128)S(1)}...) custom-call(s32[1]{0:T(128)} %bitcast.2.me_ref, ...), custom_call_target="tpu_custom_call" | custom-call | flops 10485760 | bytes 6625284 | tf_op jit(solution)/shard_map/pallas_call | solution.py:366
  65.0 2.1 %collective-permute-done.18.refs_5_ = bf16[256,512]{1,0:T(8,128)(2,1)S(1)} collective-permute-done((bf16[256,512]{1,0:T(8,128)(2,1)S(1)}, bf16[256,512]{1,0:T(8,128)(2,1)S(1)}, u32[]{:S(2)}, u32[]{:S(2)}) %collective-permute-start.18) | collective-permute-done | bytes 262176 | tf_op jit(solution)/shard_map/ppermute | solution.py:391
  67.1 20.2 %collective-permute-done.19.refs_6_ = bf16[256,512]{1,0:T(8,128)(2,1)S(1)} collective-permute-done((bf16[256,512]{1,0:T(8,128)(2,1)S(1)}, bf16[256,512]{1,0:T(8,128)(2,1)S(1)}, u32[]{:S(2)}, u32[]{:S(2)}) %collective-permute-start.19) | collective-permute-done | bytes 262176 | tf_op jit(solution)/shard_map/ppermute | solution.py:391
  88.6 1.8 %shard_map.119 = f32[256,512]{1,0:T(8,128)S(1)} custom-call(s32[2]{0:T(128)S(1)} %pad_add_fusion.3.at_ref, bf16[8,512,1024]{2,1,0:T(8,128)(2,1)S(1)} %shard_map.114.basis_ref, bf16[256,512]{1,0:T(8,128)(2,1)S(1)} %get-tuple-element.150.refs_0_, bf16[256,512]{1,0:T(8,128)(2,1)S(1)} %collective-permute-done.14.refs_1_, ...), custom_call_target="tpu_custom_call" | custom-call | flops 1073741824 | bytes 6815744 | tf_op jit(solution)/shard_map/pallas_call | solution.py:348
  91.0 1.8 %shard_map.118.refs_0_ = f32[256,512]{1,0:T(8,128)S(1)} custom-call(s32[2]{0:T(128)S(1)} %pad_add_fusion.at_ref, bf16[8,512,1024]{2,1,0:T(8,128)(2,1)S(1)} %shard_map.114.basis_ref, bf16[256,512]{1,0:T(8,128)(2,1)S(1)} %get-tuple-element.150.refs_0_, bf16[256,512]{1,0:T(8,128)(2,1)S(1)} %collective-permute-done.14.refs_1_, ...), custom_call_target="tpu_custom_call" | custom-call | flops 1073741824 | bytes 6815744 | tf_op jit(solution)/shard_map/pallas_call | solution.py:348
  92.8 11.5 %collective-permute-done.21.refs_1_ = f32[256,512]{1,0:T(8,128)S(1)} collective-permute-done((f32[256,512]{1,0:T(8,128)S(1)}, f32[256,512]{1,0:T(8,128)S(1)}, u32[]{:S(2)}, u32[]{:S(2)}) %collective-permute-start.21) | collective-permute-done | bytes 524320 | tf_op jit(solution)/shard_map/ppermute | solution.py:386
  104.3 1.8 %shard_map.120 = (f32[256,512]{1,0:T(8,128)}, f32[16,16,512]{2,1,0:T(8,128)S(1)}, f32[16,16,512]{2,1,0:T(8,128)S(1)}, f32[2,512]{1,0:T(2,128)S(1)}) custom-call(f32[256,512]{1,0:T(8,128)S(1)} %shard_map.118.refs_0_, f32[256,512]{1,0:T(8,128)S(1)} %collective-permute-done.21.refs_1_, f32[256,512]{1,0:T(8,128)S(1)} %collective-permute-done.22.refs_2_, ...), custom_call_target="tpu_custom_call" | custom-call | flops 1572864 | bytes 6361088 | tf_op jit(solution)/shard_map/pallas_call | solution.py:366
  106.1 10.2 %all_to_all.5.blocks_ref = f32[16,2,512]{2,1,0:T(2,128)S(1)} all-to-all(f32[16,2,512]{2,1,0:T(2,128)S(1)} %broadcast_in_dim.29), channel_id=1, replica_groups=mesh['tm'=16,'space'=2] {'tm'}, dimensions={0} | all-to-all | bytes 131072 | tf_op jit(solution)/shard_map/all_to_all | solution.py:455
  (64 shorter events, 17.4 us)
Async XLA Ops:
  4.8 18.1 %collective-permute-start.5 = (bf16[256,512]{1,0:T(8,128)(2,1)}, bf16[256,512]{1,0:T(8,128)(2,1)S(1)}, u32[]{:S(2)}, u32[]{:S(2)}) collective-permute-start(bf16[256,512]{1,0:T(8,128)(2,1)} %get-tuple-element.120), channel_id=1, source_target_pairs={{0,12},{2,14},{4,8},{6,10},{8,4},{10,6},{12,0},{14,2},{16,28},{18,... | collective-permute-start | bytes 786440 | tf_op jit(solution)/shard_map/ppermute | solution.py:391
  8.9 15.8 %collective-permute-start.6 = (bf16[256,512]{1,0:T(8,128)(2,1)}, bf16[256,512]{1,0:T(8,128)(2,1)S(1)}, u32[]{:S(2)}, u32[]{:S(2)}) collective-permute-start(bf16[256,512]{1,0:T(8,128)(2,1)} %get-tuple-element.122), channel_id=1, source_target_pairs={{0,14},{2,12},{4,10},{6,8},{8,6},{10,4},{12,2},{14,0},{16,30},{18,... | collective-permute-start | bytes 786440 | tf_op jit(solution)/shard_map/ppermute | solution.py:391
  13.0 3.0 %collective-permute-start.9 = (f32[3,512]{1,0:T(4,128)S(1)}, f32[3,512]{1,0:T(4,128)S(1)}, u32[]{:S(2)}, u32[]{:S(2)}) collective-permute-start(f32[3,512]{1,0:T(4,128)S(1)} %get-tuple-element.132), channel_id=1, source_target_pairs={{0,6},{2,0},{4,2},{6,4},{8,14},{10,8},{12,10},{14,12},{16,22},{18,... | collective-permute-start | bytes 18440 | tf_op jit(solution)/shard_map/ppermute | solution.py:25
  14.6 6.7 %collective-permute-start.8 = (f32[3,512]{1,0:T(4,128)S(1)}, f32[3,512]{1,0:T(4,128)S(1)}, u32[]{:S(2)}, u32[]{:S(2)}) collective-permute-start(f32[3,512]{1,0:T(4,128)S(1)} %get-tuple-element.132), channel_id=1, source_target_pairs={{0,4},{2,6},{4,0},{6,2},{8,12},{10,14},{12,8},{14,10},{16,20},{18,... | collective-permute-start | bytes 18440 | tf_op jit(solution)/shard_map/ppermute | solution.py:25
  14.8 8.1 %collective-permute-start.7 = (f32[3,512]{1,0:T(4,128)S(1)}, f32[3,512]{1,0:T(4,128)S(1)}, u32[]{:S(2)}, u32[]{:S(2)}) collective-permute-start(f32[3,512]{1,0:T(4,128)S(1)} %get-tuple-element.132), channel_id=1, source_target_pairs={{0,2},{2,4},{4,6},{6,0},{8,10},{10,12},{12,14},{14,8},{16,18},{18,... | collective-permute-start | bytes 18440 | tf_op jit(solution)/shard_map/ppermute | solution.py:25
  16.0 21.1 %collective-permute-start = (bf16[256,512]{1,0:T(8,128)(2,1)}, bf16[256,512]{1,0:T(8,128)(2,1)S(1)}, u32[]{:S(2)}, u32[]{:S(2)}) collective-permute-start(bf16[256,512]{1,0:T(8,128)(2,1)} %get-tuple-element.110), channel_id=1, source_target_pairs={{0,2},{2,0},{4,6},{6,4},{8,10},{10,8},{12,14},{14,12},{16,18},{18,... | collective-permute-start | bytes 786440 | tf_op jit(solution)/shard_map/ppermute | solution.py:391
  21.3 15.7 %collective-permute-start.1 = (bf16[256,512]{1,0:T(8,128)(2,1)}, bf16[256,512]{1,0:T(8,128)(2,1)S(1)}, u32[]{:S(2)}, u32[]{:S(2)}) collective-permute-start(bf16[256,512]{1,0:T(8,128)(2,1)} %get-tuple-element.112), channel_id=1, source_target_pairs={{0,4},{2,6},{4,0},{6,2},{8,12},{10,14},{12,8},{14,10},{16,20},{18,... | collective-permute-start | bytes 786440 | tf_op jit(solution)/shard_map/ppermute | solution.py:391
  23.0 14.1 %collective-permute-start.2 = (bf16[256,512]{1,0:T(8,128)(2,1)}, bf16[256,512]{1,0:T(8,128)(2,1)S(1)}, u32[]{:S(2)}, u32[]{:S(2)}) collective-permute-start(bf16[256,512]{1,0:T(8,128)(2,1)} %get-tuple-element.114), channel_id=1, source_target_pairs={{0,6},{2,4},{4,2},{6,0},{8,14},{10,12},{12,10},{14,8},{16,22},{18,... | collective-permute-start | bytes 786440 | tf_op jit(solution)/shard_map/ppermute | solution.py:391
  23.0 14.1 %collective-permute-start.3 = (bf16[256,512]{1,0:T(8,128)(2,1)}, bf16[256,512]{1,0:T(8,128)(2,1)S(1)}, u32[]{:S(2)}, u32[]{:S(2)}) collective-permute-start(bf16[256,512]{1,0:T(8,128)(2,1)} %get-tuple-element.116), channel_id=1, source_target_pairs={{0,8},{2,10},{4,12},{6,14},{8,0},{10,2},{12,4},{14,6},{16,24},{18,... | collective-permute-start | bytes 786440 | tf_op jit(solution)/shard_map/ppermute | solution.py:391
  24.6 12.4 %collective-permute-start.4 = (bf16[256,512]{1,0:T(8,128)(2,1)}, bf16[256,512]{1,0:T(8,128)(2,1)S(1)}, u32[]{:S(2)}, u32[]{:S(2)}) collective-permute-start(bf16[256,512]{1,0:T(8,128)(2,1)} %get-tuple-element.118), channel_id=1, source_target_pairs={{0,10},{2,8},{4,14},{6,12},{8,2},{10,0},{12,6},{14,4},{16,26},{18,... | collective-permute-start | bytes 786440 | tf_op jit(solution)/shard_map/ppermute | solution.py:391
  31.4 26.3 %copy-start.9 = (bf16[256,512]{1,0:T(8,128)(2,1)S(1)}, bf16[256,512]{1,0:T(8,128)(2,1)}, u32[]{:S(2)}) copy-start(bf16[256,512]{1,0:T(8,128)(2,1)} %get-tuple-element.157) | copy-start | bytes 786436
  39.0 18.7 %collective-permute-start.13 = (f32[256,512]{1,0:T(8,128)S(1)}, f32[256,512]{1,0:T(8,128)S(1)}, u32[]{:S(2)}, u32[]{:S(2)}) collective-permute-start(f32[256,512]{1,0:T(8,128)S(1)} %shard_map.116), channel_id=1, source_target_pairs={{0,1},{1,0},{2,3},{3,2},{4,5},{5,4},{6,7},{7,6},{8,9},{9,8},{10,11... | collective-permute-start | bytes 1572872 | tf_op jit(solution)/shard_map/ppermute | solution.py:386
  40.9 14.9 %collective-permute-start.14 = (bf16[256,512]{1,0:T(8,128)(2,1)S(1)}, bf16[256,512]{1,0:T(8,128)(2,1)S(1)}, u32[]{:S(2)}, u32[]{:S(2)}) collective-permute-start(bf16[256,512]{1,0:T(8,128)(2,1)S(1)} %get-tuple-element.151), channel_id=1, source_target_pairs={{0,2},{2,0},{4,6},{6,4},{8,10},{10,8},{12,14},{14,12},{16,18},{18,... | collective-permute-start | bytes 786440 | tf_op jit(solution)/shard_map/ppermute | solution.py:391
  40.9 14.9 %collective-permute-start.15 = (bf16[256,512]{1,0:T(8,128)(2,1)S(1)}, bf16[256,512]{1,0:T(8,128)(2,1)S(1)}, u32[]{:S(2)}, u32[]{:S(2)}) collective-permute-start(bf16[256,512]{1,0:T(8,128)(2,1)S(1)} %get-tuple-element.152), channel_id=1, source_target_pairs={{0,4},{2,6},{4,0},{6,2},{8,12},{10,14},{12,8},{14,10},{16,20},{18,... | collective-permute-start | bytes 786440 | tf_op jit(solution)/shard_map/ppermute | solution.py:391
  44.4 5.2 %collective-permute-start.12 = (f32[4,3,512]{2,1,0:T(4,128)S(1)}, f32[4,3,512]{2,1,0:T(4,128)S(1)}, u32[]{:S(2)}, u32[]{:S(2)}) collective-permute-start(f32[4,3,512]{2,1,0:T(4,128)S(1)} %pad_maximum_fusion.1), channel_id=1, source_target_pairs={{0,24},{2,26},{4,28},{6,30},{8,0},{10,2},{12,4},{14,6},{16,8},{18,... | collective-permute-start | bytes 73736 | tf_op jit(solution)/shard_map/ppermute | solution.py:25
  48.1 4.8 %collective-permute-start.11 = (f32[4,3,512]{2,1,0:T(4,128)S(1)}, f32[4,3,512]{2,1,0:T(4,128)S(1)}, u32[]{:S(2)}, u32[]{:S(2)}) collective-permute-start(f32[4,3,512]{2,1,0:T(4,128)S(1)} %pad_maximum_fusion.1), channel_id=1, source_target_pairs={{0,16},{2,18},{4,20},{6,22},{8,24},{10,26},{12,28},{14,30},{16,0},... | collective-permute-start | bytes 73736 | tf_op jit(solution)/shard_map/ppermute | solution.py:25
  49.7 6.1 %collective-permute-start.10 = (f32[4,3,512]{2,1,0:T(4,128)S(1)}, f32[4,3,512]{2,1,0:T(4,128)S(1)}, u32[]{:S(2)}, u32[]{:S(2)}) collective-permute-start(f32[4,3,512]{2,1,0:T(4,128)S(1)} %pad_maximum_fusion.1), channel_id=1, source_target_pairs={{0,8},{2,10},{4,12},{6,14},{8,16},{10,18},{12,20},{14,22},{16,24},... | collective-permute-start | bytes 73736 | tf_op jit(solution)/shard_map/ppermute | solution.py:25
  52.9 10.2 %collective-permute-start.16 = (bf16[256,512]{1,0:T(8,128)(2,1)S(1)}, bf16[256,512]{1,0:T(8,128)(2,1)S(1)}, u32[]{:S(2)}, u32[]{:S(2)}) collective-permute-start(bf16[256,512]{1,0:T(8,128)(2,1)S(1)} %get-tuple-element.153), channel_id=1, source_target_pairs={{0,6},{2,4},{4,2},{6,0},{8,14},{10,12},{12,10},{14,8},{16,22},{18,... | collective-permute-start | bytes 786440 | tf_op jit(solution)/shard_map/ppermute | solution.py:391
  55.7 9.2 %collective-permute-start.17 = (bf16[256,512]{1,0:T(8,128)(2,1)S(1)}, bf16[256,512]{1,0:T(8,128)(2,1)S(1)}, u32[]{:S(2)}, u32[]{:S(2)}) collective-permute-start(bf16[256,512]{1,0:T(8,128)(2,1)S(1)} %get-tuple-element.154), channel_id=1, source_target_pairs={{0,8},{2,10},{4,12},{6,14},{8,0},{10,2},{12,4},{14,6},{16,24},{18,... | collective-permute-start | bytes 786440 | tf_op jit(solution)/shard_map/ppermute | solution.py:391
  55.8 11.3 %collective-permute-start.18 = (bf16[256,512]{1,0:T(8,128)(2,1)S(1)}, bf16[256,512]{1,0:T(8,128)(2,1)S(1)}, u32[]{:S(2)}, u32[]{:S(2)}) collective-permute-start(bf16[256,512]{1,0:T(8,128)(2,1)S(1)} %get-tuple-element.155), channel_id=1, source_target_pairs={{0,10},{2,8},{4,14},{6,12},{8,2},{10,0},{12,6},{14,4},{16,26},{18,... | collective-permute-start | bytes 786440 | tf_op jit(solution)/shard_map/ppermute | solution.py:391
  55.8 31.5 %collective-permute-start.19 = (bf16[256,512]{1,0:T(8,128)(2,1)S(1)}, bf16[256,512]{1,0:T(8,128)(2,1)S(1)}, u32[]{:S(2)}, u32[]{:S(2)}) collective-permute-start(bf16[256,512]{1,0:T(8,128)(2,1)S(1)} %get-tuple-element.156), channel_id=1, source_target_pairs={{0,12},{2,14},{4,8},{6,10},{8,4},{10,6},{12,0},{14,2},{16,28},{18,... | collective-permute-start | bytes 786440 | tf_op jit(solution)/shard_map/ppermute | solution.py:391
  57.7 30.9 %collective-permute-start.20 = (bf16[256,512]{1,0:T(8,128)(2,1)S(1)}, bf16[256,512]{1,0:T(8,128)(2,1)S(1)}, u32[]{:S(2)}, u32[]{:S(2)}) collective-permute-start(bf16[256,512]{1,0:T(8,128)(2,1)S(1)} %copy-done.9), channel_id=1, source_target_pairs={{0,14},{2,12},{4,10},{6,8},{8,6},{10,4},{12,2},{14,0},{16,30},{18,... | collective-permute-start | bytes 786440 | tf_op jit(solution)/shard_map/ppermute | solution.py:391
  63.1 29.7 %collective-permute-start.22 = (f32[256,512]{1,0:T(8,128)S(1)}, f32[256,512]{1,0:T(8,128)S(1)}, u32[]{:S(2)}, u32[]{:S(2)}) collective-permute-start(f32[256,512]{1,0:T(8,128)S(1)} %add.9), channel_id=1, source_target_pairs={{0,16},{2,18},{4,20},{6,22},{8,24},{10,26},{12,28},{14,30},{16,0},... | collective-permute-start | bytes 1572872 | tf_op jit(solution)/shard_map/ppermute | solution.py:379
  90.4 13.9 %collective-permute-start.21 = (f32[256,512]{1,0:T(8,128)S(1)}, f32[256,512]{1,0:T(8,128)S(1)}, u32[]{:S(2)}, u32[]{:S(2)}) collective-permute-start(f32[256,512]{1,0:T(8,128)S(1)} %shard_map.119), channel_id=1, source_target_pairs={{0,1},{1,0},{2,3},{3,2},{4,5},{5,4},{6,7},{7,6},{8,9},{9,8},{10,11... | collective-permute-start | bytes 1572872 | tf_op jit(solution)/shard_map/ppermute | solution.py:386
  (9 other events, 122.8 us)

commit v4 on v1

--- a/solution.py
+++ b/solution.py
@@ -10,7 +10,7 @@
 CHUNK = 16
 LANES = 128
 F32 = jnp.float32
-LIMIT = 48 * 1024 * 1024
+LIMIT = 16 * 1024 * 1024
 
 
 def rotate(block, axis, turn, count, group, outer):
@@ -32,12 +32,16 @@
     return group if count % group == 0 else count
 
 
-def gather_rows(rows, axis):
+def gather_near(rows, axis):
     count = lax.axis_size(axis)
     group = inner_size(count)
-    near = jnp.stack([rows] + [rotate(rows, axis, s, count, group, False) for s in range(1, group)])
-    far = [near] + [rotate(near, axis, s, count, group, True) for s in range(1, count // group)]
-    return jnp.concatenate(far, 0)
+    return jnp.stack([rows] + [rotate(rows, axis, s, count, group, False) for s in range(1, group)])
+
+
+def gather_far(near, axis):
+    count = lax.axis_size(axis)
+    group = inner_size(count)
+    return [rotate(near, axis, s, count, group, True) for s in range(1, count // group)]
 
 
 def place(me, j, count):
@@ -316,7 +320,7 @@
             pltpu.SemaphoreType.DMA((count,)),
             pltpu.SemaphoreType.DMA((count,)),
         ],
-        compiler_params=pltpu.CompilerParams(vmem_limit_bytes=LIMIT),
+        compiler_params=pltpu.CompilerParams(vmem_limit_bytes=60 * LIMIT // 16),
         cost_estimate=pl.CostEstimate(
             flops=2 * count * steps * cells * modes,
             bytes_accessed=2 * count * cells * (steps + modes) + 4 * steps * modes,
@@ -345,12 +349,9 @@
     return lax.ppermute(block, axis, [(i, (i + half) % (2 * half)) for i in range(2 * half)])
 
 
-def project_all(slabs, basis, first, side, count, modes):
-    arriving = []
-    for turn in range(1, count):
-        theirs = project(slabs, basis, first, lax.rem(side + turn, count), modes)
-        arriving.append(lax.ppermute(theirs, "space", [(i, (i + turn) % count) for i in range(count)]))
-    return [project(slabs, basis, first, side, modes)] + arriving
+def send_along(term, axis, turn):
+    count = lax.axis_size(axis)
+    return lax.ppermute(term, axis, [(i, (i + turn) % count) for i in range(count)])
 
 
 def body(observations, pod_basis, decay, step_mask, process_var, obs_var, prior_mean, prior_var):
@@ -374,20 +375,33 @@
     strips = area((modes // LANES, steps, LANES), F32)
     slabs = observations.reshape(2, group, steps, observations.shape[3])
     basis = pod_basis.reshape(tm_count, -1, pod_basis.shape[3])
+    first = half * group
+    others = [lax.rem(side + turn, space_count) for turn in range(1, space_count)]
     far = lax.dynamic_index_in_dim(slabs, 1 - half, 0, keepdims=False)
-    far, seen = lax.optimization_barrier((far, seen))
+    far, q = lax.optimization_barrier((far, q))
     far = lax.all_to_all(far, "tm", 0, 0, axis_index_groups=groups, tiled=True)
     chunk_totals, block_totals = call(
         totals_kernel, (me, decay, seen, q, r), [shape((3,) + flat), shape((3, modes))], [strips] * 2, 40 * steps * modes
     )
     block_totals, own_half = lax.optimization_barrier((block_totals, half))
     near = lax.dynamic_index_in_dim(slabs, own_half, 0, keepdims=False)
-    far, near, chunk_totals = lax.optimization_barrier((far, near, chunk_totals))
+    blocks = gather_near(block_totals, "tm")
+    far, near, blocks = lax.optimization_barrier((far, near, blocks))
     near = lax.all_to_all(near, "tm", 0, 0, axis_index_groups=groups, tiled=True)
-    blocks = gather_rows(block_totals, "tm")
-    crossing = sum(project_all(far, basis, half * group, side, space_count, modes))
-    crossing, blocks = lax.optimization_barrier((crossing, blocks))
+
+    theirs = [project(far, basis, first, owner, modes) for owner in others]
+    arriving = [send_along(term, "space", turn + 1) for turn, term in enumerate(theirs)]
+    crossing = sum(arriving, project(far, basis, first, side, modes))
+    _, blocks = lax.optimization_barrier((theirs, blocks))
+    rest = gather_far(blocks, "tm")
+    rest, near, _ = lax.optimization_barrier((rest, near, crossing))
     crossing = swap_halves(crossing, "tm")
+    blocks = jnp.concatenate([blocks] + rest, 0)
+
+    theirs = [project(near, basis, first, owner, modes) for owner in others]
+    parts = [send_along(term, "space", turn + 1) for turn, term in enumerate(theirs)] + [crossing]
+    chunk_totals, own_near, _ = lax.optimization_barrier((chunk_totals, near, theirs))
+    parts.append(project(own_near, basis, first, side, modes))
     *maps, whole, carry, edge, log_variance = call(
         functools.partial(gains_kernel, tm_count),
         (me, decay, seen, q, r, prior_var[None, :], chunk_totals, blocks),
@@ -395,8 +409,6 @@
         [area((2,) + flat, F32), area(deep, F32), area(deep, F32), strips, strips],
         80 * steps * modes,
     )
-    near, maps = lax.optimization_barrier((near, maps))
-    parts = project_all(near, basis, half * group, side, space_count, modes) + [crossing]
 
     coefficients, mean, smooth, ends = call(
         functools.partial(means_kernel, len(parts)),

time: 131 us -> 112 us (0.85)
  waiting for transfers between devices: 60.4 us -> 29.4 us
  Pallas kernels: 20.9 us -> 25.6 us
  local copies, waits for them, and re-layouts: 15.2 us -> 18.4 us
  other arithmetic: 1.71 us -> 3.19 us
    all_to_all x1, waiting for transfers between devices: 21.7 us -> 0.01 us  [body(): far = lax.all_to_all(far, 'tm', 0, 0, axis_index_groups=groups, tiled=True)]
    ppermute x2, waiting for transfers between devices: 9.83 us -> 2.93 us  [send_along(): lax.ppermute(term, axis, [(i, (i + turn) % count) for i in range(count)])]
    pallas_call x4, Pallas kernels: 13.5 us -> 18.7 us  [project(): pl.pallas_call(project_kernel, in_specs=[pl.BlockSpec(memory_space=pltpu....]
    ppermute x1, waiting for transfers between devices: 5.23 us -> 0.01 us  [swap_halves(): lax.ppermute(block, axis, [(i, (i + half) % (2 * half)) for i in range(2...]
    unnamed x48 -> x40, local copies, waits for them, and re-layouts: 8.96 us -> 12.1 us
    ppermute x6, waiting for transfers between devices: 23.6 us -> 26.4 us  [rotate(): return lax.ppermute(block, axis, route)]
  transfers between devices with their start and end apart: 11 -> 11, of which waited for: 6 -> 4; matrix products, arithmetic and copies ran while one was open for 3% -> 6% of each run, Pallas kernels for 13% -> 20%
where the time goes in v4:
time: 112 us; the launch traced here: 111 us
  waiting for transfers between devices  29.4 us (26%)
  Pallas kernels  25.6 us (23%)
  starting transfers between devices  22.4 us (20%)
  local copies, waits for them, and re-layouts  18.4 us (16%)
  blocking collectives  11.1 us (10%)
  other arithmetic  3.19 us (3%)
    ppermute x6, waiting for transfers between devices, rotate(): return lax.ppermute(block, axis, route)  26.4 us
    pallas_call x4, Pallas kernels, project(): pl.pallas_call(project_kernel, in_specs=[pl.BlockSpec(memory_space=pltpu....  18.7 us
    unnamed x40, local copies, waits for them, and re-layouts  12.1 us
    all_to_all x1, blocking collectives, body(): ends = lax.all_to_all(ends, 'tm', 0, 0, tiled=True)  11.1 us
    pallas_call x4, Pallas kernels, call(): pl.pallas_call(kernel, in_specs=[smem if x.dtype == jnp.int32 else vmem f...  6.96 us
    ppermute x6, starting transfers between devices, rotate(): return lax.ppermute(block, axis, route)  6.94 us
    all_to_all x1, starting transfers between devices, body(): far = lax.all_to_all(far, 'tm', 0, 0, axis_index_groups=groups, tiled=True)  5.37 us
    all_to_all x1, starting transfers between devices, body(): lax.all_to_all(near, 'tm', 0, 0, axis_index_groups=groups, tiled=True)  4.35 us
  transfers between devices with their start and end apart: 11, of which 4 were waited for; matrix products, arithmetic and copies ran while one was open for 6% of the time, Pallas kernels for 20%

profile of v4, /device:TPU:0, one launch (start us, length us, event | category | flops | bytes accessed | tf_op | source)
XLA Modules:
  0.0 110.9 jit_solution(10375931567702699818)
XLA Ops:
  0.7 3.1 %dynamic-slice_bitcast_fusion.1 = bf16[8,256,512]{2,1,0:T(8,128)(2,1)} fusion(bf16[2,8,256,512]{3,2,1,0:T(8,128)(2,1)} %bitcast.29, s32[]{:T(128)S(6)} %select_n.13), kind=kLoop, calls=%fused_computation.1 | loop fusion | bytes 4194308 | tf_op jit(solution)/shard_map/jit(dynamic_index_in_dim)/squeeze | solution.py:380
  3.7 5.4 %all-to-all-start = ((bf16[8,256,512]{2,1,0:T(8,128)(2,1)}), bf16[8,256,512]{2,1,0:T(8,128)(2,1)S(1)}, u32[]{:S(2)}, u32[]{:S(2)}) async-start(bf16[8,256,512]{2,1,0:T(8,128)(2,1)} %dynamic-slice_bitcast_fusion.1), calls=%async_computation | async-start | bytes 4194304 | tf_op jit(solution)/shard_map/all_to_all | solution.py:382
  10.2 1.8 %collective-permute-start.2 = (f32[3,512]{1,0:T(4,128)S(1)}, f32[3,512]{1,0:T(4,128)S(1)}, u32[]{:S(2)}, u32[]{:S(2)}) collective-permute-start(f32[3,512]{1,0:T(4,128)S(1)} %get-tuple-element.40), channel_id=1, source_target_pairs={{0,6},{2,0},{4,2},{6,4},{8,14},{10,8},{12,10},{14,12},{16,22},{18,... | collective-permute-start | bytes 18440 | tf_op jit(solution)/shard_map/ppermute | solution.py:25
  12.5 3.0 %dynamic-slice_bitcast_fusion = bf16[8,256,512]{2,1,0:T(8,128)(2,1)} fusion(bf16[2,8,256,512]{3,2,1,0:T(8,128)(2,1)} %bitcast.30, s32[]{:T(128)S(6)} %select_n.14), kind=kLoop, calls=%fused_computation | loop fusion | bytes 4194308 | tf_op jit(solution)/shard_map/jit(dynamic_index_in_dim)/squeeze | solution.py:387
  15.5 17.4 %collective-permute-done.2 = f32[3,512]{1,0:T(4,128)S(1)} collective-permute-done((f32[3,512]{1,0:T(4,128)S(1)}, f32[3,512]{1,0:T(4,128)S(1)}, u32[]{:S(2)}, u32[]{:S(2)}) %collective-permute-start.2) | collective-permute-done | bytes 6176 | tf_op jit(solution)/shard_map/ppermute | solution.py:25
  33.0 2.2 %collective-permute-done.1 = f32[3,512]{1,0:T(4,128)S(1)} collective-permute-done((f32[3,512]{1,0:T(4,128)S(1)}, f32[3,512]{1,0:T(4,128)S(1)}, u32[]{:S(2)}, u32[]{:S(2)}) %collective-permute-start.1) | collective-permute-done | bytes 6176 | tf_op jit(solution)/shard_map/ppermute | solution.py:25
  35.2 4.4 %all-to-all-start.1 = ((bf16[8,256,512]{2,1,0:T(8,128)(2,1)}), bf16[8,256,512]{2,1,0:T(8,128)(2,1)}, u32[]{:S(2)}, u32[]{:S(2)}) async-start(bf16[8,256,512]{2,1,0:T(8,128)(2,1)} %dynamic-slice_bitcast_fusion), calls=%async_computation.1 | async-start | bytes 4194304 | tf_op jit(solution)/shard_map/all_to_all | solution.py:390
  40.2 4.7 %shard_map.112 = f32[256,512]{1,0:T(8,128)} custom-call(s32[2]{0:T(128)} %pad_add_fusion.at_ref, bf16[8,256,512]{2,1,0:T(8,128)(2,1)} %copy-done.18, bf16[16,512,1024]{2,1,0:T(8,128)(2,1)} %bitcast.25), custom_call_target="tpu_custom_call" | custom-call | flops 1073741824 | bytes 6815744 | tf_op jit(solution)/shard_map/pallas_call | solution.py:308
  44.8 1.6 %collective-permute-start.6 = (f32[256,512]{1,0:T(8,128)}, f32[256,512]{1,0:T(8,128)S(1)}, u32[]{:S(2)}, u32[]{:S(2)}) collective-permute-start(f32[256,512]{1,0:T(8,128)} %shard_map.112), channel_id=1, source_target_pairs={{0,1},{1,0},{2,3},{3,2},{4,5},{5,4},{6,7},{7,6},{8,9},{9,8},{10,11... | collective-permute-start | bytes 1572872 | tf_op jit(solution)/shard_map/ppermute | solution.py:354
  47.1 3.9 %collective-permute-start.5 = (f32[4,3,512]{2,1,0:T(4,128)S(1)}, f32[4,3,512]{2,1,0:T(4,128)S(1)}, u32[]{:S(2)}, u32[]{:S(2)}) collective-permute-start(f32[4,3,512]{2,1,0:T(4,128)S(1)} %pad_maximum_fusion.1), channel_id=1, source_target_pairs={{0,24},{2,26},{4,28},{6,30},{8,0},{10,2},{12,4},{14,6},{16,8},{18,... | collective-permute-start | bytes 73736 | tf_op jit(solution)/shard_map/ppermute | solution.py:25
  51.7 4.7 %shard_map.113 = f32[256,512]{1,0:T(8,128)} custom-call(s32[2]{0:T(128)} %pad_add_fusion.1.at_ref, bf16[8,256,512]{2,1,0:T(8,128)(2,1)} %copy-done.18, bf16[16,512,1024]{2,1,0:T(8,128)(2,1)} %bitcast.26), custom_call_target="tpu_custom_call" | custom-call | flops 1073741824 | bytes 6815744 | tf_op jit(solution)/shard_map/pallas_call | solution.py:308
  56.4 2.9 %collective-permute-done.6 = f32[256,512]{1,0:T(8,128)S(1)} collective-permute-done((f32[256,512]{1,0:T(8,128)}, f32[256,512]{1,0:T(8,128)S(1)}, u32[]{:S(2)}, u32[]{:S(2)}) %collective-permute-start.6) | collective-permute-done | bytes 524320 | tf_op jit(solution)/shard_map/ppermute | solution.py:354
  59.3 1.9 %add.18 = f32[256,512]{1,0:T(8,128)} add(f32[256,512]{1,0:T(8,128)} %shard_map.113, f32[256,512]{1,0:T(8,128)S(1)} %collective-permute-done.6) | non-fusion elementwise | flops 131072 | bytes 1572864 | tf_op jit(solution)/shard_map/add | solution.py:394
  61.2 2.6 %collective-permute-start.8 = (f32[256,512]{1,0:T(8,128)}, f32[256,512]{1,0:T(8,128)S(1)}, u32[]{:S(2)}, u32[]{:S(2)}) collective-permute-start(f32[256,512]{1,0:T(8,128)} %add.18), channel_id=1, source_target_pairs={{0,16},{2,18},{4,20},{6,22},{8,24},{10,26},{12,28},{14,30},{16,0},... | collective-permute-start | bytes 1572872 | tf_op jit(solution)/shard_map/ppermute | solution.py:349
  63.8 6.8 %collective-permute-done.5 = f32[4,3,512]{2,1,0:T(4,128)S(1)} collective-permute-done((f32[4,3,512]{2,1,0:T(4,128)S(1)}, f32[4,3,512]{2,1,0:T(4,128)S(1)}, u32[]{:S(2)}, u32[]{:S(2)}) %collective-permute-start.5) | collective-permute-done | bytes 24608 | tf_op jit(solution)/shard_map/ppermute | solution.py:25
  70.6 4.7 %shard_map.114 = f32[256,512]{1,0:T(8,128)} custom-call(s32[2]{0:T(128)} %pad_add_fusion.at_ref, bf16[8,256,512]{2,1,0:T(8,128)(2,1)} %all-to-all-done.1.slab_ref, bf16[16,512,1024]{2,1,0:T(8,128)(2,1)} %bitcast.27), custom_call_target="tpu_custom_call" | custom-call | flops 1073741824 | bytes 6815744 | tf_op jit(solution)/shard_map/pallas_call | solution.py:308
  75.3 1.6 %collective-permute-start.7 = (f32[256,512]{1,0:T(8,128)}, f32[256,512]{1,0:T(8,128)S(1)}, u32[]{:S(2)}, u32[]{:S(2)}) collective-permute-start(f32[256,512]{1,0:T(8,128)} %shard_map.114), channel_id=1, source_target_pairs={{0,1},{1,0},{2,3},{3,2},{4,5},{5,4},{6,7},{7,6},{8,9},{9,8},{10,11... | collective-permute-start | bytes 1572872 | tf_op jit(solution)/shard_map/ppermute | solution.py:354
  76.9 2.8 %shard_map.116 = (f32[16,16,512]{2,1,0:T(8,128)S(1)}, f32[16,16,512]{2,1,0:T(8,128)S(1)}, f32[16,16,512]{2,1,0:T(8,128)S(1)}, f32[16,16,512]{2,1,0:T(8,128)S(1)}...) custom-call(s32[1]{0:T(128)} %bitcast.5.me_ref, ...), custom_call_target="tpu_custom_call" | custom-call | flops 10485760 | bytes 6625284 | tf_op jit(solution)/shard_map/pallas_call | solution.py:336
  84.6 4.7 %shard_map.115.refs_2_ = f32[256,512]{1,0:T(8,128)} custom-call(s32[2]{0:T(128)} %pad_add_fusion.1.at_ref, bf16[8,256,512]{2,1,0:T(8,128)(2,1)} %all-to-all-done.1.slab_ref, bf16[16,512,1024]{2,1,0:T(8,128)(2,1)} %bitcast.28), custom_call_target="tpu_custom_call" | custom-call | flops 1073741824 | bytes 6815744 | tf_op jit(solution)/shard_map/pallas_call | solution.py:308
  90.3 1.0 copy-done.3
  92.4 1.0 copy-done.7
  96.6 1.6 %shard_map.117 = (f32[256,512]{1,0:T(8,128)}, f32[16,16,512]{2,1,0:T(8,128)S(1)}, f32[16,16,512]{2,1,0:T(8,128)S(1)}, f32[2,512]{1,0:T(2,128)S(1)}) custom-call(f32[256,512]{1,0:T(8,128)S(1)} %collective-permute-done.7.refs_0_, f32[256,512]{1,0:T(8,128)S(1)} %collective-permute-done.8.refs_1_, f32[256,512]{1,0:T(8,128)S(1)} %copy-done, ...), custom_call_target="tpu_custom_call" | custom-call | flops 1572864 | bytes 6361088 | tf_op jit(solution)/shard_map/pallas_call | solution.py:336
  98.2 11.1 %all_to_all.15.blocks_ref = f32[16,2,512]{2,1,0:T(2,128)S(1)} all-to-all(f32[16,2,512]{2,1,0:T(2,128)S(1)} %broadcast_in_dim.29), channel_id=1, replica_groups=mesh['tm'=16,'space'=2] {'tm'}, dimensions={0} | all-to-all | bytes 131072 | tf_op jit(solution)/shard_map/all_to_all | solution.py:421
  109.3 1.6 %shard_map.118 = (f32[256,512]{1,0:T(8,128)}, f32[256,512]{1,0:T(8,128)}) custom-call(s32[1]{0:T(128)} %bitcast.5.me_ref, f32[1,512]{1,0:T(1,128)S(1)} %bitcast.24, f32[3,16,16,512]{3,2,1,0:T(8,128)S(1)} %get-tuple-element.60.whole_ref, f32[2,16,512]{2,1,0:T(8,128)S(1)} %get-tuple-element.61.edge_ref, f32[16,2,512]{2,1,0:T(2,128)S(1)} %all_to_all.15.blocks_ref, ...), custom_call_target="tpu_custom_call" | custom-call | flops 1048576 | bytes 3803140 | tf_op jit(solution)/shard_map/pallas_call | solution.py:336
  (57 shorter events, 13.6 us)
Async XLA Ops:
  3.7 5.4 %copy-start.19 = (s32[256]{0:T(256)S(1)}, s32[256]{0:T(256)}, u32[]{:S(2)}) copy-start(s32[256]{0:T(256)} %param.11) | copy-start | bytes 3076
  3.7 5.5 %copy-start.1 = (f32[256,512]{1,0:T(8,128)S(1)}, f32[256,512]{1,0:T(8,128)}, u32[]{:S(2)}) copy-start(f32[256,512]{1,0:T(8,128)} %decay_in.3) | copy-start | bytes 1572868
  3.7 5.5 %copy-start.14 = (f32[512]{0:T(512)S(1)}, f32[512]{0:T(512)}, u32[]{:S(2)}) copy-start(f32[512]{0:T(512)} %param.12) | copy-start | bytes 6148
  3.7 5.5 %copy-start.15 = (f32[512]{0:T(512)S(1)}, f32[512]{0:T(512)}, u32[]{:S(2)}) copy-start(f32[512]{0:T(512)} %param.13) | copy-start | bytes 6148
  3.7 31.4 %all-to-all-start = ((bf16[8,256,512]{2,1,0:T(8,128)(2,1)}), bf16[8,256,512]{2,1,0:T(8,128)(2,1)S(1)}, u32[]{:S(2)}, u32[]{:S(2)}) async-start(bf16[8,256,512]{2,1,0:T(8,128)(2,1)} %dynamic-slice_bitcast_fusion.1), calls=%async_computation | async-start | bytes 4194304 | tf_op jit(solution)/shard_map/all_to_all | solution.py:382
  10.2 22.8 %collective-permute-start.2 = (f32[3,512]{1,0:T(4,128)S(1)}, f32[3,512]{1,0:T(4,128)S(1)}, u32[]{:S(2)}, u32[]{:S(2)}) collective-permute-start(f32[3,512]{1,0:T(4,128)S(1)} %get-tuple-element.40), channel_id=1, source_target_pairs={{0,6},{2,0},{4,2},{6,4},{8,14},{10,8},{12,10},{14,12},{16,22},{18,... | collective-permute-start | bytes 18440 | tf_op jit(solution)/shard_map/ppermute | solution.py:25
  12.0 23.2 %collective-permute-start.1 = (f32[3,512]{1,0:T(4,128)S(1)}, f32[3,512]{1,0:T(4,128)S(1)}, u32[]{:S(2)}, u32[]{:S(2)}) collective-permute-start(f32[3,512]{1,0:T(4,128)S(1)} %get-tuple-element.40), channel_id=1, source_target_pairs={{0,4},{2,6},{4,0},{6,2},{8,12},{10,14},{12,8},{14,10},{16,20},{18,... | collective-permute-start | bytes 18440 | tf_op jit(solution)/shard_map/ppermute | solution.py:25
  12.3 22.8 %collective-permute-start = (f32[3,512]{1,0:T(4,128)S(1)}, f32[3,512]{1,0:T(4,128)S(1)}, u32[]{:S(2)}, u32[]{:S(2)}) collective-permute-start(f32[3,512]{1,0:T(4,128)S(1)} %get-tuple-element.40), channel_id=1, source_target_pairs={{0,2},{2,4},{4,6},{6,0},{8,10},{10,12},{12,14},{14,8},{16,18},{18,... | collective-permute-start | bytes 18440 | tf_op jit(solution)/shard_map/ppermute | solution.py:25
  35.2 4.4 %copy-start.18 = (bf16[8,256,512]{2,1,0:T(8,128)(2,1)}, bf16[8,256,512]{2,1,0:T(8,128)(2,1)S(1)}, u32[]{:S(2)}) copy-start(bf16[8,256,512]{2,1,0:T(8,128)(2,1)S(1)} %all-to-all-done.slab_ref) | copy-start | bytes 6291460
  35.2 35.4 %all-to-all-start.1 = ((bf16[8,256,512]{2,1,0:T(8,128)(2,1)}), bf16[8,256,512]{2,1,0:T(8,128)(2,1)}, u32[]{:S(2)}, u32[]{:S(2)}) async-start(bf16[8,256,512]{2,1,0:T(8,128)(2,1)} %dynamic-slice_bitcast_fusion), calls=%async_computation.1 | async-start | bytes 4194304 | tf_op jit(solution)/shard_map/all_to_all | solution.py:390
  44.8 14.5 %collective-permute-start.6 = (f32[256,512]{1,0:T(8,128)}, f32[256,512]{1,0:T(8,128)S(1)}, u32[]{:S(2)}, u32[]{:S(2)}) collective-permute-start(f32[256,512]{1,0:T(8,128)} %shard_map.112), channel_id=1, source_target_pairs={{0,1},{1,0},{2,3},{3,2},{4,5},{5,4},{6,7},{7,6},{8,9},{9,8},{10,11... | collective-permute-start | bytes 1572872 | tf_op jit(solution)/shard_map/ppermute | solution.py:354
  47.1 23.5 %collective-permute-start.5 = (f32[4,3,512]{2,1,0:T(4,128)S(1)}, f32[4,3,512]{2,1,0:T(4,128)S(1)}, u32[]{:S(2)}, u32[]{:S(2)}) collective-permute-start(f32[4,3,512]{2,1,0:T(4,128)S(1)} %pad_maximum_fusion.1), channel_id=1, source_target_pairs={{0,24},{2,26},{4,28},{6,30},{8,0},{10,2},{12,4},{14,6},{16,8},{18,... | collective-permute-start | bytes 73736 | tf_op jit(solution)/shard_map/ppermute | solution.py:25
  51.0 19.6 %collective-permute-start.4 = (f32[4,3,512]{2,1,0:T(4,128)S(1)}, f32[4,3,512]{2,1,0:T(4,128)S(1)}, u32[]{:S(2)}, u32[]{:S(2)}) collective-permute-start(f32[4,3,512]{2,1,0:T(4,128)S(1)} %pad_maximum_fusion.1), channel_id=1, source_target_pairs={{0,16},{2,18},{4,20},{6,22},{8,24},{10,26},{12,28},{14,30},{16,0},... | collective-permute-start | bytes 73736 | tf_op jit(solution)/shard_map/ppermute | solution.py:25
  51.0 19.6 %collective-permute-start.3 = (f32[4,3,512]{2,1,0:T(4,128)S(1)}, f32[4,3,512]{2,1,0:T(4,128)S(1)}, u32[]{:S(2)}, u32[]{:S(2)}) collective-permute-start(f32[4,3,512]{2,1,0:T(4,128)S(1)} %pad_maximum_fusion.1), channel_id=1, source_target_pairs={{0,8},{2,10},{4,12},{6,14},{8,16},{10,18},{12,20},{14,22},{16,24},... | collective-permute-start | bytes 73736 | tf_op jit(solution)/shard_map/ppermute | solution.py:25
  61.2 15.7 %copy-start.16 = (f32[512]{0:T(512)S(1)}, f32[512]{0:T(512)}, u32[]{:S(2)}) copy-start(f32[512]{0:T(512)} %param.15) | copy-start | bytes 6148
  61.2 28.0 %collective-permute-start.8 = (f32[256,512]{1,0:T(8,128)}, f32[256,512]{1,0:T(8,128)S(1)}, u32[]{:S(2)}, u32[]{:S(2)}) collective-permute-start(f32[256,512]{1,0:T(8,128)} %add.18), channel_id=1, source_target_pairs={{0,16},{2,18},{4,20},{6,22},{8,24},{10,26},{12,28},{14,30},{16,0},... | collective-permute-start | bytes 1572872 | tf_op jit(solution)/shard_map/ppermute | solution.py:349
  75.3 14.0 %collective-permute-start.7 = (f32[256,512]{1,0:T(8,128)}, f32[256,512]{1,0:T(8,128)S(1)}, u32[]{:S(2)}, u32[]{:S(2)}) collective-permute-start(f32[256,512]{1,0:T(8,128)} %shard_map.114), channel_id=1, source_target_pairs={{0,1},{1,0},{2,3},{3,2},{4,5},{5,4},{6,7},{7,6},{8,9},{9,8},{10,11... | collective-permute-start | bytes 1572872 | tf_op jit(solution)/shard_map/ppermute | solution.py:354
  89.3 1.0 copy-start
  90.3 1.0 copy-start.3
  91.3 1.0 copy-start.5
  92.4 1.0 copy-start.7
  93.4 1.0 copy-start.9
  94.5 1.0 copy-start.11
  96.6 12.7 %copy-start.17 = (f32[512]{0:T(512)S(1)}, f32[512]{0:T(512)}, u32[]{:S(2)}) copy-start(f32[512]{0:T(512)} %param.14) | copy-start | bytes 6148
  (7 other events, 5.9 us)

commit v5 on v4

--- a/solution.py
+++ b/solution.py
@@ -9,6 +9,9 @@
 
 CHUNK = 16
 LANES = 128
+PAD = 16
+STEPS16 = 32767.0
+TINY = 1e-30
 F32 = jnp.float32
 LIMIT = 16 * 1024 * 1024
 
@@ -235,7 +238,7 @@
     chunks = steps // CHUNK
     c = part_refs[0][...]
     for ref in part_refs[1:]:
-        c = c + ref[...]
+        c = c + decode(ref)
     coef_ref[...] = c
     lanes(coef_ref, strip_ref)
     f = e = jnp.zeros((chunks, modes), F32)
@@ -283,15 +286,33 @@
     unlanes(smooth_strip_ref, out_smooth_ref)
 
 
-def project_kernel(at_ref, slab_ref, basis_ref, out_ref, slab_area, basis_area, slab_sems, basis_sems):
+def encode(values, ref):
+    steps = values.shape[0]
+    top = jnp.max(jnp.abs(values), axis=0, keepdims=True)
+    power = jnp.floor(jnp.log2(jnp.maximum(top, TINY))) + 1.0
+    coded = jnp.floor(values * (jnp.exp2(-power) * STEPS16) + 0.5)
+    ref[0:steps, :] = jnp.clip(coded, -STEPS16, STEPS16).astype(jnp.int32).astype(jnp.int16)
+    power = jnp.broadcast_to(power, (PAD, power.shape[1]))
+    ref[steps : steps + PAD, :] = power.astype(jnp.int32).astype(jnp.int16)
+
+
+def decode(ref):
+    steps = ref.shape[0] - PAD
+    power = ref[steps : steps + PAD, :].astype(jnp.int32).astype(F32)[0:1, :]
+    return ref[0:steps, :].astype(jnp.int32).astype(F32) * (jnp.exp2(power) * (1.0 / STEPS16))
+
+
+def project_kernel(at_ref, slab_ref, basis_ref, own_ref, *refs):
+    owners = at_ref.shape[0] - 1
+    coded_refs = refs[: owners - 1]
+    slab_area, basis_area, sum_area, slab_sems, basis_sems = refs[owners - 1 :]
     count = slab_ref.shape[0]
-    modes = out_ref.shape[1]
-    columns = pl.ds(pl.multiple_of(at_ref[1] * modes, LANES), modes)
+    modes = own_ref.shape[1]
     copies = []
     for g in range(count):
         copies.append((
             pltpu.make_async_copy(slab_ref.at[g], slab_area.at[g], slab_sems.at[g]),
-            pltpu.make_async_copy(basis_ref.at[at_ref[0] + g, :, columns], basis_area.at[g], basis_sems.at[g]),
+            pltpu.make_async_copy(basis_ref.at[at_ref[0] + g], basis_area.at[g], basis_sems.at[g]),
         ))
     for pair in copies:
         for copy in pair:
@@ -299,34 +320,50 @@
     for g in range(count):
         for copy in copies[g]:
             copy.wait()
-        term = jnp.dot(slab_area[g], basis_area[g], preferred_element_type=F32)
-        out_ref[...] = term if g == 0 else out_ref[...] + term
-
-
-def project(slabs, basis, first, owner, modes):
+        for turn in range(owners):
+            columns = pl.ds(pl.multiple_of(at_ref[1 + turn] * modes, LANES), modes)
+            term = jnp.dot(slab_area[g], basis_area[g, :, columns], preferred_element_type=F32)
+            sum_area[turn] = term if g == 0 else sum_area[turn] + term
+    own_ref[...] = sum_area[0]
+    for turn in range(1, owners):
+        encode(sum_area[turn], coded_refs[turn - 1])
+
+
+def project(slabs, basis, first, owners, modes):
     count, steps, cells = slabs.shape
-    return pl.pallas_call(
+    others = len(owners) - 1
+    own, *coded = pl.pallas_call(
         project_kernel,
         in_specs=[
             pl.BlockSpec(memory_space=pltpu.SMEM),
             pl.BlockSpec(memory_space=pl.ANY),
             pl.BlockSpec(memory_space=pl.ANY),
         ],
-        out_specs=pl.BlockSpec(memory_space=pltpu.VMEM),
-        out_shape=jax.ShapeDtypeStruct((steps, modes), F32),
+        out_specs=[pl.BlockSpec(memory_space=pltpu.VMEM)] * (1 + others),
+        out_shape=[jax.ShapeDtypeStruct((steps, modes), F32)]
+        + [jax.ShapeDtypeStruct((steps + PAD, modes), jnp.int16)] * others,
         scratch_shapes=[
             pltpu.VMEM(slabs.shape, slabs.dtype),
-            pltpu.VMEM((count, cells, modes), basis.dtype),
+            pltpu.VMEM((count,) + basis.shape[1:], basis.dtype),
+            pltpu.VMEM((1 + others, steps, modes), F32),
             pltpu.SemaphoreType.DMA((count,)),
             pltpu.SemaphoreType.DMA((count,)),
         ],
         compiler_params=pltpu.CompilerParams(vmem_limit_bytes=60 * LIMIT // 16),
         cost_estimate=pl.CostEstimate(
-            flops=2 * count * steps * cells * modes,
-            bytes_accessed=2 * count * cells * (steps + modes) + 4 * steps * modes,
+            flops=2 * count * steps * cells * modes * (1 + others),
+            bytes_accessed=2 * count * cells * (steps + modes * (1 + others)) + 4 * steps * modes,
             transcendentals=0,
         ),
-    )(jnp.stack([first, owner]), slabs, basis)
+    )(jnp.stack([first] + owners), slabs, basis)
+    return own, coded
+
+
+def fold_kernel(own_ref, *refs):
+    total = own_ref[...]
+    for ref in refs[:-1]:
+        total = total + decode(ref)
+    encode(total, refs[-1])
 
 
 def call(kernel, inputs, outputs, scratch, flops):
@@ -376,7 +413,7 @@
     slabs = observations.reshape(2, group, steps, observations.shape[3])
     basis = pod_basis.reshape(tm_count, -1, pod_basis.shape[3])
     first = half * group
-    others = [lax.rem(side + turn, space_count) for turn in range(1, space_count)]
+    owners = [lax.rem(side + turn, space_count) for turn in range(space_count)]
     far = lax.dynamic_index_in_dim(slabs, 1 - half, 0, keepdims=False)
     far, q = lax.optimization_barrier((far, q))
     far = lax.all_to_all(far, "tm", 0, 0, axis_index_groups=groups, tiled=True)
@@ -389,19 +426,20 @@
     far, near, blocks = lax.optimization_barrier((far, near, blocks))
     near = lax.all_to_all(near, "tm", 0, 0, axis_index_groups=groups, tiled=True)
 
-    theirs = [project(far, basis, first, owner, modes) for owner in others]
+    own, theirs = project(far, basis, first, owners, modes)
     arriving = [send_along(term, "space", turn + 1) for turn, term in enumerate(theirs)]
-    crossing = sum(arriving, project(far, basis, first, side, modes))
-    _, blocks = lax.optimization_barrier((theirs, blocks))
+    own, blocks = lax.optimization_barrier((own, blocks))
     rest = gather_far(blocks, "tm")
+    coded = jax.ShapeDtypeStruct((steps + PAD, modes), jnp.int16)
+    (crossing,) = call(fold_kernel, (own, *arriving), [coded], [], 8 * steps * modes)
     rest, near, _ = lax.optimization_barrier((rest, near, crossing))
     crossing = swap_halves(crossing, "tm")
     blocks = jnp.concatenate([blocks] + rest, 0)
 
-    theirs = [project(near, basis, first, owner, modes) for owner in others]
+    own, theirs = project(near, basis, first, owners, modes)
     parts = [send_along(term, "space", turn + 1) for turn, term in enumerate(theirs)] + [crossing]
-    chunk_totals, own_near, _ = lax.optimization_barrier((chunk_totals, near, theirs))
-    parts.append(project(own_near, basis, first, side, modes))
+    own, chunk_totals = lax.optimization_barrier((own, chunk_totals))
+    parts.insert(0, own)
     *maps, whole, carry, edge, log_variance = call(
         functools.partial(gains_kernel, tm_count),
         (me, decay, seen, q, r, prior_var[None, :], chunk_totals, blocks),

time: 112 us -> 103 us (0.920)
  waiting for transfers between devices: 29.4 us -> 40.5 us
  local copies, waits for them, and re-layouts: 18.4 us -> 8.31 us
  Pallas kernels: 25.6 us -> 19.7 us
  other arithmetic: 3.19 us -> 0.63 us
    unnamed x40 -> x18, local copies, waits for them, and re-layouts: 12.1 us -> 2.11 us
    ppermute x6, waiting for transfers between devices: 26.4 us -> 33.4 us  [rotate(): return lax.ppermute(block, axis, route)]
    pallas_call x4 -> x2, Pallas kernels: 18.7 us -> 12.2 us  [project(): pl.pallas_call(project_kernel, in_specs=[pl.BlockSpec(memory_space=pltpu....]
    ppermute x2, waiting for transfers between devices: 2.93 us -> 7.11 us  [send_along(): lax.ppermute(term, axis, [(i, (i + turn) % count) for i in range(count)])]
    add x1 -> x0, other arithmetic: 1.91 us -> none  [body(): crossing = sum(arriving, project(far, basis, first, side, modes))]
    pallas_call x4 -> x5, Pallas kernels: 6.96 us -> 7.42 us  [call(): pl.pallas_call(kernel, in_specs=[smem if x.dtype == jnp.int32 else vmem f...]
  transfers between devices with their start and end apart: 11 -> 11, of which waited for: 4 -> 5; matrix products, arithmetic and copies ran while one was open for 6% -> 4% of each run, Pallas kernels for 20% -> 16%
where the time goes in v5:
time: 103 us
  waiting for transfers between devices  40.5 us (39%)
  starting transfers between devices  22.5 us (22%)
  Pallas kernels  19.7 us (19%)
  blocking collectives  10.2 us (10%)
  local copies, waits for them, and re-layouts  8.31 us (8%)
    ppermute x6, waiting for transfers between devices, rotate(): return lax.ppermute(block, axis, route)  33.4 us
    pallas_call x2, Pallas kernels, project(): pl.pallas_call(project_kernel, in_specs=[pl.BlockSpec(memory_space=pltpu....  12.2 us
    all_to_all x1, blocking collectives, body(): ends = lax.all_to_all(ends, 'tm', 0, 0, tiled=True)  10.2 us
    pallas_call x5, Pallas kernels, call(): pl.pallas_call(kernel, in_specs=[smem if x.dtype == jnp.int32 else vmem f...  7.42 us
    ppermute x2, waiting for transfers between devices, send_along(): lax.ppermute(term, axis, [(i, (i + turn) % count) for i in range(count)])  7.11 us
    ppermute x6, starting transfers between devices, rotate(): return lax.ppermute(block, axis, route)  6.94 us
    all_to_all x1, starting transfers between devices, body(): far = lax.all_to_all(far, 'tm', 0, 0, axis_index_groups=groups, tiled=True)  5.37 us
    all_to_all x1, starting transfers between devices, body(): lax.all_to_all(near, 'tm', 0, 0, axis_index_groups=groups, tiled=True)  4.35 us
  transfers between devices with their start and end apart: 11, of which 5 were waited for; matrix products, arithmetic and copies ran while one was open for 4% of the time, Pallas kernels for 16%

profile of v5, /device:TPU:0, one launch (start us, length us, event | category | flops | bytes accessed | tf_op | source)
XLA Modules:
  0.0 102.7 jit_solution(12812121258942921177)
XLA Ops:
  0.7 3.0 %dynamic-slice_bitcast_fusion.1 = bf16[8,256,512]{2,1,0:T(8,128)(2,1)} fusion(bf16[2,8,256,512]{3,2,1,0:T(8,128)(2,1)} %bitcast.27, s32[]{:T(128)S(6)} %select_n.13), kind=kLoop, calls=%fused_computation.1 | loop fusion | bytes 4194308 | tf_op jit(solution)/shard_map/jit(dynamic_index_in_dim)/squeeze | solution.py:417
  3.7 5.4 %all-to-all-start = ((bf16[8,256,512]{2,1,0:T(8,128)(2,1)}), bf16[8,256,512]{2,1,0:T(8,128)(2,1)S(1)}, u32[]{:S(2)}, u32[]{:S(2)}) async-start(bf16[8,256,512]{2,1,0:T(8,128)(2,1)} %dynamic-slice_bitcast_fusion.1), calls=%async_computation | async-start | bytes 4194304 | tf_op jit(solution)/shard_map/all_to_all | solution.py:419
  9.2 0.9 shard_map.111
  10.1 1.8 %collective-permute-start.2 = (f32[3,512]{1,0:T(4,128)S(1)}, f32[3,512]{1,0:T(4,128)S(1)}, u32[]{:S(2)}, u32[]{:S(2)}) collective-permute-start(f32[3,512]{1,0:T(4,128)S(1)} %get-tuple-element.45), channel_id=1, source_target_pairs={{0,6},{2,0},{4,2},{6,4},{8,14},{10,8},{12,10},{14,12},{16,22},{18,... | collective-permute-start | bytes 18440 | tf_op jit(solution)/shard_map/ppermute | solution.py:28
  12.4 3.1 %dynamic-slice_bitcast_fusion = bf16[8,256,512]{2,1,0:T(8,128)(2,1)} fusion(bf16[2,8,256,512]{3,2,1,0:T(8,128)(2,1)} %bitcast.28, s32[]{:T(128)S(6)} %select_n.14), kind=kLoop, calls=%fused_computation | loop fusion | bytes 4194308 | tf_op jit(solution)/shard_map/jit(dynamic_index_in_dim)/squeeze | solution.py:424
  15.5 17.4 %collective-permute-done.2 = f32[3,512]{1,0:T(4,128)S(1)} collective-permute-done((f32[3,512]{1,0:T(4,128)S(1)}, f32[3,512]{1,0:T(4,128)S(1)}, u32[]{:S(2)}, u32[]{:S(2)}) %collective-permute-start.2) | collective-permute-done | bytes 6176 | tf_op jit(solution)/shard_map/ppermute | solution.py:28
  32.9 2.2 %collective-permute-done.1 = f32[3,512]{1,0:T(4,128)S(1)} collective-permute-done((f32[3,512]{1,0:T(4,128)S(1)}, f32[3,512]{1,0:T(4,128)S(1)}, u32[]{:S(2)}, u32[]{:S(2)}) %collective-permute-start.1) | collective-permute-done | bytes 6176 | tf_op jit(solution)/shard_map/ppermute | solution.py:28
  35.1 4.3 %all-to-all-start.1 = ((bf16[8,256,512]{2,1,0:T(8,128)(2,1)}), bf16[8,256,512]{2,1,0:T(8,128)(2,1)}, u32[]{:S(2)}, u32[]{:S(2)}) async-start(bf16[8,256,512]{2,1,0:T(8,128)(2,1)} %dynamic-slice_bitcast_fusion), calls=%async_computation.1 | async-start | bytes 4194304 | tf_op jit(solution)/shard_map/all_to_all | solution.py:427
  40.1 6.1 %shard_map.112 = (f32[256,512]{1,0:T(8,128)}, s16[272,512]{1,0:T(8,128)(2,1)}) custom-call(s32[3]{0:T(128)} %pad_add_fusion.at_ref, bf16[8,256,512]{2,1,0:T(8,128)(2,1)} %copy-done.7, bf16[16,512,1024]{2,1,0:T(8,128)(2,1)} %bitcast.25), custom_call_target="tpu_custom_call" | custom-call | flops 2147483648 | bytes 11010048 | tf_op jit(solution)/shard_map/pallas_call | solution.py:335
  46.2 1.6 %collective-permute-start.6 = (s16[272,512]{1,0:T(8,128)(2,1)}, s16[272,512]{1,0:T(8,128)(2,1)S(1)}, u32[]{:S(2)}, u32[]{:S(2)}) collective-permute-start(s16[272,512]{1,0:T(8,128)(2,1)} %get-tuple-element.52), channel_id=1, source_target_pairs={{0,1},{1,0},{2,3},{3,2},{4,5},{5,4},{6,7},{7,6},{8,9},{9,8},{10,11... | collective-permute-start | bytes 835592 | tf_op jit(solution)/shard_map/ppermute | solution.py:391
  47.8 3.9 %collective-permute-start.5 = (f32[4,3,512]{2,1,0:T(4,128)S(1)}, f32[4,3,512]{2,1,0:T(4,128)S(1)}, u32[]{:S(2)}, u32[]{:S(2)}) collective-permute-start(f32[4,3,512]{2,1,0:T(4,128)S(1)} %pad_maximum_fusion.1), channel_id=1, source_target_pairs={{0,24},{2,26},{4,28},{6,30},{8,0},{10,2},{12,4},{14,6},{16,8},{18,... | collective-permute-start | bytes 73736 | tf_op jit(solution)/shard_map/ppermute | solution.py:28
  51.7 0.7 collective-permute-start.3
  52.5 3.0 %collective-permute-done.6.refs_0_ = s16[272,512]{1,0:T(8,128)(2,1)S(1)} collective-permute-done((s16[272,512]{1,0:T(8,128)(2,1)}, s16[272,512]{1,0:T(8,128)(2,1)S(1)}, u32[]{:S(2)}, u32[]{:S(2)}) %collective-permute-start.6) | collective-permute-done | bytes 278560 | tf_op jit(solution)/shard_map/ppermute | solution.py:391
  55.4 1.0 %copy-done.1 = f32[256,512]{1,0:T(8,128)S(1)} copy-done((f32[256,512]{1,0:T(8,128)S(1)}, f32[256,512]{1,0:T(8,128)}, u32[]{:S(2)}) %copy-start.1) | copy-done | bytes 524312
  56.7 2.7 %collective-permute-start.8 = (s16[272,512]{1,0:T(8,128)(2,1)S(1)}, s16[272,512]{1,0:T(8,128)(2,1)S(1)}, u32[]{:S(2)}, u32[]{:S(2)}) collective-permute-start(s16[272,512]{1,0:T(8,128)(2,1)S(1)} %shard_map.113), channel_id=1, source_target_pairs={{0,16},{2,18},{4,20},{6,22},{8,24},{10,26},{12,28},{14,30},{16,0},... | collective-permute-start | bytes 835592 | tf_op jit(solution)/shard_map/ppermute | solution.py:386
  59.4 13.8 %collective-permute-done.5 = f32[4,3,512]{2,1,0:T(4,128)S(1)} collective-permute-done((f32[4,3,512]{2,1,0:T(4,128)S(1)}, f32[4,3,512]{2,1,0:T(4,128)S(1)}, u32[]{:S(2)}, u32[]{:S(2)}) %collective-permute-start.5) | collective-permute-done | bytes 24608 | tf_op jit(solution)/shard_map/ppermute | solution.py:28
  73.2 6.1 %shard_map.114 = (f32[256,512]{1,0:T(8,128)}, s16[272,512]{1,0:T(8,128)(2,1)}) custom-call(s32[3]{0:T(128)} %pad_add_fusion.at_ref, bf16[8,256,512]{2,1,0:T(8,128)(2,1)} %all-to-all-done.1.slab_ref, bf16[16,512,1024]{2,1,0:T(8,128)(2,1)} %bitcast.26), custom_call_target="tpu_custom_call" | custom-call | flops 2147483648 | bytes 11010048 | tf_op jit(solution)/shard_map/pallas_call | solution.py:335
  79.3 1.6 %collective-permute-start.7 = (s16[272,512]{1,0:T(8,128)(2,1)}, s16[272,512]{1,0:T(8,128)(2,1)S(1)}, u32[]{:S(2)}, u32[]{:S(2)}) collective-permute-start(s16[272,512]{1,0:T(8,128)(2,1)} %get-tuple-element.57), channel_id=1, source_target_pairs={{0,1},{1,0},{2,3},{3,2},{4,5},{5,4},{6,7},{7,6},{8,9},{9,8},{10,11... | collective-permute-start | bytes 835592 | tf_op jit(solution)/shard_map/ppermute | solution.py:391
  80.9 2.8 %shard_map.115 = (f32[16,16,512]{2,1,0:T(8,128)S(1)}, f32[16,16,512]{2,1,0:T(8,128)S(1)}, f32[16,16,512]{2,1,0:T(8,128)S(1)}, f32[16,16,512]{2,1,0:T(8,128)S(1)}...) custom-call(s32[1]{0:T(128)} %bitcast.6.me_ref, ...), custom_call_target="tpu_custom_call" | custom-call | flops 10485760 | bytes 6625284 | tf_op jit(solution)/shard_map/pallas_call | solution.py:373
  83.8 4.1 %collective-permute-done.7.refs_1_ = s16[272,512]{1,0:T(8,128)(2,1)S(1)} collective-permute-done((s16[272,512]{1,0:T(8,128)(2,1)}, s16[272,512]{1,0:T(8,128)(2,1)S(1)}, u32[]{:S(2)}, u32[]{:S(2)}) %collective-permute-start.7) | collective-permute-done | bytes 278560 | tf_op jit(solution)/shard_map/ppermute | solution.py:391
  87.9 1.0 %copy-done.2 = f32[256,512]{1,0:T(8,128)S(1)} copy-done((f32[256,512]{1,0:T(8,128)S(1)}, f32[256,512]{1,0:T(8,128)}, u32[]{:S(2)}) %copy-start.2) | copy-done | bytes 524312
  88.9 1.9 %shard_map.116 = (f32[256,512]{1,0:T(8,128)}, f32[16,16,512]{2,1,0:T(8,128)S(1)}, f32[16,16,512]{2,1,0:T(8,128)S(1)}, f32[2,512]{1,0:T(2,128)S(1)}) custom-call(f32[256,512]{1,0:T(8,128)S(1)} %copy-done.2, s16[272,512]{1,0:T(8,128)(2,1)S(1)} %collective-permute-done.7.refs_1_, s16[272,512]{1,0:T(8,128)(2,1)S(1)} %collective-permute-done.8.refs_2_, ...), custom_call_target="tpu_custom_call" | custom-call | flops 1572864 | bytes 6426624 | tf_op jit(solution)/shard_map/pallas_call | solution.py:373
  90.8 10.2 %all_to_all.15.blocks_ref = f32[16,2,512]{2,1,0:T(2,128)S(1)} all-to-all(f32[16,2,512]{2,1,0:T(2,128)S(1)} %broadcast_in_dim.29), channel_id=1, replica_groups=mesh['tm'=16,'space'=2] {'tm'}, dimensions={0} | all-to-all | bytes 131072 | tf_op jit(solution)/shard_map/all_to_all | solution.py:459
  101.1 1.6 %shard_map.117 = (f32[256,512]{1,0:T(8,128)}, f32[256,512]{1,0:T(8,128)}) custom-call(s32[1]{0:T(128)} %bitcast.6.me_ref, f32[1,512]{1,0:T(1,128)S(1)} %bitcast.24, f32[3,16,16,512]{3,2,1,0:T(8,128)S(1)} %get-tuple-element.70.whole_ref, f32[2,16,512]{2,1,0:T(8,128)S(1)} %get-tuple-element.71.edge_ref, f32[16,2,512]{2,1,0:T(2,128)S(1)} %all_to_all.15.blocks_ref, ...), custom_call_target="tpu_custom_call" | custom-call | flops 1048576 | bytes 3803140 | tf_op jit(solution)/shard_map/pallas_call | solution.py:373
  (32 shorter events, 1.5 us)
Async XLA Ops:
  3.7 5.4 %copy-start.8 = (s32[256]{0:T(256)S(1)}, s32[256]{0:T(256)}, u32[]{:S(2)}) copy-start(s32[256]{0:T(256)} %param.11) | copy-start | bytes 3076
  3.7 5.5 %copy-start = (f32[256,512]{1,0:T(8,128)S(1)}, f32[256,512]{1,0:T(8,128)}, u32[]{:S(2)}) copy-start(f32[256,512]{1,0:T(8,128)} %decay_in.3) | copy-start | bytes 1572868
  3.7 5.5 %copy-start.3 = (f32[512]{0:T(512)S(1)}, f32[512]{0:T(512)}, u32[]{:S(2)}) copy-start(f32[512]{0:T(512)} %param.12) | copy-start | bytes 6148
  3.7 5.5 %copy-start.4 = (f32[512]{0:T(512)S(1)}, f32[512]{0:T(512)}, u32[]{:S(2)}) copy-start(f32[512]{0:T(512)} %param.13) | copy-start | bytes 6148
  3.7 31.4 %all-to-all-start = ((bf16[8,256,512]{2,1,0:T(8,128)(2,1)}), bf16[8,256,512]{2,1,0:T(8,128)(2,1)S(1)}, u32[]{:S(2)}, u32[]{:S(2)}) async-start(bf16[8,256,512]{2,1,0:T(8,128)(2,1)} %dynamic-slice_bitcast_fusion.1), calls=%async_computation | async-start | bytes 4194304 | tf_op jit(solution)/shard_map/all_to_all | solution.py:419
  10.1 22.8 %collective-permute-start.2 = (f32[3,512]{1,0:T(4,128)S(1)}, f32[3,512]{1,0:T(4,128)S(1)}, u32[]{:S(2)}, u32[]{:S(2)}) collective-permute-start(f32[3,512]{1,0:T(4,128)S(1)} %get-tuple-element.45), channel_id=1, source_target_pairs={{0,6},{2,0},{4,2},{6,4},{8,14},{10,8},{12,10},{14,12},{16,22},{18,... | collective-permute-start | bytes 18440 | tf_op jit(solution)/shard_map/ppermute | solution.py:28
  11.9 23.2 %collective-permute-start.1 = (f32[3,512]{1,0:T(4,128)S(1)}, f32[3,512]{1,0:T(4,128)S(1)}, u32[]{:S(2)}, u32[]{:S(2)}) collective-permute-start(f32[3,512]{1,0:T(4,128)S(1)} %get-tuple-element.45), channel_id=1, source_target_pairs={{0,4},{2,6},{4,0},{6,2},{8,12},{10,14},{12,8},{14,10},{16,20},{18,... | collective-permute-start | bytes 18440 | tf_op jit(solution)/shard_map/ppermute | solution.py:28
  12.3 22.8 %collective-permute-start = (f32[3,512]{1,0:T(4,128)S(1)}, f32[3,512]{1,0:T(4,128)S(1)}, u32[]{:S(2)}, u32[]{:S(2)}) collective-permute-start(f32[3,512]{1,0:T(4,128)S(1)} %get-tuple-element.45), channel_id=1, source_target_pairs={{0,2},{2,4},{4,6},{6,0},{8,10},{10,12},{12,14},{14,8},{16,18},{18,... | collective-permute-start | bytes 18440 | tf_op jit(solution)/shard_map/ppermute | solution.py:28
  35.1 4.4 %copy-start.7 = (bf16[8,256,512]{2,1,0:T(8,128)(2,1)}, bf16[8,256,512]{2,1,0:T(8,128)(2,1)S(1)}, u32[]{:S(2)}) copy-start(bf16[8,256,512]{2,1,0:T(8,128)(2,1)S(1)} %all-to-all-done.slab_ref) | copy-start | bytes 6291460
  35.1 38.0 %all-to-all-start.1 = ((bf16[8,256,512]{2,1,0:T(8,128)(2,1)}), bf16[8,256,512]{2,1,0:T(8,128)(2,1)}, u32[]{:S(2)}, u32[]{:S(2)}) async-start(bf16[8,256,512]{2,1,0:T(8,128)(2,1)} %dynamic-slice_bitcast_fusion), calls=%async_computation.1 | async-start | bytes 4194304 | tf_op jit(solution)/shard_map/all_to_all | solution.py:427
  46.2 9.2 %collective-permute-start.6 = (s16[272,512]{1,0:T(8,128)(2,1)}, s16[272,512]{1,0:T(8,128)(2,1)S(1)}, u32[]{:S(2)}, u32[]{:S(2)}) collective-permute-start(s16[272,512]{1,0:T(8,128)(2,1)} %get-tuple-element.52), channel_id=1, source_target_pairs={{0,1},{1,0},{2,3},{3,2},{4,5},{5,4},{6,7},{7,6},{8,9},{9,8},{10,11... | collective-permute-start | bytes 835592 | tf_op jit(solution)/shard_map/ppermute | solution.py:391
  47.8 25.3 %collective-permute-start.5 = (f32[4,3,512]{2,1,0:T(4,128)S(1)}, f32[4,3,512]{2,1,0:T(4,128)S(1)}, u32[]{:S(2)}, u32[]{:S(2)}) collective-permute-start(f32[4,3,512]{2,1,0:T(4,128)S(1)} %pad_maximum_fusion.1), channel_id=1, source_target_pairs={{0,24},{2,26},{4,28},{6,30},{8,0},{10,2},{12,4},{14,6},{16,8},{18,... | collective-permute-start | bytes 73736 | tf_op jit(solution)/shard_map/ppermute | solution.py:28
  51.7 21.4 %collective-permute-start.4 = (f32[4,3,512]{2,1,0:T(4,128)S(1)}, f32[4,3,512]{2,1,0:T(4,128)S(1)}, u32[]{:S(2)}, u32[]{:S(2)}) collective-permute-start(f32[4,3,512]{2,1,0:T(4,128)S(1)} %pad_maximum_fusion.1), channel_id=1, source_target_pairs={{0,16},{2,18},{4,20},{6,22},{8,24},{10,26},{12,28},{14,30},{16,0},... | collective-permute-start | bytes 73736 | tf_op jit(solution)/shard_map/ppermute | solution.py:28
  51.7 21.4 %collective-permute-start.3 = (f32[4,3,512]{2,1,0:T(4,128)S(1)}, f32[4,3,512]{2,1,0:T(4,128)S(1)}, u32[]{:S(2)}, u32[]{:S(2)}) collective-permute-start(f32[4,3,512]{2,1,0:T(4,128)S(1)} %pad_maximum_fusion.1), channel_id=1, source_target_pairs={{0,8},{2,10},{4,12},{6,14},{8,16},{10,18},{12,20},{14,22},{16,24},... | collective-permute-start | bytes 73736 | tf_op jit(solution)/shard_map/ppermute | solution.py:28
  55.4 1.0 %copy-start.1 = (f32[256,512]{1,0:T(8,128)S(1)}, f32[256,512]{1,0:T(8,128)}, u32[]{:S(2)}) copy-start(f32[256,512]{1,0:T(8,128)} %get-tuple-element.51.own_ref) | copy-start | bytes 1572868
  56.7 24.2 %copy-start.5 = (f32[512]{0:T(512)S(1)}, f32[512]{0:T(512)}, u32[]{:S(2)}) copy-start(f32[512]{0:T(512)} %param.15) | copy-start | bytes 6148
  56.7 27.0 %collective-permute-start.8 = (s16[272,512]{1,0:T(8,128)(2,1)S(1)}, s16[272,512]{1,0:T(8,128)(2,1)S(1)}, u32[]{:S(2)}, u32[]{:S(2)}) collective-permute-start(s16[272,512]{1,0:T(8,128)(2,1)S(1)} %shard_map.113), channel_id=1, source_target_pairs={{0,16},{2,18},{4,20},{6,22},{8,24},{10,26},{12,28},{14,30},{16,0},... | collective-permute-start | bytes 835592 | tf_op jit(solution)/shard_map/ppermute | solution.py:386
  79.3 8.6 %collective-permute-start.7 = (s16[272,512]{1,0:T(8,128)(2,1)}, s16[272,512]{1,0:T(8,128)(2,1)S(1)}, u32[]{:S(2)}, u32[]{:S(2)}) collective-permute-start(s16[272,512]{1,0:T(8,128)(2,1)} %get-tuple-element.57), channel_id=1, source_target_pairs={{0,1},{1,0},{2,3},{3,2},{4,5},{5,4},{6,7},{7,6},{8,9},{9,8},{10,11... | collective-permute-start | bytes 835592 | tf_op jit(solution)/shard_map/ppermute | solution.py:391
  87.9 1.0 %copy-start.2 = (f32[256,512]{1,0:T(8,128)S(1)}, f32[256,512]{1,0:T(8,128)}, u32[]{:S(2)}) copy-start(f32[256,512]{1,0:T(8,128)} %get-tuple-element.56.refs_0_) | copy-start | bytes 1572868
  88.9 12.1 %copy-start.6 = (f32[512]{0:T(512)S(1)}, f32[512]{0:T(512)}, u32[]{:S(2)}) copy-start(f32[512]{0:T(512)} %param.14) | copy-start | bytes 6148
